TPU v7x, 256 devices: a whole 4x4x8 slice. The times are simulated.
256 devices in a mesh: ctx: 32 (over z, y_lo, core), head: 8 (over y_hi, x).
Axes of the slice: x: 4, y: 4 (y_hi: 2, y_lo: 2; y = y_hi * 2 + y_lo), z: 8, core: 2. Of those that a mesh axis runs over, the one named last changes fastest.
Arguments:
- queries: bfloat16 [2048, 64, 576], P('ctx', 'head'), may hold values from -4.5 to 4.5
- latent: bfloat16 [2048, 576], P('ctx'), may hold values from -5 to 5
- grad_out: bfloat16 [2048, 64, 512], P('ctx', 'head'), may hold values from -1.1953125 to 1.1953125
- block_order: int32 [64], replicated, may hold values from 0 to 63, each once
Outputs:
- grad_queries: bfloat16 [2048, 64, 576], P('ctx', 'head')
- grad_latent: float32 [2048, 576], P(('ctx', 'head'))
All inputs are finite; a program needn't handle non-finite values.
Results may differ from a plain program's by a relative error of at most 0.0045.
Values may be sent and summed in bfloat16 or wider, within the bound.
No kernel may reach another device: no remote copies, remote signals or barrier semaphores. Data moves between devices by JAX's collectives and lax.ppermute only.
A program may use at most 64 MiB of HBM per device.

v0:
```python
import jax
import jax.numpy as jnp
from jax import lax
from jax.sharding import PartitionSpec as P

KV_RANK = 512


score_scale = 192.0 ** (-0.5)
masked_low = -1e30


def seq_positions(block_table, first_row, row_count, half_rows):
    row_ids = first_row + jnp.arange(row_count, dtype=jnp.int32)
    block_ids = row_ids // half_rows
    table_ids = jnp.arange(block_table.shape[0], dtype=jnp.int32)
    picked = jnp.sum(
        jnp.where(block_ids[:, None] == table_ids[None, :], block_table[None, :], 0), axis=1
    )
    return picked * half_rows + row_ids % half_rows


def block_scores(key_block, key_pos, query_flat, grad_flat, query_pos):
    scores = (
        jnp.einsum("kc,rc->kr", key_block, query_flat, preferred_element_type=jnp.float32)
        * score_scale
    )
    value_prod = jnp.einsum(
        "kv,rv->kr", key_block[:, :KV_RANK], grad_flat, preferred_element_type=jnp.float32
    )
    visible = key_pos[:, None] <= query_pos[None, :]
    return (jnp.where(visible, scores, masked_low), value_prod, visible)


def forward_update(partial_value, key_block, key_pos, query_flat, grad_flat, query_pos):

    def forward_compute(current):
        running_max, running_sum, weighted = current
        scores, value_prod, visible = block_scores(
            key_block, key_pos, query_flat, grad_flat, query_pos
        )
        new_max = jnp.maximum(running_max, jnp.max(scores, axis=0))
        attention = jnp.where(visible, jnp.exp(scores - new_max[None, :]), 0.0)
        return (new_max, jnp.sum(attention, axis=0), jnp.sum(attention * value_prod, axis=0))

    any_live = jnp.min(key_pos) <= jnp.max(query_pos)
    return lax.cond(any_live, forward_compute, lambda current: current, partial_value)


def backward_terms(key_block, key_pos, query_flat, grad_flat, query_pos, log_norm, row_delta):
    lat_width = key_block.shape[1]

    def backward_compute(unused):
        scores, value_prod, visible = block_scores(
            key_block, key_pos, query_flat, grad_flat, query_pos
        )
        attention = jnp.where(visible, jnp.exp(scores - log_norm[None, :]), 0.0)
        score_grad = (score_scale * attention * (value_prod - row_delta[None, :])).astype(
            jnp.bfloat16
        )
        weights = attention.astype(jnp.bfloat16)
        query_term = jnp.einsum(
            "kr,kc->rc", score_grad, key_block, preferred_element_type=jnp.float32
        )
        key_term = jnp.einsum(
            "kr,rc->kc", score_grad, query_flat, preferred_element_type=jnp.float32
        )
        value_term = jnp.einsum("kr,rv->kv", weights, grad_flat, preferred_element_type=jnp.float32)
        key_term = key_term + jnp.pad(value_term, ((0, 0), (0, lat_width - KV_RANK)))
        return (query_term, key_term)

    def skip(unused):
        return (
            jnp.zeros((query_flat.shape[0], lat_width), jnp.float32),
            jnp.zeros((key_block.shape[0], lat_width), jnp.float32),
        )

    any_live = jnp.min(key_pos) <= jnp.max(query_pos)
    return lax.cond(any_live, backward_compute, skip, 0)


def backward_update(key_block, key_pos, query_flat, grad_flat, query_pos, log_norm, row_delta):
    query_term, key_term = backward_terms(
        key_block, key_pos, query_flat, grad_flat, query_pos, log_norm, row_delta
    )
    return (query_term, key_term)


def shards(queries, latent, grad_out, block_order):
    tok_rows, head_count, lat_width = queries.shape
    half_rows = tok_rows // 2
    cycle_index = lax.axis_index("ctx")
    first_row = cycle_index * tok_rows
    query_flat = queries.reshape(tok_rows * head_count, lat_width)
    grad_flat = grad_out.reshape(tok_rows * head_count, KV_RANK)
    query_pos = jnp.repeat(seq_positions(block_order, first_row, tok_rows, half_rows), head_count)
    flat_rows = query_flat.shape[0]
    start_stats = (
        jnp.full((flat_rows,), masked_low, jnp.float32),
        jnp.zeros((flat_rows,), jnp.float32),
        jnp.zeros((flat_rows,), jnp.float32),
    )
    shard_keys = lax.all_gather(latent, "ctx", axis=0, tiled=True)
    key_pos = seq_positions(block_order, jnp.int32(0), shard_keys.shape[0], half_rows)
    running_max, running_sum, weighted = forward_update(
        start_stats, shard_keys, key_pos, query_flat, grad_flat, query_pos
    )
    log_norm = running_max + jnp.log(running_sum)
    row_delta = weighted / running_sum
    shard_keys = lax.all_gather(latent, "ctx", axis=0, tiled=True)
    key_pos = seq_positions(block_order, jnp.int32(0), shard_keys.shape[0], half_rows)
    grad_query, grad_lat = backward_update(
        shard_keys, key_pos, query_flat, grad_flat, query_pos, log_norm, row_delta
    )
    ctx_part = lax.psum_scatter(grad_lat, "ctx", scatter_dimension=0, tiled=True)
    grad_latent = lax.psum_scatter(ctx_part, "head", scatter_dimension=0, tiled=True)
    return (grad_query.reshape(tok_rows, head_count, lat_width).astype(jnp.bfloat16), grad_latent)


def solution(mesh):
    placed = (P("ctx", "head", None), P("ctx", None), P("ctx", "head", None), P())
    return jax.shard_map(
        shards,
        mesh=mesh,
        in_specs=placed,
        out_specs=(P("ctx", "head", None), P(("ctx", "head"), None)),
        check_vma=False,
    )
```

profile of v0, /device:TPU:1, one launch (start us, length us, event | category | flops | bytes accessed | tf_op | source)
XLA Modules:
  0.0 322.7 jit_solution(11266046131053835962)
XLA Ops:
  7.2 0.0 all-gather.2.cloned.1.call-start
  7.2 0.7 all-gather.2.cloned.1.call-update
  7.9 0.0 reduce-scatter.2.cloned.1.call-start
  8.0 0.8 select_reduce_fusion.1
  8.8 0.7 broadcast_reduce_fusion
  9.5 0.8 select_reduce_fusion
  10.4 0.6 fusion.17
  12.3 67.2 %all-gather.2.cloned.1.call-done = bf16[2048,576]{1,0:T(8,128)(2,1)} async-done(((bf16[64,576]{1,0:T(8,128)(2,1)}), bf16[2048,576]{1,0:T(8,128)(2,1)}) %all-gather.2.cloned.1.call-update) | async-done | bytes 2359312 | tf_op jit(solution)/shard_map/all_gather | solution.py:110
  79.6 0.1 broadcast_in_dim.72
  79.6 9.4 %conditional.2 = (f32[512]{0:T(512)}, f32[512]{0:T(512)S(1)}, f32[512]{0:T(512)S(1)}) conditional(s32[]{:T(128)} %convert_element_type.21, () %tuple.35, (s32[2048]{0:T(1024)S(1)}, s32[64,8]{1,0:T(8,128)S(1)}, bf16[2048,576]{1,0:T(8,128)(2,1)}, bf16[512,576]{1,0:T(8,128)(2,1)}, bf16[512,512]{1,0:T(8,128)(2,1)}) %tuple.55), branch_computations={%region_4.5_spmd, %region_5.9_spmd} | conditional | flops 2299526656 | bytes 29745232 | solution.py:47
  79.6 0.1 le.21
  79.7 3.6 %fusion = (f32[512]{0:T(512)S(1)}, f32[2048,512]{1,0:T(8,128)S(1)}) fusion(s32[512]{0:T(512)S(1)} %le.21, s32[2048]{0:T(1024)S(1)} %get-tuple-element.41, bf16[2048,576]{1,0:T(8,128)(2,1)} %get-tuple-element.43, bf16[512,576]{1,0:T(8,128)(2,1)} %get-tuple-element.44), kind=kOutput, calls=%fused_computation.3 | convolution fusion | flops 1212153344 | bytes 7155712 | tf_op jit(solution)/shard_map/cond/branch_1_fun/kc,rc->kr/dot_general | solution.py:25
  83.3 0.0 copy-start.2
  83.3 0.0 copy-start.4
  83.3 0.6 broadcast_maximum_fusion
  83.9 2.2 fusion.1
  86.2 0.0 copy-done.2
  86.2 0.0 copy-done.4
  86.2 2.8 multiply_reduce_fusion
  89.0 13.1 %conditional.3 = (f32[2048,576]{0,1:T(8,128)}, bf16[64,8,576]{2,1,0:T(8,128)(2,1)S(1)}) conditional(s32[]{:T(128)} %convert_element_type.21, () %tuple.34, (s32[2048]{0:T(1024)S(1)}, s32[64,8]{1,0:T(8,128)S(1)}, bf16[2048,576]{1,0:T(8,128)(2,1)}, bf16[512,576]{1,0:T(8,128)(2,1)}, f32[512]{0:T(512)}, /*index=5*/f32[512]{0:T(512)S(1)}, ...), branch_computations={%region_9.10_spmd, %region_10.11_spmd} | conditional | flops 5783323136 | bytes 56713316 | solution.py:79
  89.0 0.7 add.46
  89.7 0.1 le.34
  89.8 0.0 copy-start.3
  89.8 0.0 copy-start.5
  89.8 4.2 %compare_select_fusion.2 = f32[2048,512]{1,0:T(8,128)S(1)} fusion(bf16[2048,576]{1,0:T(8,128)(2,1)} %get-tuple-element.48, bf16[512,576]{1,0:T(8,128)(2,1)} %get-tuple-element.49, f32[512]{0:T(512)S(1)} %add.46, s32[512]{0:T(512)S(1)} %le.34, s32[2048]{0:T(1024)S(1)} %get-tuple-element.46), kind=kOutput, calls=%fused_computation.7 | convolution fusion | flops 1213202432 | bytes 7155712 | tf_op jit(solution)/shard_map/cond/branch_1_fun/kc,rc->kr/dot_general | solution.py:25
  94.0 0.0 copy-done.3
  94.0 0.0 copy-done.5
  94.0 1.4 multiply_convert_fusion
  95.4 0.0 copy-start
  95.4 1.3 fusion.5
  96.7 0.0 copy-done
  96.8 3.6 %pad_add_fusion = f32[2048,576]{0,1:T(8,128)} fusion(f32[2048,512]{0,1:T(8,128)S(1)} %fusion.5, bf16[2048,512]{1,0:T(8,128)(2,1)S(1)} %multiply_convert_fusion, bf16[512,576]{1,0:T(8,128)(2,1)S(1)} %copy-done), kind=kOutput, calls=%fused_computation.9 | convolution fusion | flops 1209139200 | bytes 11599872 | tf_op jit(solution)/shard_map/cond/branch_1_fun/kr,rc->kc/dot_general | solution.py:65
  100.4 1.4 convolution_convert_fusion
  101.8 0.3 copy.12
  102.1 0.0 copy-start.1
  102.1 6.0 %copy.13 = f32[2048,576]{1,0:T(8,128)} copy(f32[2048,576]{0,1:T(8,128)} %get-tuple-element.65) | data formatting | bytes 9437184 | tf_op jit(solution)/shard_map/cond | solution.py:79
  108.1 0.0 copy-done.1
  108.1 0.0 copy-start.6
  108.2 0.0 reduce-scatter.2.cloned.1.call-update
  108.2 0.0 all-reduce.4.cloned.1.call-start
  108.2 121.1 %reduce-scatter.2.cloned.1.call-done = f32[64,576]{1,0:T(8,128)} async-done(((f32[2048,576]{1,0:T(8,128)}), f32[64,576]{1,0:T(8,128)}) %reduce-scatter.2.cloned.1.call-update) | async-done | bytes 147472 | tf_op jit(solution)/shard_map/reduce_scatter | solution.py:115
  229.4 0.0 all-reduce.4.cloned.1.call-update
  229.4 0.0 copy-done.6
  229.4 0.6 dynamic-slice
  230.6 84.2 %all-reduce.4.cloned.1.call-done = f32[64,576]{1,0:T(8,128)} async-done(((f32[64,576]{1,0:T(8,128)}), f32[64,576]{1,0:T(8,128)}) %all-reduce.4.cloned.1.call-update) | async-done | bytes 147472
  314.8 1.3 constant_dynamic-slice_fusion
  (4 shorter events, 0.0 us)
Async XLA Ops:
  7.2 72.4 %all-gather.2.cloned.1.call-start = ((), (), s32[]{:S(2)}) async-start(), calls=%async_computation.1 | async-start | bytes 2703360 | tf_op jit(solution)/shard_map/all_gather | solution.py:110
  7.9 221.5 %reduce-scatter.2.cloned.1.call-start = ((), (), s32[]{:S(2)}) async-start(), calls=%async_computation.2 | async-start | bytes 5406720 | tf_op jit(solution)/shard_map/reduce_scatter | solution.py:115
  83.3 2.8 copy-start.2
  83.3 2.8 copy-start.4
  89.8 4.2 %copy-start.3 = (bf16[512,512]{1,0:T(8,128)(2,1)S(1)}, bf16[512,512]{1,0:T(8,128)(2,1)}, u32[]{:S(2)}) copy-start(bf16[512,512]{1,0:T(8,128)(2,1)} %get-tuple-element.52) | copy-start | bytes 1572868 | tf_op jit(solution)/shard_map/cond
  89.8 4.2 %copy-start.5 = (bf16[2048,576]{1,0:T(8,128)(2,1)S(1)}, bf16[2048,576]{1,0:T(8,128)(2,1)}, u32[]{:S(2)}) copy-start(bf16[2048,576]{1,0:T(8,128)(2,1)} %get-tuple-element.48) | copy-start | bytes 7077892 | tf_op jit(solution)/shard_map/cond
  95.4 1.3 copy-start
  102.1 6.0 %copy-start.1 = (bf16[64,8,576]{2,1,0:T(8,128)(2,1)}, bf16[64,8,576]{2,1,0:T(8,128)(2,1)S(1)}, u32[]{:S(2)}) copy-start(bf16[64,8,576]{2,1,0:T(8,128)(2,1)S(1)} %get-tuple-element.66) | copy-start | bytes 1769476
  108.1 121.3 %copy-start.6 = (u32[256]{0:T(256)S(1)}, u32[256]{0:T(256)}, u32[]{:S(2)}) copy-start(u32[256]{0:T(256)} %constant.109) | copy-start | bytes 3076
  108.2 206.7 %all-reduce.4.cloned.1.call-start = ((), (), s32[]{:S(2)}) async-start(), calls=%async_computation.3 | async-start | bytes 327680
Sparse Core Ops, SparseCore 0:
  9.9 69.6 all-gather.1
  108.3 121.0 reduce-scatter.1
  232.0 82.7 all-reduce.3
where the time goes:
time: 327 us; the launch traced here: 323 us
  waiting for transfers between devices  273 us (83%)
  matrix products  18.3 us (6%)
  between operations  15.8 us (5%)
  local copies, waits for them, and re-layouts  8.53 us (3%)
  other arithmetic  6.53 us (2%)
    reduce_scatter x1, waiting for transfers between devices, shards(): lax.psum_scatter(grad_lat, 'ctx', scatter_dimension=0, tiled=True)  121 us
    unnamed x4, waiting for transfers between devices  84.9 us
    all_gather x1, waiting for transfers between devices, shards(): shard_keys = lax.all_gather(latent, 'ctx', axis=0, tiled=True)  67.2 us
    dot_general x2, matrix products, block_scores(): jnp.einsum('kc,rc->kr', key_block, query_flat, preferred_element_type=jnp...  7.79 us
  transfers between devices with their start and end apart: 3, of which 3 were waited for; matrix products, arithmetic and copies ran while one was open for 1% of the time, Pallas kernels for 0%

commit v1 on v0

v1 whole, which is shorter than its diff:
```python
import jax
import jax.numpy as jnp
from jax import lax
from jax.experimental import pallas as pl
from jax.experimental.pallas import tpu as pltpu
from jax.sharding import Mesh, PartitionSpec as P

CTX = ("z", "yl", "c")
HEAD = ("yh", "x")
KV_RANK = 512
WIDTH = 576
SCALE = 192.0 ** (-0.5)
LOW = -1e30
CHUNK = 256
KEYS = 2048
ROWS = 512


def nn(a, b):
    return lax.dot_general(a, b, (((1,), (0,)), ((), ())), preferred_element_type=jnp.float32)


def nt(a, b):
    return lax.dot_general(a, b, (((1,), (1,)), ((), ())), preferred_element_type=jnp.float32)


def tn(a, b):
    return lax.dot_general(a, b, (((0,), (0,)), ((), ())), preferred_element_type=jnp.float32)


def attention_kernel(
    order_ref, where_ref, own_ref, other_ref, q_ref, g_ref,
    dq_ref, own_out, other_out,
    p_scr, vp_scr, ds_scr, stat_scr,
):
    ctx, core = where_ref[0], where_ref[1]
    lane = lax.broadcasted_iota(jnp.int32, (1, ROWS), 1)
    tok = lane // 8
    query_pos = jnp.where(
        tok < 32, order_ref[2 * ctx] * 32 + tok, order_ref[2 * ctx + 1] * 32 + tok - 32
    )
    sub = lax.broadcasted_iota(jnp.int32, (8, 128), 0)
    q = q_ref[...]
    g = g_ref[...]
    n_chunks = KEYS // CHUNK
    half_chunks = n_chunks // 2

    running_max = jnp.full((1, ROWS), LOW, jnp.float32)
    total = jnp.zeros((1, ROWS), jnp.float32)
    weighted = jnp.zeros((1, ROWS), jnp.float32)
    for i in range(n_chunks):
        k_ref = own_ref if i < half_chunks else other_ref
        base = (i % half_chunks) * CHUNK
        key_core = core if i < half_chunks else 1 - core
        keys = k_ref[base:base + CHUNK, :]
        tiles = []
        for t in range(CHUNK // 8):
            u = base // 8 + t
            z, piece = u % 8, u // 8
            yl, yh, x = piece // 8, (piece // 4) % 2, piece % 4
            block = ((z * 2 + yl) * 2 + key_core) * 2 + yh
            tiles.append(sub + (order_ref[block] * 32 + x * 8))
        key_pos = jnp.concatenate(tiles, axis=0)
        key_pos = jnp.concatenate([key_pos] * (ROWS // 128), axis=1)
        visible = key_pos <= query_pos
        scores = jnp.where(visible, nt(keys, q) * SCALE, LOW)
        value_prod = nt(keys[:, :KV_RANK], g)
        new_max = jnp.maximum(running_max, jnp.max(scores, axis=0, keepdims=True))
        carry = jnp.exp(running_max - new_max)
        p = jnp.where(visible, jnp.exp(scores - new_max), 0.0)
        total = total * carry + jnp.sum(p, axis=0, keepdims=True)
        weighted = weighted * carry + jnp.sum(p * value_prod, axis=0, keepdims=True)
        running_max = new_max
        p_scr[i * CHUNK:(i + 1) * CHUNK, :] = p
        vp_scr[i * CHUNK:(i + 1) * CHUNK, :] = value_prod
        stat_scr[i:i + 1, :] = new_max
    inv = 1.0 / total
    delta = weighted * inv
    for i in range(n_chunks):
        out_ref = own_out if i < half_chunks else other_out
        base = (i % half_chunks) * CHUNK
        factor = jnp.exp(stat_scr[i:i + 1, :] - running_max) * inv
        attention = p_scr[i * CHUNK:(i + 1) * CHUNK, :] * factor
        ds = (SCALE * attention * (vp_scr[i * CHUNK:(i + 1) * CHUNK, :] - delta)).astype(jnp.bfloat16)
        w = attention.astype(jnp.bfloat16)
        ds_scr[i * CHUNK:(i + 1) * CHUNK, :] = ds
        out_ref[base:base + CHUNK, :KV_RANK] = (nn(ds, q[:, :KV_RANK]) + nn(w, g)).astype(out_ref.dtype)
        out_ref[base:base + CHUNK, KV_RANK:] = nn(ds, q[:, KV_RANK:]).astype(out_ref.dtype)
    half = KEYS // 2
    dq_ref[...] = (
        tn(ds_scr[:half, :], own_ref[...]) + tn(ds_scr[half:, :], other_ref[...])
    ).astype(dq_ref.dtype)


def attention_call(order, where, own, other, q, g):
    half = KEYS // 2
    vmem = pl.BlockSpec(memory_space=pltpu.VMEM)
    smem = pl.BlockSpec(memory_space=pltpu.SMEM)
    return pl.pallas_call(
        attention_kernel,
        out_shape=(
            jax.ShapeDtypeStruct((ROWS, WIDTH), jnp.bfloat16),
            jax.ShapeDtypeStruct((half, WIDTH), jnp.float32),
            jax.ShapeDtypeStruct((half, WIDTH), jnp.bfloat16),
        ),
        in_specs=[smem, smem, vmem, vmem, vmem, vmem],
        out_specs=(vmem, vmem, vmem),
        scratch_shapes=[
            pltpu.VMEM((KEYS, ROWS), jnp.float32),
            pltpu.VMEM((KEYS, ROWS), jnp.float32),
            pltpu.VMEM((KEYS, ROWS), jnp.bfloat16),
            pltpu.VMEM((8, ROWS), jnp.float32),
        ],
        compiler_params=pltpu.CompilerParams(vmem_limit_bytes=48 * 2**20),
        cost_estimate=pl.CostEstimate(
            flops=2 * KEYS * ROWS * (3 * WIDTH + 2 * KV_RANK),
            bytes_accessed=10 * 2**20, transcendentals=KEYS * ROWS,
        ),
        name="attention",
    )(order, where, own, other, q, g)


def shards(queries, latent, grad_out, block_order):
    tok_rows, head_count, width = queries.shape
    q = queries.reshape(tok_rows * head_count, width)
    g = grad_out.reshape(tok_rows * head_count, KV_RANK)
    core = lax.axis_index("c")
    where = jnp.stack([lax.axis_index(CTX), core]).astype(jnp.int32)
    piece = lax.dynamic_slice_in_dim(latent, lax.axis_index(HEAD) * 8, 8, 0)
    column = lax.all_to_all(
        jnp.broadcast_to(piece[None], (8, 8, width)), "z", 0, 0, tiled=True
    ).reshape(64, width)
    own = lax.all_to_all(
        jnp.broadcast_to(column[None], (16, 64, width)), ("yl", "yh", "x"), 0, 0, tiled=True
    ).reshape(1024, width)
    swap = [(0, 1), (1, 0)]
    other = lax.ppermute(own, "c", swap)
    dq, kept, given = attention_call(block_order, where, own, other, q, g)
    taken = lax.ppermute(given, "c", swap)
    part = (kept + taken.astype(jnp.float32)).astype(jnp.bfloat16)
    part = lax.all_to_all(part.reshape(16, 64, width), ("yl", "yh", "x"), 0, 0, tiled=True)
    part = jnp.sum(part.astype(jnp.float32), axis=0).astype(jnp.bfloat16)
    part = lax.all_to_all(part.reshape(8, 8, width), "z", 0, 0, tiled=True)
    return dq.reshape(tok_rows, head_count, width), jnp.sum(part.astype(jnp.float32), axis=0)


def solution(mesh):
    fine = Mesh(mesh.devices.reshape(8, 2, 2, 2, 4), CTX + HEAD)
    placed = (P(CTX, HEAD, None), P(CTX, None), P(CTX, HEAD, None), P())
    return jax.shard_map(
        shards, mesh=fine, in_specs=placed,
        out_specs=(P(CTX, HEAD, None), P(CTX + HEAD, None)), check_vma=False,
    )
```

time: 327 us -> 104 us (0.32); the launches traced: 323 us -> 104 us
  waiting for transfers between devices: 273 us -> 5.01 us
  blocking collectives: 0 us -> 73 us
  matrix products: 18.3 us -> 0 us
  between operations: 15.8 us -> 0.74 us
  Pallas kernels: 0 us -> 10.7 us
  other arithmetic: 6.53 us -> 2.88 us
  starting transfers between devices: 0.12 us -> 3.71 us
    reduce_scatter x1 -> x0, waiting for transfers between devices: 121 us -> none  [shards(): lax.psum_scatter(grad_lat, 'ctx', scatter_dimension=0, tiled=True)]
    unnamed x4 -> x0, waiting for transfers between devices: 84.9 us -> none
    all_to_all x0 -> x4, blocking collectives: none -> 73 us  [the longest x1 24.7 us: shards(): lax.all_to_all(jnp.broadcast_to(column[None], (16, 64, width)), ('yl', 'y...]
    all_gather x1 -> x0, waiting for transfers between devices: 67.2 us -> none  [shards(): shard_keys = lax.all_gather(latent, 'ctx', axis=0, tiled=True)]
    dot_general x7 -> x0, matrix products: 18.3 us -> none  [the longest x2 7.79 us: block_scores(): jnp.einsum('kc,rc->kr', key_block, query_flat, preferred_element_type=jnp...]
    pallas_call x0 -> x1, Pallas kernels: none -> 10.7 us  [attention_call(): pl.pallas_call(attention_kernel, out_shape=(jax.ShapeDtypeStruct((ROWS, W...]
    cond x11 -> x0, local copies, waits for them, and re-layouts: 6.06 us -> none  [the longest x1 6.03 us: backward_terms(): return lax.cond(any_live, backward_compute, skip, 0)]
    ppermute x0 -> x2, waiting for transfers between devices: none -> 5.01 us  [the longest x1 2.53 us: shards(): other = lax.ppermute(own, 'c', swap)]
  transfers between devices with their start and end apart: 3 -> 2, of which waited for: 3 -> 2; matrix products, arithmetic and copies ran while one was open for 1% -> 0% of each run, Pallas kernels for 0% -> 0%
where the time goes in v1:
time: 104 us
  blocking collectives  73 us (70%)
  Pallas kernels  10.7 us (10%)
  local copies, waits for them, and re-layouts  7.73 us (7%)
  waiting for transfers between devices  5.01 us (5%)
  starting transfers between devices  3.71 us (4%)
  other arithmetic  2.88 us (3%)
    all_to_all x1, blocking collectives, shards(): lax.all_to_all(jnp.broadcast_to(column[None], (16, 64, width)), ('yl', 'y...  24.7 us
    all_to_all x1, blocking collectives, shards(): lax.all_to_all(part.reshape(16, 64, width), ('yl', 'yh', 'x'), 0, 0, tile...  22.2 us
    all_to_all x1, blocking collectives, shards(): lax.all_to_all(jnp.broadcast_to(piece[None], (8, 8, width)), 'z', 0, 0, t...  16.3 us
    pallas_call x1, Pallas kernels, attention_call(): pl.pallas_call(attention_kernel, out_shape=(jax.ShapeDtypeStruct((ROWS, W...  10.7 us
    all_to_all x1, blocking collectives, shards(): part = lax.all_to_all(part.reshape(8, 8, width), 'z', 0, 0, tiled=True)  9.78 us
    ppermute x1, starting transfers between devices, shards(): other = lax.ppermute(own, 'c', swap)  3.25 us
    unnamed x10, local copies, waits for them, and re-layouts  3 us
    ppermute x1, waiting for transfers between devices, shards(): other = lax.ppermute(own, 'c', swap)  2.53 us
  transfers between devices with their start and end apart: 2, of which 2 were waited for; matrix products, arithmetic and copies ran while one was open for 0% of the time, Pallas kernels for 0%

profile of v1, /device:TPU:1, one launch (start us, length us, event | category | flops | bytes accessed | tf_op | source)
XLA Modules:
  0.0 103.8 jit_solution(7189848701285382388)
XLA Ops:
  0.6 0.0 copy-start
  0.7 0.9 copy-done
  1.5 16.3 %all_to_all.20 = bf16[8,8,576]{2,1,0:T(8,128)(2,1)S(1)} all-to-all(bf16[8,8,576]{2,1,0:T(8,128)(2,1)S(1)} %broadcast_in_dim.6), channel_id=1, replica_groups=mesh['z'=8,'yl'=2,'c'=2,'yh'=2,'x'=4] {'z'}, dimensions={0} | all-to-all | bytes 147456 | tf_op jit(solution)/shard_map/all_to_all | solution.py:130
  17.9 0.1 broadcast_in_dim.15
  18.0 24.7 %all_to_all.21 = bf16[16,64,576]{2,1,0:T(8,128)(2,1)S(1)} all-to-all(bf16[16,64,576]{2,1,0:T(8,128)(2,1)S(1)} %broadcast_in_dim.15), channel_id=1, replica_groups=mesh['z'=8,'yl'=2,'c'=2,'yh'=2,'x'=4] {'yl','yh','x'}, dimensions={0} | all-to-all | bytes 2359296 | tf_op jit(solution)/shard_map/all_to_all | solution.py:133
  42.8 0.6 copy.10
  43.4 0.0 copy-start.2
  43.4 0.0 copy-start.4
  43.4 3.2 %collective-permute-start = (bf16[1024,576]{0,1:T(8,128)(2,1)S(1)}, bf16[1024,576]{0,1:T(8,128)(2,1)}, u32[]{:S(2)}, u32[]{:S(2)}) collective-permute-start(bf16[1024,576]{0,1:T(8,128)(2,1)S(1)} %copy.10), channel_id=1, source_target_pairs={{0,8},{8,0},{1,9},{9,1},{2,10},{10,2},{3,11},{11,3},{4,12},{12,4},... | collective-permute-start | bytes 3538952 | tf_op jit(solution)/shard_map/ppermute | solution.py:137
  46.7 0.1 pad_add_fusion.where_ref
  46.7 2.5 %collective-permute-done = bf16[1024,576]{0,1:T(8,128)(2,1)} collective-permute-done((bf16[1024,576]{0,1:T(8,128)(2,1)S(1)}, bf16[1024,576]{0,1:T(8,128)(2,1)}, u32[]{:S(2)}, u32[]{:S(2)}) %collective-permute-start) | collective-permute-done | bytes 1179680 | tf_op jit(solution)/shard_map/ppermute | solution.py:137
  49.3 1.7 %copy.11.other_ref = bf16[1024,576]{1,0:T(8,128)(2,1)S(1)} copy(bf16[1024,576]{0,1:T(8,128)(2,1)} %collective-permute-done) | data formatting | bytes 2359296 | tf_op jit(solution)/shard_map/ppermute | solution.py:137
  50.9 0.0 copy-done.2
  51.0 0.0 copy-done.4
  51.0 0.0 copy-start.3
  51.0 1.0 copy-done.3
  52.0 10.7 %attention.1 = (bf16[512,576]{1,0:T(8,128)(2,1)}, f32[1024,576]{1,0:T(8,128)}, bf16[1024,576]{1,0:T(8,128)(2,1)S(1)}) custom-call(s32[64]{0:T(128)S(1)} %copy-done.4, s32[2]{0:T(128)S(1)} %pad_add_fusion.where_ref, bf16[1024,576]{1,0:T(8,128)(2,1)S(1)} %bitcast.10, bf16[1024,576]{1,0:T(8,128)(2,1)S(1)} %copy.11.other_ref, bf16[512,576]{1,0:T(8,128)(2,1)S(1)} %bitcast.11, ...), custom_call_target="tpu_custom_call" | custom-call | flops 5771362304 | bytes 10485760 | tf_op jit(solution)/shard_map/attention/pallas_call | solution.py:99
  62.7 0.0 copy-start.1
  62.7 1.1 %copy-done.1 = bf16[1024,576]{1,0:T(8,128)(2,1)} copy-done((bf16[1024,576]{1,0:T(8,128)(2,1)}, bf16[1024,576]{1,0:T(8,128)(2,1)S(1)}, u32[]{:S(2)}) %copy-start.1) | copy-done | bytes 1179672
  63.8 1.6 %copy.12 = bf16[1024,576]{0,1:T(8,128)(2,1)S(1)} copy(bf16[1024,576]{1,0:T(8,128)(2,1)} %copy-done.1) | data formatting | bytes 2359296 | tf_op jit(solution)/shard_map/attention/pallas_call | solution.py:99
  65.4 0.5 collective-permute-start.1
  65.8 2.5 %collective-permute-done.1 = bf16[1024,576]{0,1:T(8,128)(2,1)S(1)} collective-permute-done((bf16[1024,576]{0,1:T(8,128)(2,1)S(1)}, bf16[1024,576]{0,1:T(8,128)(2,1)S(1)}, u32[]{:S(2)}, u32[]{:S(2)}) %collective-permute-start.1) | collective-permute-done | bytes 1179680 | tf_op jit(solution)/shard_map/ppermute | solution.py:139
  68.3 0.7 copy.13
  69.0 2.0 %add_convert_fusion = bf16[1024,576]{1,0:T(8,128)(2,1)S(1)} fusion(f32[1024,576]{1,0:T(8,128)} %get-tuple-element.6, bf16[1024,576]{1,0:T(8,128)(2,1)S(1)} %copy.13), kind=kLoop, calls=%fused_computation | loop fusion | flops 1769472 | bytes 4718592 | tf_op jit(solution)/shard_map/convert_element_type | solution.py:140
  71.0 22.2 %all_to_all.22 = bf16[16,64,576]{2,1,0:T(8,128)(2,1)S(1)} all-to-all(bf16[16,64,576]{2,1,0:T(8,128)(2,1)S(1)} %bitcast.13), channel_id=1, replica_groups=mesh['z'=8,'yl'=2,'c'=2,'yh'=2,'x'=4] {'yl','yh','x'}, dimensions={0} | all-to-all | bytes 2359296 | tf_op jit(solution)/shard_map/all_to_all | solution.py:141
  93.2 0.2 reduce_sum.21
  93.4 9.8 %all_to_all.23 = bf16[8,8,576]{2,1,0:T(8,128)(2,1)S(1)} all-to-all(bf16[8,8,576]{2,1,0:T(8,128)(2,1)S(1)} %bitcast.14), channel_id=1, replica_groups=mesh['z'=8,'yl'=2,'c'=2,'yh'=2,'x'=4] {'z'}, dimensions={0} | all-to-all | bytes 147456 | tf_op jit(solution)/shard_map/all_to_all | solution.py:143
  103.1 0.6 convert_reduce_fusion
  (2 shorter events, 0.0 us)
Async XLA Ops:
  0.6 0.9 copy-start
  43.4 7.6 %copy-start.2 = (bf16[64,8,576]{2,1,0:T(8,128)(2,1)S(1)}, bf16[64,8,576]{2,1,0:T(8,128)(2,1)}, u32[]{:S(2)}) copy-start(bf16[64,8,576]{2,1,0:T(8,128)(2,1)} %param.4) | copy-start | bytes 1769476
  43.4 7.6 %copy-start.4 = (s32[64]{0:T(128)S(1)}, s32[64]{0:T(128)}, u32[]{:S(2)}) copy-start(s32[64]{0:T(128)} %order_ref.1) | copy-start | bytes 772
  43.4 5.9 %collective-permute-start = (bf16[1024,576]{0,1:T(8,128)(2,1)S(1)}, bf16[1024,576]{0,1:T(8,128)(2,1)}, u32[]{:S(2)}, u32[]{:S(2)}) collective-permute-start(bf16[1024,576]{0,1:T(8,128)(2,1)S(1)} %copy.10), channel_id=1, source_target_pairs={{0,8},{8,0},{1,9},{9,1},{2,10},{10,2},{3,11},{11,3},{4,12},{12,4},... | collective-permute-start | bytes 3538952 | tf_op jit(solution)/shard_map/ppermute | solution.py:137
  51.0 1.0 %copy-start.3 = (bf16[64,8,512]{2,1,0:T(8,128)(2,1)S(1)}, bf16[64,8,512]{2,1,0:T(8,128)(2,1)}, u32[]{:S(2)}) copy-start(bf16[64,8,512]{2,1,0:T(8,128)(2,1)} %param.6) | copy-start | bytes 1572868
  62.7 1.1 %copy-start.1 = (bf16[1024,576]{1,0:T(8,128)(2,1)}, bf16[1024,576]{1,0:T(8,128)(2,1)S(1)}, u32[]{:S(2)}) copy-start(bf16[1024,576]{1,0:T(8,128)(2,1)S(1)} %get-tuple-element.7) | copy-start | bytes 3538948
  65.4 2.9 %collective-permute-start.1 = (bf16[1024,576]{0,1:T(8,128)(2,1)S(1)}, bf16[1024,576]{0,1:T(8,128)(2,1)S(1)}, u32[]{:S(2)}, u32[]{:S(2)}) collective-permute-start(bf16[1024,576]{0,1:T(8,128)(2,1)S(1)} %copy.12), channel_id=1, source_target_pairs={{0,8},{8,0},{1,9},{9,1},{2,10},{10,2},{3,11},{11,3},{4,12},{12,4},... | collective-permute-start | bytes 3538952 | tf_op jit(solution)/shard_map/ppermute | solution.py:139

commit v2 on v1

v2 whole, which is shorter than its diff:
```python
import itertools

import jax
import jax.numpy as jnp
from jax import lax
from jax.experimental import pallas as pl
from jax.experimental.pallas import tpu as pltpu
from jax.sharding import Mesh, PartitionSpec as P

SIZES = (8, 2, 2, 2, 4)
CTX = ("z", "yl", "c")
HEAD = ("yh", "x")
ALL = CTX + HEAD
KV_RANK = 512
WIDTH = 576
SENT = 640
SCALE = 192.0 ** (-0.5)
LOW = -1e30
ROWS = 512
PART = 256
bf16, f32 = jnp.bfloat16, jnp.float32
FORWARD = (((0, 0),), ((0, 1), (0, 3)), ((0, 2), (1, 0), (1, 1), (1, 3)), ((1, 2),))
BACKWARD = (((1, 2),), ((0, 2), (1, 1)), ((0, 1), (1, 3)), ((0, 3), (1, 0)), ((0, 0),))


def places():
    return itertools.product(*(range(n) for n in SIZES))


def flat(z, yl, c, yh, x):
    return (((z * 2 + yl) * 2 + c) * 2 + yh) * 4 + x


def first_groups():
    found = {}
    for z, yl, c, yh, x in places():
        found.setdefault((c, x) if c == 0 else (c, yl, yh), []).append(flat(z, yl, c, yh, x))
    return list(found.values())


def turn(value, shift):
    pairs = []
    for z, yl, c, yh, x in places():
        y = 2 * yh + yl
        if c == 0:
            to = flat(z, yl, c, yh, (x + shift) % 4)
        else:
            y = (y + shift) % 4
            to = flat(z, y % 2, c, y // 2, x)
        pairs.append((flat(z, yl, c, yh, x), to))
    return lax.ppermute(value, ALL, pairs)


def swap(value):
    return lax.ppermute(value, "c", [(0, 1), (1, 0)])


def nn(a, b):
    return lax.dot_general(a, b, (((1,), (0,)), ((), ())), preferred_element_type=f32)


def nt(a, b):
    return lax.dot_general(a, b, (((1,), (1,)), ((), ())), preferred_element_type=f32)


def tn(a, b):
    return lax.dot_general(a, b, (((0,), (0,)), ((), ())), preferred_element_type=f32)


def key_positions(order_ref, where_ref, key_core, shift):
    x = lax.rem(where_ref[2] + 4 - shift, 4)
    y = lax.rem(where_ref[3] + 4 - shift, 4)
    yl, yh = lax.rem(y, 2), y // 2
    sub = lax.broadcasted_iota(jnp.int32, (8, 128), 0)
    tiles = []
    for t in range(PART // 8):
        z, a, b = t // 4, (t // 2) % 2, t % 2
        first = ((z * 2 + a) * 2) * 2 + b
        second = ((z * 2 + yl) * 2 + 1) * 2 + yh
        block = jnp.where(key_core == 0, first, second)
        eighth = jnp.where(key_core == 0, x, t % 4)
        tiles.append(sub + (order_ref[block] * 32 + eighth * 8))
    column = jnp.concatenate(tiles, axis=0)
    return jnp.concatenate([column] * (ROWS // 128), axis=1)


def forward_kernel(parts, order_ref, where_ref, stat_ref, *refs):
    n = len(parts)
    key_refs, (q_ref, g_ref), (stat_out, p_out, vp_out) = refs[:n], refs[n:n + 2], refs[n + 2:]
    ctx, core = where_ref[0], where_ref[1]
    tok = lax.broadcasted_iota(jnp.int32, (1, ROWS), 1) // 8
    query_pos = jnp.where(
        tok < 32, order_ref[2 * ctx] * 32 + tok, order_ref[2 * ctx + 1] * 32 + tok - 32
    )
    q, g = q_ref[...], g_ref[...]
    running_max, total, weighted = stat_ref[0:1, :], stat_ref[1:2, :], stat_ref[2:3, :]
    for i, ((half, shift), k_ref) in enumerate(zip(parts, key_refs)):
        key_pos = key_positions(order_ref, where_ref, core if half == 0 else 1 - core, shift)
        visible = key_pos <= query_pos
        scores = jnp.where(visible, nt(k_ref[:, :WIDTH], q) * SCALE, LOW)
        value_prod = nt(k_ref[:, :KV_RANK], g)
        new_max = jnp.maximum(running_max, jnp.max(scores, axis=0, keepdims=True))
        carry = jnp.exp(running_max - new_max)
        p = jnp.where(visible, jnp.exp(scores - new_max), 0.0)
        total = total * carry + jnp.sum(p, axis=0, keepdims=True)
        weighted = weighted * carry + jnp.sum(p * value_prod, axis=0, keepdims=True)
        running_max = new_max
        p_out[i * PART:(i + 1) * PART, :] = p
        vp_out[i * PART:(i + 1) * PART, :] = value_prod
        stat_out[3 + i:4 + i, :] = new_max
    stat_out[0:1, :] = running_max
    stat_out[1:2, :] = total
    stat_out[2:3, :] = weighted


def backward_kernel(parts, last_ref, *refs):
    n = len(parts)
    q, g = refs[3 * n][...], refs[3 * n + 1][...]
    outs = refs[3 * n + 2:]
    inv = 1.0 / last_ref[1:2, :]
    delta = last_ref[2:3, :] * inv
    for i, (place, _) in enumerate(parts):
        stat_ref, p_ref, vp_ref = refs[3 * i:3 * i + 3]
        out_ref, ds_ref = outs[2 * i:2 * i + 2]
        rows = slice(place * PART, (place + 1) * PART)
        factor = jnp.exp(stat_ref[3 + place:4 + place, :] - last_ref[0:1, :]) * inv
        attention = p_ref[rows, :] * factor
        ds = (SCALE * attention * (vp_ref[rows, :] - delta)).astype(bf16)
        ds_ref[...] = ds
        out_ref[:, :KV_RANK] = (nn(ds, q[:, :KV_RANK]) + nn(attention.astype(bf16), g)).astype(out_ref.dtype)
        rope = nn(ds, q[:, KV_RANK:])
        out_ref[:, KV_RANK:] = jnp.concatenate([rope, jnp.zeros_like(rope)], axis=1).astype(out_ref.dtype)


def query_kernel(*refs):
    out = refs[-1]
    ds = jnp.concatenate([r[...] for r in refs[0:-1:2]], axis=0)
    keys = jnp.concatenate([r[:, :WIDTH] for r in refs[1:-1:2]], axis=0)
    out[...] = tn(ds, keys).astype(bf16)


VMEM = pl.BlockSpec(memory_space=pltpu.VMEM)
SMEM = pl.BlockSpec(memory_space=pltpu.SMEM)
LIGHT = pl.CostEstimate(flops=1024, bytes_accessed=1024, transcendentals=0)


def forward_call(parts, order, where, stat, keys, q, g):
    n = len(parts)
    return pl.pallas_call(
        lambda *refs: forward_kernel(parts, *refs),
        out_shape=(
            jax.ShapeDtypeStruct((8, ROWS), f32),
            jax.ShapeDtypeStruct((n * PART, ROWS), f32),
            jax.ShapeDtypeStruct((n * PART, ROWS), f32),
        ),
        in_specs=[SMEM, SMEM] + [VMEM] * (n + 3),
        out_specs=(VMEM,) * 3,
        compiler_params=pltpu.CompilerParams(vmem_limit_bytes=16 * 2**20),
        cost_estimate=LIGHT,
        name="forward_" + "_".join(f"{h}{s}" for h, s in parts),
    )(order, where, stat, *keys, q, g)


def backward_call(wanted, last, saved, q, g):
    parts = [(saved[w][0], w) for w in wanted]
    shapes = []
    for half, _ in wanted:
        shapes.append(jax.ShapeDtypeStruct((PART, SENT), bf16 if half else f32))
        shapes.append(jax.ShapeDtypeStruct((PART, ROWS), bf16))
    out = pl.pallas_call(
        lambda *refs: backward_kernel(parts, *refs),
        out_shape=shapes,
        in_specs=[VMEM] * (3 * len(parts) + 3),
        out_specs=[VMEM] * len(shapes),
        compiler_params=pltpu.CompilerParams(vmem_limit_bytes=16 * 2**20),
        cost_estimate=LIGHT,
        name="backward_" + "_".join(f"{h}{s}" for h, s in wanted),
    )(last, *[a for w in wanted for a in saved[w][1:]], q, g)
    return {w: (out[2 * i], out[2 * i + 1]) for i, w in enumerate(wanted)}


def query_call(pairs):
    return pl.pallas_call(
        query_kernel,
        out_shape=jax.ShapeDtypeStruct((ROWS, WIDTH), bf16),
        in_specs=[VMEM] * (2 * len(pairs)),
        out_specs=VMEM,
        compiler_params=pltpu.CompilerParams(vmem_limit_bytes=16 * 2**20),
        cost_estimate=LIGHT,
        name="query_grad",
    )(*[a for pair in pairs for a in pair])


def shards(queries, latent, grad_out, block_order):
    tok_rows, head_count, width = queries.shape
    q = queries.reshape(tok_rows * head_count, width)
    g = grad_out.reshape(tok_rows * head_count, KV_RANK)
    where = jnp.stack([
        lax.axis_index(CTX), lax.axis_index("c"), lax.axis_index("x"),
        2 * lax.axis_index("yh") + lax.axis_index("yl"),
    ]).astype(jnp.int32)
    groups = first_groups()
    piece = lax.dynamic_slice_in_dim(latent, lax.axis_index(HEAD) * 8, 8, 0)
    piece = jnp.pad(piece, ((0, 0), (0, SENT - WIDTH)))
    first = lax.all_to_all(
        jnp.broadcast_to(piece[None], (32, 8, SENT)), ALL, 0, 0, axis_index_groups=groups, tiled=True
    ).reshape(PART, SENT)
    keys = {(0, 0): first}
    for shift in (1, 3, 2):
        keys[0, shift] = turn(first, shift)
    stat = jnp.concatenate([jnp.full((1, ROWS), LOW, f32), jnp.zeros((7, ROWS), f32)])
    saved = {}
    for wanted in FORWARD:
        for half, shift in wanted:
            if half == 0:
                keys[0, shift], stat = lax.optimization_barrier((keys[0, shift], stat))
                keys[1, shift] = swap(keys[0, shift])
        stat, p, vp = forward_call(wanted, block_order, where, stat, [keys[w] for w in wanted], q, g)
        for i, w in enumerate(wanted):
            saved[w] = (i, stat, p, vp)
    last = stat
    done = {}
    sums = {}
    taken = {}
    for wanted in BACKWARD:
        done.update(backward_call(wanted, last, saved, q, g))
        for half, shift in wanted:
            if half:
                taken[shift] = swap(done[1, shift][0])
        for half, shift in wanted:
            if not half and shift:
                sums[shift] = (done[0, shift][0] + taken[shift].astype(f32)).astype(bf16)
                sums[shift], last = lax.optimization_barrier((sums[shift], last))
    both = done[0, 0][0] + taken[0].astype(f32)
    dq = query_call([(done[w][1], keys[w]) for wanted in BACKWARD for w in wanted])
    arrived = [turn(sums[s], 4 - s) for s in (2, 1, 3)]
    (arrived, dq) = lax.optimization_barrier((arrived, dq))
    arrived = [both] + [a.astype(f32) for a in arrived]
    part = (arrived[0] + arrived[1] + arrived[2] + arrived[3]).astype(bf16)
    part = lax.all_to_all(
        part.reshape(32, 8, SENT), ALL, 0, 0, axis_index_groups=groups, tiled=True
    )
    grad_latent = jnp.sum(part.astype(f32), axis=0)[:, :WIDTH]
    return dq.reshape(tok_rows, head_count, width), grad_latent


def solution(mesh):
    fine = Mesh(mesh.devices.reshape(SIZES), ALL)
    placed = (P(CTX, HEAD, None), P(CTX, None), P(CTX, HEAD, None), P())
    return jax.shard_map(
        shards, mesh=fine, in_specs=placed,
        out_specs=(P(CTX, HEAD, None), P(ALL, None)), check_vma=False,
    )
```

time: 104 us -> 82.7 us (0.80)
  blocking collectives: 73 us -> 43.3 us
  starting transfers between devices: 3.71 us -> 16.8 us
  waiting for transfers between devices: 5.01 us -> 2.26 us
  local copies, waits for them, and re-layouts: 7.73 us -> 5.45 us
  Pallas kernels: 10.7 us -> 12.6 us
  other arithmetic: 2.88 us -> 1.15 us
    all_to_all x4 -> x2, blocking collectives: 73 us -> 43.3 us  [the longest x1 23.7 us: shards(): lax.all_to_all(jnp.broadcast_to(piece[None], (32, 8, SENT)), ALL, 0, 0, a...]
    ppermute x2 -> x14, starting transfers between devices: 3.71 us -> 16.8 us  [the longest x8 10.2 us: swap(): return lax.ppermute(value, 'c', [(0, 1), (1, 0)])]
    ppermute x2 -> x14, waiting for transfers between devices: 5.01 us -> 2.26 us  [the longest x6 2.09 us: turn(): return lax.ppermute(value, ALL, pairs)]
    unnamed x10 -> x14, local copies, waits for them, and re-layouts: 3 us -> 5.41 us
    ppermute x2 -> x0, local copies, waits for them, and re-layouts: 2.39 us -> none  [the longest x1 1.68 us: shards(): other = lax.ppermute(own, 'c', swap)]
    pallas_call x1 -> x10, Pallas kernels: 10.7 us -> 12.6 us  [the longest x4 6.22 us: forward_call(): pl.pallas_call(lambda *refs: forward_kernel(parts, *refs), out_shape=(jax...]
    convert_element_type x1 -> x3, other arithmetic: 1.99 us -> 0.22 us  [shards(): sums[shift] = (done[0, shift][0] + taken[shift].astype(f32)).astype(bf16)]
    pallas_call x1 -> x0, local copies, waits for them, and re-layouts: 1.57 us -> none  [attention_call(): pl.pallas_call(attention_kernel, out_shape=(jax.ShapeDtypeStruct((ROWS, W...]
  transfers between devices with their start and end apart: 2 -> 14, of which waited for: 2 -> 2; matrix products, arithmetic and copies ran while one was open for 0% -> 0% of each run, Pallas kernels for 0% -> 13%
where the time goes in v2:
time: 82.7 us; the launch traced here: 82.3 us
  blocking collectives  43.3 us (52%)
  starting transfers between devices  16.8 us (20%)
  Pallas kernels  12.6 us (15%)
  local copies, waits for them, and re-layouts  5.45 us (7%)
  waiting for transfers between devices  2.26 us (3%)
  other arithmetic  1.15 us (1%)
    all_to_all x1, blocking collectives, shards(): lax.all_to_all(jnp.broadcast_to(piece[None], (32, 8, SENT)), ALL, 0, 0, a...  23.7 us
    all_to_all x1, blocking collectives, shards(): lax.all_to_all(part.reshape(32, 8, SENT), ALL, 0, 0, axis_index_groups=gr...  19.6 us
    ppermute x8, starting transfers between devices, swap(): return lax.ppermute(value, 'c', [(0, 1), (1, 0)])  10.2 us
    ppermute x6, starting transfers between devices, turn(): return lax.ppermute(value, ALL, pairs)  6.65 us
    pallas_call x4, Pallas kernels, forward_call(): pl.pallas_call(lambda *refs: forward_kernel(parts, *refs), out_shape=(jax...  6.22 us
    unnamed x14, local copies, waits for them, and re-layouts  5.41 us
    pallas_call x5, Pallas kernels, backward_call(): pl.pallas_call(lambda *refs: backward_kernel(parts, *refs), out_shape=sha...  3.67 us
    pallas_call x1, Pallas kernels, query_call(): pl.pallas_call(query_kernel, out_shape=jax.ShapeDtypeStruct((ROWS, WIDTH)...  2.68 us
  transfers between devices with their start and end apart: 14, of which 2 were waited for; matrix products, arithmetic and copies ran while one was open for 0% of the time, Pallas kernels for 13%

profile of v2, /device:TPU:1, one launch (start us, length us, event | category | flops | bytes accessed | tf_op | source)
XLA Modules:
  0.0 82.3 jit_solution(2893913760121962789)
XLA Ops:
  0.6 0.0 copy-start
  0.6 0.0 copy-start.2
  0.7 0.9 %copy-done = bf16[64,576]{1,0:T(8,128)(2,1)S(1)} copy-done((bf16[64,576]{1,0:T(8,128)(2,1)S(1)}, bf16[64,576]{1,0:T(8,128)(2,1)}, u32[]{:S(2)}) %copy-start) | copy-done | bytes 73752
  1.6 23.7 %all_to_all.10 = bf16[32,8,640]{2,1,0:T(8,128)(2,1)S(1)} all-to-all(bf16[32,8,640]{2,1,0:T(8,128)(2,1)S(1)} %broadcast_in_dim.2), channel_id=1, replica_groups={{0,4,16,20,32,36,48,52,64,68,80,84,96,100,112,116,128,132,144,148,160,1..., dimensions={0} | all-to-all | bytes 655360 | tf_op jit(solution)/shard_map/all_to_all | solution.py:205
  25.3 1.5 %collective-permute-start.2 = (bf16[256,640]{1,0:T(8,128)(2,1)S(1)}, bf16[256,640]{1,0:T(8,128)(2,1)S(1)}, u32[]{:S(2)}, u32[]{:S(2)}) collective-permute-start(bf16[256,640]{1,0:T(8,128)(2,1)S(1)} %bitcast.29), channel_id=1, source_target_pairs={{0,1},{1,2},{2,3},{3,0},{4,5},{5,6},{6,7},{7,4},{8,24},{9,25},{10,... | collective-permute-start | bytes 983048 | tf_op jit(solution)/shard_map/ppermute | solution.py:51
  26.8 1.7 %collective-permute-start.1 = (bf16[256,640]{1,0:T(8,128)(2,1)S(1)}, bf16[256,640]{1,0:T(8,128)(2,1)S(1)}, u32[]{:S(2)}, u32[]{:S(2)}) collective-permute-start(bf16[256,640]{1,0:T(8,128)(2,1)S(1)} %bitcast.30), channel_id=1, source_target_pairs={{0,3},{1,0},{2,1},{3,2},{4,7},{5,4},{6,5},{7,6},{8,28},{9,29},{10,... | collective-permute-start | bytes 983048 | tf_op jit(solution)/shard_map/ppermute | solution.py:51
  28.6 1.6 %collective-permute-start = (bf16[256,640]{1,0:T(8,128)(2,1)S(1)}, bf16[256,640]{1,0:T(8,128)(2,1)S(1)}, u32[]{:S(2)}, u32[]{:S(2)}) collective-permute-start(bf16[256,640]{1,0:T(8,128)(2,1)S(1)} %bitcast.31), channel_id=1, source_target_pairs={{0,2},{1,3},{2,0},{3,1},{4,6},{5,7},{6,4},{7,5},{8,12},{9,13},{10,... | collective-permute-start | bytes 983048 | tf_op jit(solution)/shard_map/ppermute | solution.py:51
  30.2 0.1 pad_add_fusion.refs_1_
  30.2 3.7 %collective-permute-start.3 = (bf16[256,640]{1,0:T(8,128)(2,1)S(1)}, bf16[256,640]{1,0:T(8,128)(2,1)S(1)}, u32[]{:S(2)}, u32[]{:S(2)}) collective-permute-start(bf16[256,640]{1,0:T(8,128)(2,1)S(1)} %bitcast.32), channel_id=1, source_target_pairs={{0,8},{8,0},{1,9},{9,1},{2,10},{10,2},{3,11},{11,3},{4,12},{12,4},... | collective-permute-start | bytes 983048 | tf_op jit(solution)/shard_map/ppermute | solution.py:55
  33.9 1.1 %copy-done.1 = bf16[64,8,576]{2,1,0:T(8,128)(2,1)S(1)} copy-done((bf16[64,8,576]{2,1,0:T(8,128)(2,1)S(1)}, bf16[64,8,576]{2,1,0:T(8,128)(2,1)}, u32[]{:S(2)}) %copy-start.1) | copy-done | bytes 589848
  35.0 1.0 %copy-done.3 = bf16[64,8,512]{2,1,0:T(8,128)(2,1)S(1)} copy-done((bf16[64,8,512]{2,1,0:T(8,128)(2,1)S(1)}, bf16[64,8,512]{2,1,0:T(8,128)(2,1)}, u32[]{:S(2)}) %copy-start.3) | copy-done | bytes 524312
  36.0 0.7 copy-done.5
  36.7 0.7 copy-done.6
  37.4 1.1 %forward_00.1 = (f32[8,512]{1,0:T(8,128)S(1)}, f32[256,512]{1,0:T(8,128)S(1)}, f32[256,512]{1,0:T(8,128)S(1)}) custom-call(s32[64]{0:T(128)S(1)} %copy-done.6, s32[4]{0:T(128)S(1)} %pad_add_fusion.refs_1_, f32[8,512]{1,0:T(8,128)S(1)} %copy-done.5, bf16[256,640]{1,0:T(8,128)(2,1)S(1)} %bitcast.33, bf16[512,576]{1,0:T(8,128)(2,1)S(1)} %bitcast.11, ...), custom_call_target="tpu_custom_call" | custom-call | flops 1024 | bytes 1024 | tf_op jit(solution)/shard_map/forward_00/pallas_call | solution.py:149
  38.5 0.0 collective-permute-done.2.refs_3_.refs_7_
  38.6 0.0 collective-permute-done.1.refs_4_.refs_11_
  38.6 1.7 %collective-permute-start.5 = (bf16[256,640]{1,0:T(8,128)(2,1)S(1)}, bf16[256,640]{1,0:T(8,128)(2,1)S(1)}, u32[]{:S(2)}, u32[]{:S(2)}) collective-permute-start(bf16[256,640]{1,0:T(8,128)(2,1)S(1)} %collective-permute-done.1.refs_4_.refs_11_), channel_id=1, source_target_pairs={{0,8},{8,0},{1,9},{9,1},{2,10},{10,2},{3,11},{11,3},{4,12},{12,4},... | collective-permute-start | bytes 983048 | tf_op jit(solution)/shard_map/ppermute | solution.py:55
  40.3 0.0 collective-permute-start.4
  40.3 1.0 %copy-done.4 = bf16[64,8,512]{2,1,0:T(8,128)(2,1)S(1)} copy-done((bf16[64,8,512]{2,1,0:T(8,128)(2,1)S(1)}, bf16[64,8,512]{2,1,0:T(8,128)(2,1)}, u32[]{:S(2)}) %copy-start.4) | copy-done | bytes 524312
  41.3 1.6 %forward_01_03.1 = (f32[8,512]{1,0:T(8,128)S(1)}, f32[512,512]{1,0:T(8,128)S(1)}, f32[512,512]{1,0:T(8,128)S(1)}) custom-call(s32[64]{0:T(128)S(1)} %copy-done.6, s32[4]{0:T(128)S(1)} %pad_add_fusion.refs_1_, f32[8,512]{1,0:T(8,128)S(1)} %get-tuple-element.52.refs_2_.refs_1_, bf16[256,640]{1,0:T(8,128)(2,1)S(1)} %collective-permute-done.2.refs_3_.refs_7_, ...), custom_call_target="tpu_custom_call" | custom-call | flops 1024 | bytes 1024 | tf_op jit(solution)/shard_map/forward_01_03/pallas_call | solution.py:149
  42.9 0.0 collective-permute-done.refs_3_
  42.9 0.6 collective-permute-start.6
  43.5 2.4 %forward_02_10_11_13.1 = (f32[8,512]{1,0:T(8,128)S(1)}, f32[1024,512]{1,0:T(8,128)S(1)}, f32[1024,512]{1,0:T(8,128)S(1)}) custom-call(s32[64]{0:T(128)S(1)} %copy-done.6, s32[4]{0:T(128)S(1)} %pad_add_fusion.refs_1_, f32[8,512]{1,0:T(8,128)S(1)} %get-tuple-element.56.refs_2_.refs_1_, bf16[256,640]{1,0:T(8,128)(2,1)S(1)} %collective-permute-done.refs_3_, ...), custom_call_target="tpu_custom_call" | custom-call | flops 1024 | bytes 1024 | tf_op jit(solution)/shard_map/forward_02_10_11_13/pallas_call | solution.py:149
  45.9 0.0 collective-permute-done.6.refs_3_.refs_1_
  45.9 1.1 %forward_12.1 = (f32[8,512]{1,0:T(8,128)S(1)}, f32[256,512]{1,0:T(8,128)S(1)}, f32[256,512]{1,0:T(8,128)S(1)}) custom-call(s32[64]{0:T(128)S(1)} %copy-done.6, s32[4]{0:T(128)S(1)} %pad_add_fusion.refs_1_, f32[8,512]{1,0:T(8,128)S(1)} %get-tuple-element.58.refs_2_.refs_1_.refs_4_, bf16[256,640]{1,0:T(8,128)(2,1)S(1)} %collective-permute-done.6.refs_3_.refs_1_, ...), custom_call_target="tpu_custom_call" | custom-call | flops 1024 | bytes 1024 | tf_op jit(solution)/shard_map/forward_12/pallas_call | solution.py:149
  47.1 0.5 backward_12.1
  47.6 0.1 collective-permute-start.7
  47.7 0.9 %backward_02_11.1 = (f32[256,640]{1,0:T(8,128)S(1)}, bf16[256,512]{1,0:T(8,128)(2,1)S(1)}, bf16[256,640]{1,0:T(8,128)(2,1)S(1)}, bf16[256,512]{1,0:T(8,128)(2,1)S(1)}) custom-call(f32[8,512]{1,0:T(8,128)S(1)} %get-tuple-element.84.refs_0_.refs_1_, f32[8,512]{1,0:T(8,128)S(1)} %get-tuple-element.58.refs_2_.refs_1_.refs_4_, ...), custom_call_target="tpu_custom_call" | custom-call | flops 1024 | bytes 1024 | tf_op jit(solution)/shard_map/backward_02_11/pallas_call | solution.py:170
  48.6 0.6 collective-permute-start.9
  49.2 0.2 collective-permute-done.7
  49.3 0.1 add_convert_fusion.3
  49.4 0.9 %backward_01_13.1 = (f32[256,640]{1,0:T(8,128)S(1)}, bf16[256,512]{1,0:T(8,128)(2,1)S(1)}, bf16[256,640]{1,0:T(8,128)(2,1)S(1)}, bf16[256,512]{1,0:T(8,128)(2,1)S(1)}) custom-call(f32[8,512]{1,0:T(8,128)S(1)} %get-tuple-element.84.refs_0_.refs_1_, f32[8,512]{1,0:T(8,128)S(1)} %get-tuple-element.56.refs_2_.refs_1_, f32[512,512]{1,0:T(8,128)S(1)} %get-tuple-element.68.refs_2_, ...), custom_call_target="tpu_custom_call" | custom-call | flops 1024 | bytes 1024 | tf_op jit(solution)/shard_map/backward_01_13/pallas_call | solution.py:170
  50.3 0.2 collective-permute-start.11
  50.5 0.2 collective-permute-start.8
  50.7 0.1 add_convert_fusion.2
  50.8 0.9 %backward_03_10.1 = (f32[256,640]{1,0:T(8,128)S(1)}, bf16[256,512]{1,0:T(8,128)(2,1)S(1)}, bf16[256,640]{1,0:T(8,128)(2,1)S(1)}, bf16[256,512]{1,0:T(8,128)(2,1)S(1)}) custom-call(f32[8,512]{1,0:T(8,128)S(1)} %get-tuple-element.84.refs_0_.refs_1_, f32[8,512]{1,0:T(8,128)S(1)} %get-tuple-element.56.refs_2_.refs_1_, f32[512,512]{1,0:T(8,128)S(1)} %get-tuple-element.68.refs_2_, ...), custom_call_target="tpu_custom_call" | custom-call | flops 1024 | bytes 1024 | tf_op jit(solution)/shard_map/backward_03_10/pallas_call | solution.py:170
  51.6 0.8 collective-permute-start.10
  52.4 0.0 collective-permute-done.11
  52.4 0.1 add_convert_fusion.1
  52.5 0.9 %collective-permute-start.12 = (bf16[256,640]{1,0:T(8,128)(2,1)S(1)}, bf16[256,640]{1,0:T(8,128)(2,1)S(1)}, u32[]{:S(2)}, u32[]{:S(2)}) collective-permute-start(bf16[256,640]{1,0:T(8,128)(2,1)S(1)} %add_convert_fusion.1), channel_id=1, source_target_pairs={{0,1},{1,2},{2,3},{3,0},{4,5},{5,6},{6,7},{7,4},{8,24},{9,25},{10,... | collective-permute-start | bytes 983048 | tf_op jit(solution)/shard_map/ppermute | solution.py:51
  53.4 3.3 %collective-permute-start.13 = (bf16[256,640]{1,0:T(8,128)(2,1)S(1)}, bf16[256,640]{1,0:T(8,128)(2,1)S(1)}, u32[]{:S(2)}, u32[]{:S(2)}) collective-permute-start(bf16[256,640]{1,0:T(8,128)(2,1)S(1)} %get-tuple-element.90), channel_id=1, source_target_pairs={{0,8},{8,0},{1,9},{9,1},{2,10},{10,2},{3,11},{11,3},{4,12},{12,4},... | collective-permute-start | bytes 983048 | tf_op jit(solution)/shard_map/ppermute | solution.py:55
  56.6 0.5 backward_00.1
  57.1 2.7 %query_grad.1 = bf16[512,576]{1,0:T(8,128)(2,1)} custom-call(bf16[256,512]{1,0:T(8,128)(2,1)S(1)} %get-tuple-element.77.refs_0_, bf16[256,640]{1,0:T(8,128)(2,1)S(1)} %collective-permute-done.6.refs_3_.refs_1_, bf16[256,512]{1,0:T(8,128)(2,1)S(1)} %get-tuple-element.78.refs_2_, bf16[256,640]{1,0:T(8,128)(2,1)S(1)} %collective-permute-done.refs_3_, ...), custom_call_target="tpu_custom_call" | custom-call | flops 1024 | bytes 1024 | tf_op jit(solution)/shard_map/query_grad/pallas_call | solution.py:183
  59.8 2.1 %collective-permute-done.12 = bf16[256,640]{1,0:T(8,128)(2,1)S(1)} collective-permute-done((bf16[256,640]{1,0:T(8,128)(2,1)S(1)}, bf16[256,640]{1,0:T(8,128)(2,1)S(1)}, u32[]{:S(2)}, u32[]{:S(2)}) %collective-permute-start.12) | collective-permute-done | bytes 327712 | tf_op jit(solution)/shard_map/ppermute | solution.py:51
  61.9 0.0 collective-permute-done.13
  61.9 0.2 fusion
  62.1 19.6 %all_to_all.11 = bf16[32,8,640]{2,1,0:T(8,128)(2,1)S(1)} all-to-all(bf16[32,8,640]{2,1,0:T(8,128)(2,1)S(1)} %fusion), channel_id=1, replica_groups={{0,4,16,20,32,36,48,52,64,68,80,84,96,100,112,116,128,132,144,148,160,1..., dimensions={0} | all-to-all | bytes 655360 | tf_op jit(solution)/shard_map/all_to_all | solution.py:240
  81.6 0.7 convert_reduce_fusion
  (15 shorter events, 0.1 us)
Async XLA Ops:
  0.6 0.9 %copy-start = (bf16[64,576]{1,0:T(8,128)(2,1)S(1)}, bf16[64,576]{1,0:T(8,128)(2,1)}, u32[]{:S(2)}) copy-start(bf16[64,576]{1,0:T(8,128)(2,1)} %param.5) | copy-start | bytes 221188
  0.6 39.7 %copy-start.2 = (bf16[64,8,576]{2,1,0:T(8,128)(2,1)S(1)}, bf16[64,8,576]{2,1,0:T(8,128)(2,1)}, u32[]{:S(2)}) copy-start(bf16[64,8,576]{2,1,0:T(8,128)(2,1)} %param.4) | copy-start | bytes 1769476
  25.3 13.3 %collective-permute-start.2 = (bf16[256,640]{1,0:T(8,128)(2,1)S(1)}, bf16[256,640]{1,0:T(8,128)(2,1)S(1)}, u32[]{:S(2)}, u32[]{:S(2)}) collective-permute-start(bf16[256,640]{1,0:T(8,128)(2,1)S(1)} %bitcast.29), channel_id=1, source_target_pairs={{0,1},{1,2},{2,3},{3,0},{4,5},{5,6},{6,7},{7,4},{8,24},{9,25},{10,... | collective-permute-start | bytes 983048 | tf_op jit(solution)/shard_map/ppermute | solution.py:51
  26.8 11.7 %collective-permute-start.1 = (bf16[256,640]{1,0:T(8,128)(2,1)S(1)}, bf16[256,640]{1,0:T(8,128)(2,1)S(1)}, u32[]{:S(2)}, u32[]{:S(2)}) collective-permute-start(bf16[256,640]{1,0:T(8,128)(2,1)S(1)} %bitcast.30), channel_id=1, source_target_pairs={{0,3},{1,0},{2,1},{3,2},{4,7},{5,4},{6,5},{7,6},{8,28},{9,29},{10,... | collective-permute-start | bytes 983048 | tf_op jit(solution)/shard_map/ppermute | solution.py:51
  28.6 14.3 %collective-permute-start = (bf16[256,640]{1,0:T(8,128)(2,1)S(1)}, bf16[256,640]{1,0:T(8,128)(2,1)S(1)}, u32[]{:S(2)}, u32[]{:S(2)}) collective-permute-start(bf16[256,640]{1,0:T(8,128)(2,1)S(1)} %bitcast.31), channel_id=1, source_target_pairs={{0,2},{1,3},{2,0},{3,1},{4,6},{5,7},{6,4},{7,5},{8,12},{9,13},{10,... | collective-permute-start | bytes 983048 | tf_op jit(solution)/shard_map/ppermute | solution.py:51
  30.2 13.3 %collective-permute-start.3 = (bf16[256,640]{1,0:T(8,128)(2,1)S(1)}, bf16[256,640]{1,0:T(8,128)(2,1)S(1)}, u32[]{:S(2)}, u32[]{:S(2)}) collective-permute-start(bf16[256,640]{1,0:T(8,128)(2,1)S(1)} %bitcast.32), channel_id=1, source_target_pairs={{0,8},{8,0},{1,9},{9,1},{2,10},{10,2},{3,11},{11,3},{4,12},{12,4},... | collective-permute-start | bytes 983048 | tf_op jit(solution)/shard_map/ppermute | solution.py:55
  33.9 1.1 %copy-start.1 = (bf16[64,8,576]{2,1,0:T(8,128)(2,1)S(1)}, bf16[64,8,576]{2,1,0:T(8,128)(2,1)}, u32[]{:S(2)}) copy-start(bf16[64,8,576]{2,1,0:T(8,128)(2,1)} %param.4) | copy-start | bytes 1769476
  35.0 1.0 %copy-start.3 = (bf16[64,8,512]{2,1,0:T(8,128)(2,1)S(1)}, bf16[64,8,512]{2,1,0:T(8,128)(2,1)}, u32[]{:S(2)}) copy-start(bf16[64,8,512]{2,1,0:T(8,128)(2,1)} %param.6) | copy-start | bytes 1572868
  36.0 0.7 copy-start.5
  36.7 0.7 copy-start.6
  38.6 5.0 %collective-permute-start.5 = (bf16[256,640]{1,0:T(8,128)(2,1)S(1)}, bf16[256,640]{1,0:T(8,128)(2,1)S(1)}, u32[]{:S(2)}, u32[]{:S(2)}) collective-permute-start(bf16[256,640]{1,0:T(8,128)(2,1)S(1)} %collective-permute-done.1.refs_4_.refs_11_), channel_id=1, source_target_pairs={{0,8},{8,0},{1,9},{9,1},{2,10},{10,2},{3,11},{11,3},{4,12},{12,4},... | collective-permute-start | bytes 983048 | tf_op jit(solution)/shard_map/ppermute | solution.py:55
  40.3 3.2 %collective-permute-start.4 = (bf16[256,640]{1,0:T(8,128)(2,1)S(1)}, bf16[256,640]{1,0:T(8,128)(2,1)S(1)}, u32[]{:S(2)}, u32[]{:S(2)}) collective-permute-start(bf16[256,640]{1,0:T(8,128)(2,1)S(1)} %collective-permute-done.2.refs_3_.refs_7_), channel_id=1, source_target_pairs={{0,8},{8,0},{1,9},{9,1},{2,10},{10,2},{3,11},{11,3},{4,12},{12,4},... | collective-permute-start | bytes 983048 | tf_op jit(solution)/shard_map/ppermute | solution.py:55
  40.3 1.0 %copy-start.4 = (bf16[64,8,512]{2,1,0:T(8,128)(2,1)S(1)}, bf16[64,8,512]{2,1,0:T(8,128)(2,1)}, u32[]{:S(2)}) copy-start(bf16[64,8,512]{2,1,0:T(8,128)(2,1)} %param.6) | copy-start | bytes 1572868
  42.9 3.0 %collective-permute-start.6 = (bf16[256,640]{1,0:T(8,128)(2,1)S(1)}, bf16[256,640]{1,0:T(8,128)(2,1)S(1)}, u32[]{:S(2)}, u32[]{:S(2)}) collective-permute-start(bf16[256,640]{1,0:T(8,128)(2,1)S(1)} %collective-permute-done.refs_3_), channel_id=1, source_target_pairs={{0,8},{8,0},{1,9},{9,1},{2,10},{10,2},{3,11},{11,3},{4,12},{12,4},... | collective-permute-start | bytes 983048 | tf_op jit(solution)/shard_map/ppermute | solution.py:55
  47.6 1.7 %collective-permute-start.7 = (bf16[256,640]{1,0:T(8,128)(2,1)S(1)}, bf16[256,640]{1,0:T(8,128)(2,1)S(1)}, u32[]{:S(2)}, u32[]{:S(2)}) collective-permute-start(bf16[256,640]{1,0:T(8,128)(2,1)S(1)} %get-tuple-element.65), channel_id=1, source_target_pairs={{0,8},{8,0},{1,9},{9,1},{2,10},{10,2},{3,11},{11,3},{4,12},{12,4},... | collective-permute-start | bytes 983048 | tf_op jit(solution)/shard_map/ppermute | solution.py:55
  48.6 2.1 %collective-permute-start.9 = (bf16[256,640]{1,0:T(8,128)(2,1)S(1)}, bf16[256,640]{1,0:T(8,128)(2,1)S(1)}, u32[]{:S(2)}, u32[]{:S(2)}) collective-permute-start(bf16[256,640]{1,0:T(8,128)(2,1)S(1)} %get-tuple-element.71), channel_id=1, source_target_pairs={{0,8},{8,0},{1,9},{9,1},{2,10},{10,2},{3,11},{11,3},{4,12},{12,4},... | collective-permute-start | bytes 983048 | tf_op jit(solution)/shard_map/ppermute | solution.py:55
  50.3 2.1 %collective-permute-start.11 = (bf16[256,640]{1,0:T(8,128)(2,1)S(1)}, bf16[256,640]{1,0:T(8,128)(2,1)S(1)}, u32[]{:S(2)}, u32[]{:S(2)}) collective-permute-start(bf16[256,640]{1,0:T(8,128)(2,1)S(1)} %get-tuple-element.75), channel_id=1, source_target_pairs={{0,8},{8,0},{1,9},{9,1},{2,10},{10,2},{3,11},{11,3},{4,12},{12,4},... | collective-permute-start | bytes 983048 | tf_op jit(solution)/shard_map/ppermute | solution.py:55
  50.5 9.3 %collective-permute-start.8 = (bf16[256,640]{1,0:T(8,128)(2,1)S(1)}, bf16[256,640]{1,0:T(8,128)(2,1)S(1)}, u32[]{:S(2)}, u32[]{:S(2)}) collective-permute-start(bf16[256,640]{1,0:T(8,128)(2,1)S(1)} %add_convert_fusion.3), channel_id=1, source_target_pairs={{0,2},{1,3},{2,0},{3,1},{4,6},{5,7},{6,4},{7,5},{8,12},{9,13},{10,... | collective-permute-start | bytes 983048 | tf_op jit(solution)/shard_map/ppermute | solution.py:51
  51.6 8.2 %collective-permute-start.10 = (bf16[256,640]{1,0:T(8,128)(2,1)S(1)}, bf16[256,640]{1,0:T(8,128)(2,1)S(1)}, u32[]{:S(2)}, u32[]{:S(2)}) collective-permute-start(bf16[256,640]{1,0:T(8,128)(2,1)S(1)} %add_convert_fusion.2), channel_id=1, source_target_pairs={{0,3},{1,0},{2,1},{3,2},{4,7},{5,4},{6,5},{7,6},{8,28},{9,29},{10,... | collective-permute-start | bytes 983048 | tf_op jit(solution)/shard_map/ppermute | solution.py:51
  52.5 9.4 %collective-permute-start.12 = (bf16[256,640]{1,0:T(8,128)(2,1)S(1)}, bf16[256,640]{1,0:T(8,128)(2,1)S(1)}, u32[]{:S(2)}, u32[]{:S(2)}) collective-permute-start(bf16[256,640]{1,0:T(8,128)(2,1)S(1)} %add_convert_fusion.1), channel_id=1, source_target_pairs={{0,1},{1,2},{2,3},{3,0},{4,5},{5,6},{6,7},{7,4},{8,24},{9,25},{10,... | collective-permute-start | bytes 983048 | tf_op jit(solution)/shard_map/ppermute | solution.py:51
  53.4 8.5 %collective-permute-start.13 = (bf16[256,640]{1,0:T(8,128)(2,1)S(1)}, bf16[256,640]{1,0:T(8,128)(2,1)S(1)}, u32[]{:S(2)}, u32[]{:S(2)}) collective-permute-start(bf16[256,640]{1,0:T(8,128)(2,1)S(1)} %get-tuple-element.90), channel_id=1, source_target_pairs={{0,8},{8,0},{1,9},{9,1},{2,10},{10,2},{3,11},{11,3},{4,12},{12,4},... | collective-permute-start | bytes 983048 | tf_op jit(solution)/shard_map/ppermute | solution.py:55

commit v3 on v2

v3 whole, which is shorter than its diff:
```python
import itertools

import jax
import jax.numpy as jnp
from jax import lax
from jax.experimental import pallas as pl
from jax.experimental.pallas import tpu as pltpu
from jax.sharding import Mesh, PartitionSpec as P

SIZES = (8, 2, 2, 2, 4)
CTX = ("z", "yl", "c")
HEAD = ("yh", "x")
ALL = CTX + HEAD
KV_RANK = 512
WIDTH = 576
SENT = 640
SCALE = 192.0 ** (-0.5)
LOW = -1e30
ROWS = 512
PART = 256
bf16, f32 = jnp.bfloat16, jnp.float32
FORWARD = (((0, 0),), ((0, 1), (0, 3)), ((1, 0), (1, 1), (1, 3)), ((0, 2), (1, 2)))
BACKWARD = (((1, 2),), ((1, 1), (1, 3), (1, 0)), ((0, 2),), ((0, 1), (0, 3)), ((0, 0),))
ORDER = tuple(w for call in FORWARD for w in call)


def places():
    return itertools.product(*(range(n) for n in SIZES))


def flat(z, yl, c, yh, x):
    return (((z * 2 + yl) * 2 + c) * 2 + yh) * 4 + x


def first_groups():
    found = {}
    for z, yl, c, yh, x in places():
        found.setdefault((c, x) if c == 0 else (c, yl, yh), []).append(flat(z, yl, c, yh, x))
    return list(found.values())


def turn(value, shift):
    pairs = []
    for z, yl, c, yh, x in places():
        y = 2 * yh + yl
        if c == 0:
            to = flat(z, yl, c, yh, (x + shift) % 4)
        else:
            y = (y + shift) % 4
            to = flat(z, y % 2, c, y // 2, x)
        pairs.append((flat(z, yl, c, yh, x), to))
    return lax.ppermute(value, ALL, pairs)


def swap(value):
    return lax.ppermute(value, "c", [(0, 1), (1, 0)])


def nn(a, b):
    return lax.dot_general(a, b, (((1,), (0,)), ((), ())), preferred_element_type=f32)


def tn(a, b):
    return lax.dot_general(a, b, (((0,), (0,)), ((), ())), preferred_element_type=f32)


def key_positions(order_ref, where_ref, key_core, shift):
    x = lax.rem(where_ref[2] + 4 - shift, 4)
    y = lax.rem(where_ref[3] + 4 - shift, 4)
    yl, yh = lax.rem(y, 2), y // 2
    sub = lax.broadcasted_iota(jnp.int32, (8, 128), 0)
    tiles = []
    for t in range(PART // 8):
        z, a, b = t // 4, (t // 2) % 2, t % 2
        first = ((z * 2 + a) * 2) * 2 + b
        second = ((z * 2 + yl) * 2 + 1) * 2 + yh
        block = jnp.where(key_core == 0, first, second)
        eighth = jnp.where(key_core == 0, x, t % 4)
        tiles.append(sub + (order_ref[block] * 32 + eighth * 8))
    return jnp.concatenate(tiles, axis=0)


def prepare_kernel(order_ref, where_ref, q_ref, g_ref, q_out, g_out, qt_out, gt_out, key_out, query_out):
    ctx, core = where_ref[0], where_ref[1]
    q, g = q_ref[...], g_ref[...]
    q_out[...] = q
    g_out[...] = g
    qt_out[...] = q.T
    gt_out[...] = g.T
    for i, (half, shift) in enumerate(ORDER):
        key_core = core if half == 0 else 1 - core
        key_out[i * PART:(i + 1) * PART, :] = key_positions(order_ref, where_ref, key_core, shift)
    tok = lax.broadcasted_iota(jnp.int32, (8, ROWS), 1) // 8
    query_out[...] = jnp.where(
        tok < 32, order_ref[2 * ctx] * 32 + tok, order_ref[2 * ctx + 1] * 32 + tok - 32
    )


def load_part(refs, width):
    rows = [r[:, :width] for r in refs]
    return rows[0] if len(rows) == 1 else jnp.concatenate(rows, axis=0)


def forward_kernel(parts, counts, *refs):
    query_pos_ref, key_pos_ref, stat_ref = refs[:3]
    key_refs, at = [], 3
    for count in counts:
        key_refs.append(refs[at:at + count])
        at += count
    qt_ref, gt_ref, stat_out, p_out, vp_out = refs[at:]
    query_pos = query_pos_ref[0:1, :]
    if stat_ref is None:
        running_max = jnp.full((1, ROWS), LOW, f32)
        total = weighted = jnp.zeros((1, ROWS), f32)
    else:
        running_max, total, weighted = stat_ref[0:1, :], stat_ref[1:2, :], stat_ref[2:3, :]
    qt, gt = qt_ref[...], gt_ref[...]
    for i, part in enumerate(parts):
        start = ORDER.index(part) * PART
        key_pos = key_pos_ref[start:start + PART, :]
        key_pos = jnp.concatenate([key_pos] * (ROWS // 128), axis=1)
        visible = key_pos <= query_pos
        scores = jnp.where(visible, nn(load_part(key_refs[i], WIDTH), qt) * SCALE, LOW)
        value_prod = nn(load_part(key_refs[i], KV_RANK), gt)
        new_max = jnp.maximum(running_max, jnp.max(scores, axis=0, keepdims=True))
        carry = jnp.exp(running_max - new_max)
        p = jnp.where(visible, jnp.exp(scores - new_max), 0.0)
        total = total * carry + jnp.sum(p, axis=0, keepdims=True)
        weighted = weighted * carry + jnp.sum(p * value_prod, axis=0, keepdims=True)
        running_max = new_max
        p_out[i * PART:(i + 1) * PART, :] = p
        vp_out[i * PART:(i + 1) * PART, :] = value_prod
        stat_out[3 + i:4 + i, :] = new_max
    stat_out[0:1, :] = running_max
    stat_out[1:2, :] = total
    stat_out[2:3, :] = weighted


def backward_kernel(parts, last_ref, *refs):
    at = sum(4 if added else 3 for _, added in parts)
    q, g = refs[at][...], refs[at + 1][...]
    outs = refs[at + 2:]
    inv = 1.0 / last_ref[1:2, :]
    delta = last_ref[2:3, :] * inv
    at = 0
    for i, (place, added) in enumerate(parts):
        stat_ref, p_ref, vp_ref = refs[at:at + 3]
        out_ref, ds_ref = outs[2 * i:2 * i + 2]
        rows = slice(place * PART, (place + 1) * PART)
        factor = jnp.exp(stat_ref[3 + place:4 + place, :] - last_ref[0:1, :]) * inv
        attention = p_ref[rows, :] * factor
        ds = (SCALE * attention * (vp_ref[rows, :] - delta)).astype(bf16)
        ds_ref[...] = ds
        term = nn(ds, q[:, :KV_RANK]) + nn(attention.astype(bf16), g)
        rope = nn(ds, q[:, KV_RANK:])
        if added:
            term = term + refs[at + 3][:, :KV_RANK].astype(f32)
            rope = rope + refs[at + 3][:, KV_RANK:WIDTH].astype(f32)
        out_ref[:, :KV_RANK] = term.astype(out_ref.dtype)
        out_ref[:, KV_RANK:] = jnp.concatenate([rope, jnp.zeros_like(rope)], axis=1).astype(out_ref.dtype)
        at += 4 if added else 3


def query_kernel(counts, *refs):
    out = refs[-1]
    ds, keys, at = [], [], 0
    for count in counts:
        ds.append(refs[at][...])
        keys.append(load_part(refs[at + 1:at + 1 + count], WIDTH))
        at += 1 + count
    out[...] = tn(jnp.concatenate(ds, axis=0), jnp.concatenate(keys, axis=0)).astype(bf16)


VMEM = pl.BlockSpec(memory_space=pltpu.VMEM)
SMEM = pl.BlockSpec(memory_space=pltpu.SMEM)
LIGHT = pl.CostEstimate(flops=1024, bytes_accessed=1024, transcendentals=0)
PARAMS = pltpu.CompilerParams(vmem_limit_bytes=20 * 2**20)


def call(kernel, name, shapes, smem, args, cost=LIGHT):
    return pl.pallas_call(
        kernel,
        out_shape=shapes,
        in_specs=[SMEM] * smem + [VMEM] * (len(args) - smem),
        out_specs=[VMEM] * len(shapes),
        compiler_params=PARAMS,
        cost_estimate=cost,
        name=name,
    )(*args)


def label(parts):
    return "_".join(f"{h}{s}" for h, s in parts)


def prepare_call(order, where, q, g):
    shapes = [jax.ShapeDtypeStruct(s, bf16) for s in (
        (ROWS, WIDTH), (ROWS, KV_RANK), (WIDTH, ROWS), (KV_RANK, ROWS))]
    shapes += [jax.ShapeDtypeStruct((8 * PART, 128), jnp.int32), jax.ShapeDtypeStruct((8, ROWS), jnp.int32)]
    return call(prepare_kernel, "prepare", shapes, 2, [order, where, q, g])


def forward_call(parts, query_pos, key_pos, stat, keys, qt, gt):
    n = len(parts)
    counts = [len(k) for k in keys]
    rows = [r for k in keys for r in k]
    shapes = [jax.ShapeDtypeStruct((8, ROWS), f32)] + [jax.ShapeDtypeStruct((n * PART, ROWS), f32)] * 2

    def kernel(*refs):
        if stat is None:
            refs = (*refs[:2], None, *refs[2:])
        forward_kernel(parts, counts, *refs)

    args = [query_pos, key_pos] + ([] if stat is None else [stat]) + rows + [qt, gt]
    return call(kernel, "forward_" + label(parts), shapes, 0, args)


def backward_call(wanted, last, saved, taken, q, g):
    parts = [(saved[w][0], w[0] == 0) for w in wanted]
    shapes, args = [], [last]
    for w in wanted:
        shapes.append(jax.ShapeDtypeStruct((PART, SENT), f32 if w == (0, 0) else bf16))
        shapes.append(jax.ShapeDtypeStruct((PART, ROWS), bf16))
        args += list(saved[w][1:]) + ([] if w[0] else [taken[w[1]]])
    out = call(lambda *refs: backward_kernel(parts, *refs), "backward_" + label(wanted), shapes, 0, args + [q, g],
               LIGHT)
    return {w: (out[2 * i], out[2 * i + 1]) for i, w in enumerate(wanted)}


def query_call(pairs):
    counts = [len(k) for _, k in pairs]
    args = [a for ds, k in pairs for a in (ds, *k)]
    shapes = [jax.ShapeDtypeStruct((ROWS, WIDTH), bf16)]
    return call(lambda *refs: query_kernel(counts, *refs), "query_grad", shapes, 0, args)[0]


def shards(queries, latent, grad_out, block_order):
    tok_rows, head_count, width = queries.shape
    q = queries.reshape(tok_rows * head_count, width)
    g = grad_out.reshape(tok_rows * head_count, KV_RANK)
    where = jnp.stack([
        lax.axis_index(CTX), lax.axis_index("c"), lax.axis_index("x"),
        2 * lax.axis_index("yh") + lax.axis_index("yl"),
    ]).astype(jnp.int32)
    groups = first_groups()
    piece = lax.dynamic_slice_in_dim(latent, lax.axis_index(HEAD) * 8, 8, 0)
    piece = jnp.pad(piece, ((0, 0), (0, SENT - WIDTH)))
    first = lax.all_to_all(
        jnp.broadcast_to(piece[None], (32, 8, SENT)), ALL, 0, 0, axis_index_groups=groups, tiled=True
    ).reshape(PART, SENT)
    q, g, first = lax.optimization_barrier((q, g, first))
    keys = {(0, 0): [first]}
    keys[0, 1] = [turn(first, 1)]
    keys[0, 3] = [turn(first, 3)]
    q, g, qt, gt, key_pos, query_pos = prepare_call(block_order, where, q, g)
    stat = None
    saved = {}
    for wanted in FORWARD:
        for w in wanted:
            if w[0] == 0:
                if w[1] == 2:
                    keys[w] = [turn(keys[0, 1][0][:PART // 2], 1), turn(keys[0, 3][0][PART // 2:], 3)]
                if stat is not None:
                    (keys[w], stat) = lax.optimization_barrier((keys[w], stat))
                keys[1, w[1]] = [swap(k) for k in keys[w]]
        stat, p, vp = forward_call(wanted, query_pos, key_pos, stat, [keys[w] for w in wanted], qt, gt)
        for i, w in enumerate(wanted):
            saved[w] = (i, stat, p, vp)
    last = stat
    done = {}
    taken = {}
    arrived = []
    for wanted in BACKWARD:
        done.update(backward_call(wanted, last, saved, taken, q, g))
        for half, shift in wanted:
            if half:
                taken[shift] = swap(done[1, shift][0])
            elif shift:
                value, last = lax.optimization_barrier((done[0, shift][0], last))
                arrived.append(turn(value, 4 - shift))
    dq = query_call([(done[w][1], keys[w]) for w in ORDER])
    (arrived, dq) = lax.optimization_barrier((arrived, dq))
    arrived = [done[0, 0][0]] + [a.astype(f32) for a in arrived]
    part = (arrived[0] + arrived[1] + arrived[2] + arrived[3]).astype(bf16)
    part = lax.all_to_all(
        part.reshape(32, 8, SENT), ALL, 0, 0, axis_index_groups=groups, tiled=True
    )
    grad_latent = jnp.sum(part.astype(f32), axis=0)[:, :WIDTH]
    return dq.reshape(tok_rows, head_count, width), grad_latent


def solution(mesh):
    fine = Mesh(mesh.devices.reshape(SIZES), ALL)
    placed = (P(CTX, HEAD, None), P(CTX, None), P(CTX, HEAD, None), P())
    return jax.shard_map(
        shards, mesh=fine, in_specs=placed,
        out_specs=(P(CTX, HEAD, None), P(ALL, None)), check_vma=False,
    )
```

time: 82.7 us -> 83.2 us (level)
  waiting for transfers between devices: 2.26 us -> 7.99 us
  local copies, waits for them, and re-layouts: 5.45 us -> 3.73 us
  blocking collectives: 43.3 us -> 41.9 us
  Pallas kernels: 12.6 us -> 11.3 us
  starting transfers between devices: 16.8 us -> 15.8 us
    ppermute x6 -> x7, waiting for transfers between devices: 2.09 us -> 5.8 us  [turn(): return lax.ppermute(value, ALL, pairs)]
    ppermute x8 -> x9, starting transfers between devices: 10.2 us -> 7.02 us  [swap(): return lax.ppermute(value, 'c', [(0, 1), (1, 0)])]
    ppermute x6 -> x7, starting transfers between devices: 6.65 us -> 8.81 us  [turn(): return lax.ppermute(value, ALL, pairs)]
    ppermute x8 -> x9, waiting for transfers between devices: 0.18 us -> 2.19 us  [swap(): return lax.ppermute(value, 'c', [(0, 1), (1, 0)])]
    unnamed x14 -> x8, local copies, waits for them, and re-layouts: 5.41 us -> 3.66 us
    all_to_all x1, blocking collectives: 19.6 us -> 18.2 us  [shards(): lax.all_to_all(part.reshape(32, 8, SENT), ALL, 0, 0, axis_index_groups=gr...]
    pallas_call x10 -> x11, Pallas kernels: 12.6 us -> 11.3 us  [call(): pl.pallas_call(kernel, out_shape=shapes, in_specs=[SMEM] * smem + [VMEM]...]
  transfers between devices with their start and end apart: 14 -> 16, of which waited for: 2 -> 6; matrix products, arithmetic and copies ran while one was open for 0% -> 0% of each run, Pallas kernels for 13% -> 12%
where the time goes in v3:
time: 83.2 us; the launch traced here: 82.5 us
  blocking collectives  41.9 us (50%)
  starting transfers between devices  15.8 us (19%)
  Pallas kernels  11.3 us (14%)
  waiting for transfers between devices  7.99 us (10%)
  local copies, waits for them, and re-layouts  3.73 us (4%)
  other arithmetic  0.88 us (1%)
    all_to_all x1, blocking collectives, shards(): lax.all_to_all(jnp.broadcast_to(piece[None], (32, 8, SENT)), ALL, 0, 0, a...  23.7 us
    all_to_all x1, blocking collectives, shards(): lax.all_to_all(part.reshape(32, 8, SENT), ALL, 0, 0, axis_index_groups=gr...  18.2 us
    pallas_call x11, Pallas kernels, call(): pl.pallas_call(kernel, out_shape=shapes, in_specs=[SMEM] * smem + [VMEM]...  11.3 us
    ppermute x7, starting transfers between devices, turn(): return lax.ppermute(value, ALL, pairs)  8.81 us
    ppermute x9, starting transfers between devices, swap(): return lax.ppermute(value, 'c', [(0, 1), (1, 0)])  7.02 us
    ppermute x7, waiting for transfers between devices, turn(): return lax.ppermute(value, ALL, pairs)  5.8 us
    unnamed x8, local copies, waits for them, and re-layouts  3.66 us
    ppermute x9, waiting for transfers between devices, swap(): return lax.ppermute(value, 'c', [(0, 1), (1, 0)])  2.19 us
  transfers between devices with their start and end apart: 16, of which 6 were waited for; matrix products, arithmetic and copies ran while one was open for 0% of the time, Pallas kernels for 12%

profile of v3, /device:TPU:1, one launch (start us, length us, event | category | flops | bytes accessed | tf_op | source)
XLA Modules:
  0.0 82.5 jit_solution(7109581427424049277)
XLA Ops:
  0.6 0.0 copy-start
  0.7 0.9 %copy-done = bf16[64,576]{1,0:T(8,128)(2,1)S(1)} copy-done((bf16[64,576]{1,0:T(8,128)(2,1)S(1)}, bf16[64,576]{1,0:T(8,128)(2,1)}, u32[]{:S(2)}) %copy-start) | copy-done | bytes 73752
  1.6 23.7 %all_to_all.10 = bf16[32,8,640]{2,1,0:T(8,128)(2,1)S(1)} all-to-all(bf16[32,8,640]{2,1,0:T(8,128)(2,1)S(1)} %broadcast_in_dim.2), channel_id=1, replica_groups={{0,4,16,20,32,36,48,52,64,68,80,84,96,100,112,116,128,132,144,148,160,1..., dimensions={0} | all-to-all | bytes 655360 | tf_op jit(solution)/shard_map/all_to_all | solution.py:248
  25.3 1.5 %collective-permute-start = (bf16[256,640]{1,0:T(8,128)(2,1)S(1)}, bf16[256,640]{1,0:T(8,128)(2,1)S(1)}, u32[]{:S(2)}, u32[]{:S(2)}) collective-permute-start(bf16[256,640]{1,0:T(8,128)(2,1)S(1)} %bitcast.11), channel_id=1, source_target_pairs={{0,1},{1,2},{2,3},{3,0},{4,5},{5,6},{6,7},{7,4},{8,24},{9,25},{10,... | collective-permute-start | bytes 983048 | tf_op jit(solution)/shard_map/ppermute | solution.py:52
  26.8 1.7 %collective-permute-start.2 = (bf16[256,640]{1,0:T(8,128)(2,1)S(1)}, bf16[256,640]{1,0:T(8,128)(2,1)S(1)}, u32[]{:S(2)}, u32[]{:S(2)}) collective-permute-start(bf16[256,640]{1,0:T(8,128)(2,1)S(1)} %bitcast.12), channel_id=1, source_target_pairs={{0,3},{1,0},{2,1},{3,2},{4,7},{5,4},{6,5},{7,6},{8,28},{9,29},{10,... | collective-permute-start | bytes 983048 | tf_op jit(solution)/shard_map/ppermute | solution.py:52
  28.6 0.1 pad_add_fusion.where_ref
  28.6 3.6 %collective-permute-start.4 = (bf16[256,640]{1,0:T(8,128)(2,1)S(1)}, bf16[256,640]{1,0:T(8,128)(2,1)S(1)}, u32[]{:S(2)}, u32[]{:S(2)}) collective-permute-start(bf16[256,640]{1,0:T(8,128)(2,1)S(1)} %bitcast.13), channel_id=1, source_target_pairs={{0,8},{8,0},{1,9},{9,1},{2,10},{10,2},{3,11},{11,3},{4,12},{12,4},... | collective-permute-start | bytes 983048 | tf_op jit(solution)/shard_map/ppermute | solution.py:56
  32.3 1.1 %copy-done.1 = bf16[64,8,576]{2,1,0:T(8,128)(2,1)S(1)} copy-done((bf16[64,8,576]{2,1,0:T(8,128)(2,1)S(1)}, bf16[64,8,576]{2,1,0:T(8,128)(2,1)}, u32[]{:S(2)}) %copy-start.1) | copy-done | bytes 589848
  33.4 1.0 %copy-done.2 = bf16[64,8,512]{2,1,0:T(8,128)(2,1)S(1)} copy-done((bf16[64,8,512]{2,1,0:T(8,128)(2,1)S(1)}, bf16[64,8,512]{2,1,0:T(8,128)(2,1)}, u32[]{:S(2)}) %copy-start.2) | copy-done | bytes 524312
  34.4 0.7 copy-done.3
  35.0 1.3 %prepare.1 = (bf16[512,576]{1,0:T(8,128)(2,1)S(1)}, bf16[512,512]{1,0:T(8,128)(2,1)S(1)}, bf16[576,512]{1,0:T(8,128)(2,1)S(1)}, bf16[512,512]{1,0:T(8,128)(2,1)S...) custom-call(s32[64]{0:T(128)S(1)} %copy-done.3, s32[4]{0:T(128)S(1)} %pad_add_fusion.where_ref, ...), custom_call_target="tpu_custom_call" | custom-call | flops 1024 | bytes 1024 | tf_op jit(solution)/shard_map/prepare/pallas_call | solution.py:181
  36.4 0.5 forward_00.1
  36.9 0.0 collective-permute-done.refs_3_
  36.9 0.3 collective-permute-start.6
  37.2 0.3 collective-permute-start.5
  37.6 0.1 collective-permute-start.1
  37.7 2.7 %collective-permute-start.3 = (bf16[128,640]{1,0:T(8,128)(2,1)S(1)}, bf16[128,640]{1,0:T(8,128)(2,1)S(1)}, u32[]{:S(2)}, u32[]{:S(2)}) collective-permute-start(bf16[128,640]{1,0:T(8,128)(2,1)S(1)} %slice.10), channel_id=1, source_target_pairs={{0,3},{1,0},{2,1},{3,2},{4,7},{5,4},{6,5},{7,6},{8,28},{9,29},{10,... | collective-permute-start | bytes 491528 | tf_op jit(solution)/shard_map/ppermute | solution.py:52
  40.3 0.9 %forward_01_03.1 = (f32[8,512]{1,0:T(8,128)S(1)}, f32[512,512]{1,0:T(8,128)S(1)}, f32[512,512]{1,0:T(8,128)S(1)}) custom-call(s32[8,512]{1,0:T(8,128)S(1)} %get-tuple-element.58.refs_0_, s32[2048,128]{1,0:T(8,128)S(1)} %get-tuple-element.59.refs_1_, f32[8,512]{1,0:T(8,128)S(1)} %get-tuple-element.67.refs_2_.refs_1_, ...), custom_call_target="tpu_custom_call" | custom-call | flops 1024 | bytes 1024 | tf_op jit(solution)/shard_map/forward_01_03/pallas_call | solution.py:181
  41.3 0.0 collective-permute-done.6.refs_5_.refs_11_
  41.3 0.0 collective-permute-done.5.refs_4_.refs_9_
  41.3 1.3 %forward_10_11_13.1 = (f32[8,512]{1,0:T(8,128)S(1)}, f32[768,512]{1,0:T(8,128)S(1)}, f32[768,512]{1,0:T(8,128)S(1)}) custom-call(s32[8,512]{1,0:T(8,128)S(1)} %get-tuple-element.58.refs_0_, s32[2048,128]{1,0:T(8,128)S(1)} %get-tuple-element.59.refs_1_, f32[8,512]{1,0:T(8,128)S(1)} %get-tuple-element.68.refs_2_.refs_1_.refs_5_, ...), custom_call_target="tpu_custom_call" | custom-call | flops 1024 | bytes 1024 | tf_op jit(solution)/shard_map/forward_10_11_13/pallas_call | solution.py:181
  42.6 0.7 collective-permute-done.1.refs_3_.refs_13_
  43.3 0.0 collective-permute-done.3.refs_4_.refs_14_
  43.3 1.4 %collective-permute-start.7 = (bf16[128,640]{1,0:T(8,128)(2,1)S(1)}, bf16[128,640]{1,0:T(8,128)(2,1)S(1)}, u32[]{:S(2)}, u32[]{:S(2)}) collective-permute-start(bf16[128,640]{1,0:T(8,128)(2,1)S(1)} %collective-permute-done.1.refs_3_.refs_13_), channel_id=1, source_target_pairs={{0,8},{8,0},{1,9},{9,1},{2,10},{10,2},{3,11},{11,3},{4,12},{12,4},... | collective-permute-start | bytes 491528 | tf_op jit(solution)/shard_map/ppermute | solution.py:56
  44.8 0.0 collective-permute-start.8
  44.8 1.0 %collective-permute-done.7.refs_5_.refs_16_ = bf16[128,640]{1,0:T(8,128)(2,1)S(1)} collective-permute-done((bf16[128,640]{1,0:T(8,128)(2,1)S(1)}, bf16[128,640]{1,0:T(8,128)(2,1)S(1)}, u32[]{:S(2)}, u32[]{:S(2)}) %collective-permute-start.7) | collective-permute-done | bytes 163872 | tf_op jit(solution)/shard_map/ppermute | solution.py:56
  45.8 0.4 collective-permute-done.8.refs_6_.refs_17_
  46.1 0.9 %forward_02_12.1 = (f32[8,512]{1,0:T(8,128)S(1)}, f32[512,512]{1,0:T(8,128)S(1)}, f32[512,512]{1,0:T(8,128)S(1)}) custom-call(s32[8,512]{1,0:T(8,128)S(1)} %get-tuple-element.58.refs_0_, s32[2048,128]{1,0:T(8,128)S(1)} %get-tuple-element.59.refs_1_, f32[8,512]{1,0:T(8,128)S(1)} %get-tuple-element.70.refs_2_.refs_1_.refs_4_.refs_7_, ...), custom_call_target="tpu_custom_call" | custom-call | flops 1024 | bytes 1024 | tf_op jit(solution)/shard_map/forward_02_12/pallas_call | solution.py:181
  47.1 0.5 backward_12.1
  47.6 0.5 collective-permute-start.9
  48.1 1.2 %backward_11_13_10.1 = (bf16[256,640]{1,0:T(8,128)(2,1)S(1)}, bf16[256,512]{1,0:T(8,128)(2,1)S(1)}, bf16[256,640]{1,0:T(8,128)(2,1)S(1)}, bf16[256,512]{1,0:T(8,...) custom-call(f32[8,512]{1,0:T(8,128)S(1)} %get-tuple-element.93.refs_0_.refs_1_, ...), custom_call_target="tpu_custom_call" | custom-call | flops 1024 | bytes 1024 | tf_op jit(solution)/shard_map/backward_11_13_10/pallas_call | solution.py:181
  49.3 0.4 collective-permute-start.11
  49.7 0.2 collective-permute-start.12
  49.9 0.3 collective-permute-start.15
  50.2 0.5 backward_02.1
  50.7 0.3 collective-permute-done.11.refs_4_
  51.0 0.5 collective-permute-done.12.refs_8_
  51.5 0.9 %backward_01_03.1 = (bf16[256,640]{1,0:T(8,128)(2,1)S(1)}, bf16[256,512]{1,0:T(8,128)(2,1)S(1)}, bf16[256,640]{1,0:T(8,128)(2,1)S(1)}, bf16[256,512]{1,0:T(8,128)(2,1)S(1)}) custom-call(f32[8,512]{1,0:T(8,128)S(1)} %get-tuple-element.93.refs_0_.refs_1_, f32[8,512]{1,0:T(8,128)S(1)} %get-tuple-element.68.refs_2_.refs_1_.refs_5_, ...), custom_call_target="tpu_custom_call" | custom-call | flops 1024 | bytes 1024 | tf_op jit(solution)/shard_map/backward_01_03/pallas_call | solution.py:181
  52.4 0.1 collective-permute-start.14
  52.5 2.7 %collective-permute-start.13 = (bf16[256,640]{1,0:T(8,128)(2,1)S(1)}, bf16[256,640]{1,0:T(8,128)(2,1)S(1)}, u32[]{:S(2)}, u32[]{:S(2)}) collective-permute-start(bf16[256,640]{1,0:T(8,128)(2,1)S(1)} %get-tuple-element.89), channel_id=1, source_target_pairs={{0,3},{1,0},{2,1},{3,2},{4,7},{5,4},{6,5},{7,6},{8,28},{9,29},{10,... | collective-permute-start | bytes 983048 | tf_op jit(solution)/shard_map/ppermute | solution.py:52
  55.1 0.0 collective-permute-start.10
  55.2 0.0 collective-permute-done.15.refs_4_
  55.2 0.5 backward_00.1
  55.7 2.7 %query_grad.1 = bf16[512,576]{1,0:T(8,128)(2,1)} custom-call(bf16[256,512]{1,0:T(8,128)(2,1)S(1)} %get-tuple-element.97.refs_0_, bf16[256,640]{1,0:T(8,128)(2,1)S(1)} %bitcast.15, bf16[256,512]{1,0:T(8,128)(2,1)S(1)} %get-tuple-element.98.refs_2_, bf16[256,640]{1,0:T(8,128)(2,1)S(1)} %collective-permute-done.refs_3_, ...), custom_call_target="tpu_custom_call" | custom-call | flops 1024 | bytes 1024 | tf_op jit(solution)/shard_map/query_grad/pallas_call | solution.py:181
  58.4 5.0 %collective-permute-done.14 = bf16[256,640]{1,0:T(8,128)(2,1)S(1)} collective-permute-done((bf16[256,640]{1,0:T(8,128)(2,1)S(1)}, bf16[256,640]{1,0:T(8,128)(2,1)S(1)}, u32[]{:S(2)}, u32[]{:S(2)}) %collective-permute-start.14) | collective-permute-done | bytes 327712 | tf_op jit(solution)/shard_map/ppermute | solution.py:52
  63.4 0.1 fusion
  63.6 18.2 %all_to_all.11 = bf16[32,8,640]{2,1,0:T(8,128)(2,1)S(1)} all-to-all(bf16[32,8,640]{2,1,0:T(8,128)(2,1)S(1)} %fusion), channel_id=1, replica_groups={{0,4,16,20,32,36,48,52,64,68,80,84,96,100,112,116,128,132,144,148,160,1..., dimensions={0} | all-to-all | bytes 655360 | tf_op jit(solution)/shard_map/all_to_all | solution.py:285
  81.8 0.7 convert_reduce_fusion
  (13 shorter events, 0.1 us)
Async XLA Ops:
  0.6 0.9 %copy-start = (bf16[64,576]{1,0:T(8,128)(2,1)S(1)}, bf16[64,576]{1,0:T(8,128)(2,1)}, u32[]{:S(2)}) copy-start(bf16[64,576]{1,0:T(8,128)(2,1)} %param.5) | copy-start | bytes 221188
  25.3 11.6 %collective-permute-start = (bf16[256,640]{1,0:T(8,128)(2,1)S(1)}, bf16[256,640]{1,0:T(8,128)(2,1)S(1)}, u32[]{:S(2)}, u32[]{:S(2)}) collective-permute-start(bf16[256,640]{1,0:T(8,128)(2,1)S(1)} %bitcast.11), channel_id=1, source_target_pairs={{0,1},{1,2},{2,3},{3,0},{4,5},{5,6},{6,7},{7,4},{8,24},{9,25},{10,... | collective-permute-start | bytes 983048 | tf_op jit(solution)/shard_map/ppermute | solution.py:52
  26.8 10.1 %collective-permute-start.2 = (bf16[256,640]{1,0:T(8,128)(2,1)S(1)}, bf16[256,640]{1,0:T(8,128)(2,1)S(1)}, u32[]{:S(2)}, u32[]{:S(2)}) collective-permute-start(bf16[256,640]{1,0:T(8,128)(2,1)S(1)} %bitcast.12), channel_id=1, source_target_pairs={{0,3},{1,0},{2,1},{3,2},{4,7},{5,4},{6,5},{7,6},{8,28},{9,29},{10,... | collective-permute-start | bytes 983048 | tf_op jit(solution)/shard_map/ppermute | solution.py:52
  28.6 12.6 %collective-permute-start.4 = (bf16[256,640]{1,0:T(8,128)(2,1)S(1)}, bf16[256,640]{1,0:T(8,128)(2,1)S(1)}, u32[]{:S(2)}, u32[]{:S(2)}) collective-permute-start(bf16[256,640]{1,0:T(8,128)(2,1)S(1)} %bitcast.13), channel_id=1, source_target_pairs={{0,8},{8,0},{1,9},{9,1},{2,10},{10,2},{3,11},{11,3},{4,12},{12,4},... | collective-permute-start | bytes 983048 | tf_op jit(solution)/shard_map/ppermute | solution.py:56
  32.3 1.1 %copy-start.1 = (bf16[64,8,576]{2,1,0:T(8,128)(2,1)S(1)}, bf16[64,8,576]{2,1,0:T(8,128)(2,1)}, u32[]{:S(2)}) copy-start(bf16[64,8,576]{2,1,0:T(8,128)(2,1)} %param.4) | copy-start | bytes 1769476
  33.4 1.0 %copy-start.2 = (bf16[64,8,512]{2,1,0:T(8,128)(2,1)S(1)}, bf16[64,8,512]{2,1,0:T(8,128)(2,1)}, u32[]{:S(2)}) copy-start(bf16[64,8,512]{2,1,0:T(8,128)(2,1)} %param.6) | copy-start | bytes 1572868
  34.4 0.7 copy-start.3
  36.9 4.3 %collective-permute-start.6 = (bf16[256,640]{1,0:T(8,128)(2,1)S(1)}, bf16[256,640]{1,0:T(8,128)(2,1)S(1)}, u32[]{:S(2)}, u32[]{:S(2)}) collective-permute-start(bf16[256,640]{1,0:T(8,128)(2,1)S(1)} %collective-permute-done.2.refs_4_.refs_5_), channel_id=1, source_target_pairs={{0,8},{8,0},{1,9},{9,1},{2,10},{10,2},{3,11},{11,3},{4,12},{12,4},... | collective-permute-start | bytes 983048 | tf_op jit(solution)/shard_map/ppermute | solution.py:56
  37.2 4.0 %collective-permute-start.5 = (bf16[256,640]{1,0:T(8,128)(2,1)S(1)}, bf16[256,640]{1,0:T(8,128)(2,1)S(1)}, u32[]{:S(2)}, u32[]{:S(2)}) collective-permute-start(bf16[256,640]{1,0:T(8,128)(2,1)S(1)} %collective-permute-done.refs_3_), channel_id=1, source_target_pairs={{0,8},{8,0},{1,9},{9,1},{2,10},{10,2},{3,11},{11,3},{4,12},{12,4},... | collective-permute-start | bytes 983048 | tf_op jit(solution)/shard_map/ppermute | solution.py:56
  37.6 5.8 %collective-permute-start.1 = (bf16[128,640]{1,0:T(8,128)(2,1)S(1)}, bf16[128,640]{1,0:T(8,128)(2,1)S(1)}, u32[]{:S(2)}, u32[]{:S(2)}) collective-permute-start(bf16[128,640]{1,0:T(8,128)(2,1)S(1)} %slice.9), channel_id=1, source_target_pairs={{0,1},{1,2},{2,3},{3,0},{4,5},{5,6},{6,7},{7,4},{8,24},{9,25},{10,... | collective-permute-start | bytes 491528 | tf_op jit(solution)/shard_map/ppermute | solution.py:52
  37.7 5.7 %collective-permute-start.3 = (bf16[128,640]{1,0:T(8,128)(2,1)S(1)}, bf16[128,640]{1,0:T(8,128)(2,1)S(1)}, u32[]{:S(2)}, u32[]{:S(2)}) collective-permute-start(bf16[128,640]{1,0:T(8,128)(2,1)S(1)} %slice.10), channel_id=1, source_target_pairs={{0,3},{1,0},{2,1},{3,2},{4,7},{5,4},{6,5},{7,6},{8,28},{9,29},{10,... | collective-permute-start | bytes 491528 | tf_op jit(solution)/shard_map/ppermute | solution.py:52
  43.3 2.5 %collective-permute-start.7 = (bf16[128,640]{1,0:T(8,128)(2,1)S(1)}, bf16[128,640]{1,0:T(8,128)(2,1)S(1)}, u32[]{:S(2)}, u32[]{:S(2)}) collective-permute-start(bf16[128,640]{1,0:T(8,128)(2,1)S(1)} %collective-permute-done.1.refs_3_.refs_13_), channel_id=1, source_target_pairs={{0,8},{8,0},{1,9},{9,1},{2,10},{10,2},{3,11},{11,3},{4,12},{12,4},... | collective-permute-start | bytes 491528 | tf_op jit(solution)/shard_map/ppermute | solution.py:56
  44.8 1.4 %collective-permute-start.8 = (bf16[128,640]{1,0:T(8,128)(2,1)S(1)}, bf16[128,640]{1,0:T(8,128)(2,1)S(1)}, u32[]{:S(2)}, u32[]{:S(2)}) collective-permute-start(bf16[128,640]{1,0:T(8,128)(2,1)S(1)} %collective-permute-done.3.refs_4_.refs_14_), channel_id=1, source_target_pairs={{0,8},{8,0},{1,9},{9,1},{2,10},{10,2},{3,11},{11,3},{4,12},{12,4},... | collective-permute-start | bytes 491528 | tf_op jit(solution)/shard_map/ppermute | solution.py:56
  47.6 2.6 %collective-permute-start.9 = (bf16[256,640]{1,0:T(8,128)(2,1)S(1)}, bf16[256,640]{1,0:T(8,128)(2,1)S(1)}, u32[]{:S(2)}, u32[]{:S(2)}) collective-permute-start(bf16[256,640]{1,0:T(8,128)(2,1)S(1)} %get-tuple-element.78), channel_id=1, source_target_pairs={{0,8},{8,0},{1,9},{9,1},{2,10},{10,2},{3,11},{11,3},{4,12},{12,4},... | collective-permute-start | bytes 983048 | tf_op jit(solution)/shard_map/ppermute | solution.py:56
  49.3 1.7 %collective-permute-start.11 = (bf16[256,640]{1,0:T(8,128)(2,1)S(1)}, bf16[256,640]{1,0:T(8,128)(2,1)S(1)}, u32[]{:S(2)}, u32[]{:S(2)}) collective-permute-start(bf16[256,640]{1,0:T(8,128)(2,1)S(1)} %get-tuple-element.86), channel_id=1, source_target_pairs={{0,8},{8,0},{1,9},{9,1},{2,10},{10,2},{3,11},{11,3},{4,12},{12,4},... | collective-permute-start | bytes 983048 | tf_op jit(solution)/shard_map/ppermute | solution.py:56
  49.7 1.8 %collective-permute-start.12 = (bf16[256,640]{1,0:T(8,128)(2,1)S(1)}, bf16[256,640]{1,0:T(8,128)(2,1)S(1)}, u32[]{:S(2)}, u32[]{:S(2)}) collective-permute-start(bf16[256,640]{1,0:T(8,128)(2,1)S(1)} %get-tuple-element.87), channel_id=1, source_target_pairs={{0,8},{8,0},{1,9},{9,1},{2,10},{10,2},{3,11},{11,3},{4,12},{12,4},... | collective-permute-start | bytes 983048 | tf_op jit(solution)/shard_map/ppermute | solution.py:56
  49.9 5.3 %collective-permute-start.15 = (bf16[256,640]{1,0:T(8,128)(2,1)S(1)}, bf16[256,640]{1,0:T(8,128)(2,1)S(1)}, u32[]{:S(2)}, u32[]{:S(2)}) collective-permute-start(bf16[256,640]{1,0:T(8,128)(2,1)S(1)} %get-tuple-element.96), channel_id=1, source_target_pairs={{0,8},{8,0},{1,9},{9,1},{2,10},{10,2},{3,11},{11,3},{4,12},{12,4},... | collective-permute-start | bytes 983048 | tf_op jit(solution)/shard_map/ppermute | solution.py:56
  52.4 11.0 %collective-permute-start.14 = (bf16[256,640]{1,0:T(8,128)(2,1)S(1)}, bf16[256,640]{1,0:T(8,128)(2,1)S(1)}, u32[]{:S(2)}, u32[]{:S(2)}) collective-permute-start(bf16[256,640]{1,0:T(8,128)(2,1)S(1)} %get-tuple-element.92), channel_id=1, source_target_pairs={{0,1},{1,2},{2,3},{3,0},{4,5},{5,6},{6,7},{7,4},{8,24},{9,25},{10,... | collective-permute-start | bytes 983048 | tf_op jit(solution)/shard_map/ppermute | solution.py:52
  52.5 10.9 %collective-permute-start.13 = (bf16[256,640]{1,0:T(8,128)(2,1)S(1)}, bf16[256,640]{1,0:T(8,128)(2,1)S(1)}, u32[]{:S(2)}, u32[]{:S(2)}) collective-permute-start(bf16[256,640]{1,0:T(8,128)(2,1)S(1)} %get-tuple-element.89), channel_id=1, source_target_pairs={{0,3},{1,0},{2,1},{3,2},{4,7},{5,4},{6,5},{7,6},{8,28},{9,29},{10,... | collective-permute-start | bytes 983048 | tf_op jit(solution)/shard_map/ppermute | solution.py:52
  55.1 8.3 %collective-permute-start.10 = (bf16[256,640]{1,0:T(8,128)(2,1)S(1)}, bf16[256,640]{1,0:T(8,128)(2,1)S(1)}, u32[]{:S(2)}, u32[]{:S(2)}) collective-permute-start(bf16[256,640]{1,0:T(8,128)(2,1)S(1)} %get-tuple-element.80), channel_id=1, source_target_pairs={{0,2},{1,3},{2,0},{3,1},{4,6},{5,7},{6,4},{7,5},{8,12},{9,13},{10,... | collective-permute-start | bytes 983048 | tf_op jit(solution)/shard_map/ppermute | solution.py:52

commit v4 on v3

--- a/solution.py
+++ b/solution.py
@@ -19,8 +19,8 @@
 ROWS = 512
 PART = 256
 bf16, f32 = jnp.bfloat16, jnp.float32
-FORWARD = (((0, 0),), ((0, 1), (0, 3)), ((1, 0), (1, 1), (1, 3)), ((0, 2), (1, 2)))
-BACKWARD = (((1, 2),), ((1, 1), (1, 3), (1, 0)), ((0, 2),), ((0, 1), (0, 3)), ((0, 0),))
+FORWARD = (((0, 0),), ((0, 1), (0, 3)), ((0, 2), (1, 0), (1, 1), (1, 3)), ((1, 2),))
+BACKWARD = (((1, 2, 0),), ((1, 1, 0), (1, 3, 0)), ((0, 2, 1), (0, 1, 0), (0, 3, 0)), ((1, 0, 0), (0, 0, 0)))
 ORDER = tuple(w for call in FORWARD for w in call)
 
 
@@ -216,15 +216,26 @@
 
 
 def backward_call(wanted, last, saved, taken, q, g):
-    parts = [(saved[w][0], w[0] == 0) for w in wanted]
+    parts = [(saved[h, s][0], added) for h, s, added in wanted]
     shapes, args = [], [last]
-    for w in wanted:
-        shapes.append(jax.ShapeDtypeStruct((PART, SENT), f32 if w == (0, 0) else bf16))
+    for h, s, added in wanted:
+        shapes.append(jax.ShapeDtypeStruct((PART, SENT), bf16 if h or added else f32))
         shapes.append(jax.ShapeDtypeStruct((PART, ROWS), bf16))
-        args += list(saved[w][1:]) + ([] if w[0] else [taken[w[1]]])
-    out = call(lambda *refs: backward_kernel(parts, *refs), "backward_" + label(wanted), shapes, 0, args + [q, g],
-               LIGHT)
-    return {w: (out[2 * i], out[2 * i + 1]) for i, w in enumerate(wanted)}
+        args += list(saved[h, s][1:]) + ([taken[s]] if added else [])
+    name = "backward_" + label([w[:2] for w in wanted])
+    out = call(lambda *refs: backward_kernel(parts, *refs), name, shapes, 0, args + [q, g])
+    return {w[:2]: (out[2 * i], out[2 * i + 1]) for i, w in enumerate(wanted)}
+
+
+def add_kernel(*refs):
+    n = len(refs) // 3
+    for i in range(n):
+        refs[2 * n + i][...] = (refs[i][...] + refs[n + i][...].astype(f32)).astype(bf16)
+
+
+def add_call(kept, taken):
+    shapes = [jax.ShapeDtypeStruct((PART, SENT), bf16)] * len(kept)
+    return call(add_kernel, "add_cores", shapes, 0, [*kept, *taken])
 
 
 def query_call(pairs):
@@ -250,16 +261,14 @@
     ).reshape(PART, SENT)
     q, g, first = lax.optimization_barrier((q, g, first))
     keys = {(0, 0): [first]}
-    keys[0, 1] = [turn(first, 1)]
-    keys[0, 3] = [turn(first, 3)]
+    for shift in (1, 3, 2):
+        keys[0, shift] = [turn(first, shift)]
     q, g, qt, gt, key_pos, query_pos = prepare_call(block_order, where, q, g)
     stat = None
     saved = {}
     for wanted in FORWARD:
         for w in wanted:
             if w[0] == 0:
-                if w[1] == 2:
-                    keys[w] = [turn(keys[0, 1][0][:PART // 2], 1), turn(keys[0, 3][0][PART // 2:], 3)]
                 if stat is not None:
                     (keys[w], stat) = lax.optimization_barrier((keys[w], stat))
                 keys[1, w[1]] = [swap(k) for k in keys[w]]
@@ -269,19 +278,20 @@
     last = stat
     done = {}
     taken = {}
-    arrived = []
-    for wanted in BACKWARD:
+    for wanted in BACKWARD[:3]:
         done.update(backward_call(wanted, last, saved, taken, q, g))
-        for half, shift in wanted:
+        for half, shift, _ in wanted:
             if half:
                 taken[shift] = swap(done[1, shift][0])
-            elif shift:
-                value, last = lax.optimization_barrier((done[0, shift][0], last))
-                arrived.append(turn(value, 4 - shift))
+    near = add_call([done[0, s][0] for s in (1, 3)], [taken[s] for s in (1, 3)])
+    far, near, last = lax.optimization_barrier((done[0, 2][0], near, last))
+    done.update(backward_call(BACKWARD[3], last, saved, taken, q, g))
+    taken[0] = swap(done[1, 0][0])
+    arrived = [turn(far, 2), turn(near[0], 3), turn(near[1], 1), taken[0]]
     dq = query_call([(done[w][1], keys[w]) for w in ORDER])
     (arrived, dq) = lax.optimization_barrier((arrived, dq))
-    arrived = [done[0, 0][0]] + [a.astype(f32) for a in arrived]
-    part = (arrived[0] + arrived[1] + arrived[2] + arrived[3]).astype(bf16)
+    arrived = [a.astype(f32) for a in arrived] + [done[0, 0][0]]
+    part = (arrived[0] + arrived[1] + arrived[2] + arrived[3] + arrived[4]).astype(bf16)
     part = lax.all_to_all(
         part.reshape(32, 8, SENT), ALL, 0, 0, axis_index_groups=groups, tiled=True
     )

time: 83.2 us -> 80.2 us (0.964)
  waiting for transfers between devices: 7.99 us -> 3.49 us
  blocking collectives: 41.9 us -> 43.1 us
  starting transfers between devices: 15.8 us -> 16.8 us
    ppermute x7 -> x6, waiting for transfers between devices: 5.8 us -> 2.94 us  [turn(): return lax.ppermute(value, ALL, pairs)]
    ppermute x9 -> x8, starting transfers between devices: 7.02 us -> 9.84 us  [swap(): return lax.ppermute(value, 'c', [(0, 1), (1, 0)])]
    ppermute x7 -> x6, starting transfers between devices: 8.81 us -> 6.92 us  [turn(): return lax.ppermute(value, ALL, pairs)]
    ppermute x9 -> x8, waiting for transfers between devices: 2.19 us -> 0.55 us  [swap(): return lax.ppermute(value, 'c', [(0, 1), (1, 0)])]
    all_to_all x1, blocking collectives: 18.2 us -> 19.4 us  [shards(): lax.all_to_all(part.reshape(32, 8, SENT), ALL, 0, 0, axis_index_groups=gr...]
  transfers between devices with their start and end apart: 16 -> 14, of which waited for: 6 -> 4; matrix products, arithmetic and copies ran while one was open for 0% -> 0% of each run, Pallas kernels for 12% -> 13%
where the time goes in v4:
time: 80.2 us; the launch traced here: 79.9 us
  blocking collectives  43.1 us (54%)
  starting transfers between devices  16.8 us (21%)
  Pallas kernels  11.2 us (14%)
  local copies, waits for them, and re-layouts  3.7 us (5%)
  waiting for transfers between devices  3.49 us (4%)
  other arithmetic  0.93 us (1%)
    all_to_all x1, blocking collectives, shards(): lax.all_to_all(jnp.broadcast_to(piece[None], (32, 8, SENT)), ALL, 0, 0, a...  23.7 us
    all_to_all x1, blocking collectives, shards(): lax.all_to_all(part.reshape(32, 8, SENT), ALL, 0, 0, axis_index_groups=gr...  19.4 us
    pallas_call x11, Pallas kernels, call(): pl.pallas_call(kernel, out_shape=shapes, in_specs=[SMEM] * smem + [VMEM]...  11.2 us
    ppermute x8, starting transfers between devices, swap(): return lax.ppermute(value, 'c', [(0, 1), (1, 0)])  9.84 us
    ppermute x6, starting transfers between devices, turn(): return lax.ppermute(value, ALL, pairs)  6.92 us
    unnamed x8, local copies, waits for them, and re-layouts  3.66 us
    ppermute x6, waiting for transfers between devices, turn(): return lax.ppermute(value, ALL, pairs)  2.94 us
  transfers between devices with their start and end apart: 14, of which 4 were waited for; matrix products, arithmetic and copies ran while one was open for 0% of the time, Pallas kernels for 13%

profile of v4, /device:TPU:1, one launch (start us, length us, event | category | flops | bytes accessed | tf_op | source)
XLA Modules:
  0.0 79.9 jit_solution(223647207392264999)
XLA Ops:
  0.6 0.0 copy-start
  0.7 0.9 %copy-done = bf16[64,576]{1,0:T(8,128)(2,1)S(1)} copy-done((bf16[64,576]{1,0:T(8,128)(2,1)S(1)}, bf16[64,576]{1,0:T(8,128)(2,1)}, u32[]{:S(2)}) %copy-start) | copy-done | bytes 73752
  1.6 23.7 %all_to_all.10 = bf16[32,8,640]{2,1,0:T(8,128)(2,1)S(1)} all-to-all(bf16[32,8,640]{2,1,0:T(8,128)(2,1)S(1)} %broadcast_in_dim.2), channel_id=1, replica_groups={{0,4,16,20,32,36,48,52,64,68,80,84,96,100,112,116,128,132,144,148,160,1..., dimensions={0} | all-to-all | bytes 655360 | tf_op jit(solution)/shard_map/all_to_all | solution.py:259
  25.3 1.5 %collective-permute-start.2 = (bf16[256,640]{1,0:T(8,128)(2,1)S(1)}, bf16[256,640]{1,0:T(8,128)(2,1)S(1)}, u32[]{:S(2)}, u32[]{:S(2)}) collective-permute-start(bf16[256,640]{1,0:T(8,128)(2,1)S(1)} %bitcast.11), channel_id=1, source_target_pairs={{0,1},{1,2},{2,3},{3,0},{4,5},{5,6},{6,7},{7,4},{8,24},{9,25},{10,... | collective-permute-start | bytes 983048 | tf_op jit(solution)/shard_map/ppermute | solution.py:52
  26.8 1.7 %collective-permute-start.1 = (bf16[256,640]{1,0:T(8,128)(2,1)S(1)}, bf16[256,640]{1,0:T(8,128)(2,1)S(1)}, u32[]{:S(2)}, u32[]{:S(2)}) collective-permute-start(bf16[256,640]{1,0:T(8,128)(2,1)S(1)} %bitcast.12), channel_id=1, source_target_pairs={{0,3},{1,0},{2,1},{3,2},{4,7},{5,4},{6,5},{7,6},{8,28},{9,29},{10,... | collective-permute-start | bytes 983048 | tf_op jit(solution)/shard_map/ppermute | solution.py:52
  28.6 1.6 %collective-permute-start = (bf16[256,640]{1,0:T(8,128)(2,1)S(1)}, bf16[256,640]{1,0:T(8,128)(2,1)S(1)}, u32[]{:S(2)}, u32[]{:S(2)}) collective-permute-start(bf16[256,640]{1,0:T(8,128)(2,1)S(1)} %bitcast.13), channel_id=1, source_target_pairs={{0,2},{1,3},{2,0},{3,1},{4,6},{5,7},{6,4},{7,5},{8,12},{9,13},{10,... | collective-permute-start | bytes 983048 | tf_op jit(solution)/shard_map/ppermute | solution.py:52
  30.2 0.1 pad_add_fusion.where_ref
  30.2 3.7 %collective-permute-start.3 = (bf16[256,640]{1,0:T(8,128)(2,1)S(1)}, bf16[256,640]{1,0:T(8,128)(2,1)S(1)}, u32[]{:S(2)}, u32[]{:S(2)}) collective-permute-start(bf16[256,640]{1,0:T(8,128)(2,1)S(1)} %bitcast.14), channel_id=1, source_target_pairs={{0,8},{8,0},{1,9},{9,1},{2,10},{10,2},{3,11},{11,3},{4,12},{12,4},... | collective-permute-start | bytes 983048 | tf_op jit(solution)/shard_map/ppermute | solution.py:56
  33.9 1.1 %copy-done.1 = bf16[64,8,576]{2,1,0:T(8,128)(2,1)S(1)} copy-done((bf16[64,8,576]{2,1,0:T(8,128)(2,1)S(1)}, bf16[64,8,576]{2,1,0:T(8,128)(2,1)}, u32[]{:S(2)}) %copy-start.1) | copy-done | bytes 589848
  35.0 1.0 %copy-done.2 = bf16[64,8,512]{2,1,0:T(8,128)(2,1)S(1)} copy-done((bf16[64,8,512]{2,1,0:T(8,128)(2,1)S(1)}, bf16[64,8,512]{2,1,0:T(8,128)(2,1)}, u32[]{:S(2)}) %copy-start.2) | copy-done | bytes 524312
  36.0 0.7 copy-done.3
  36.7 1.3 %prepare.1 = (bf16[512,576]{1,0:T(8,128)(2,1)S(1)}, bf16[512,512]{1,0:T(8,128)(2,1)S(1)}, bf16[576,512]{1,0:T(8,128)(2,1)S(1)}, bf16[512,512]{1,0:T(8,128)(2,1)S...) custom-call(s32[64]{0:T(128)S(1)} %copy-done.3, s32[4]{0:T(128)S(1)} %pad_add_fusion.where_ref, ...), custom_call_target="tpu_custom_call" | custom-call | flops 1024 | bytes 1024 | tf_op jit(solution)/shard_map/prepare/pallas_call | solution.py:181
  38.0 0.5 forward_00.1
  38.5 0.0 collective-permute-done.2.refs_3_
  38.6 0.0 collective-permute-done.1.refs_4_.refs_5_
  38.6 1.7 %collective-permute-start.5 = (bf16[256,640]{1,0:T(8,128)(2,1)S(1)}, bf16[256,640]{1,0:T(8,128)(2,1)S(1)}, u32[]{:S(2)}, u32[]{:S(2)}) collective-permute-start(bf16[256,640]{1,0:T(8,128)(2,1)S(1)} %collective-permute-done.1.refs_4_.refs_5_), channel_id=1, source_target_pairs={{0,8},{8,0},{1,9},{9,1},{2,10},{10,2},{3,11},{11,3},{4,12},{12,4},... | collective-permute-start | bytes 983048 | tf_op jit(solution)/shard_map/ppermute | solution.py:56
  40.3 0.0 collective-permute-start.4
  40.3 0.9 %forward_01_03.1 = (f32[8,512]{1,0:T(8,128)S(1)}, f32[512,512]{1,0:T(8,128)S(1)}, f32[512,512]{1,0:T(8,128)S(1)}) custom-call(s32[8,512]{1,0:T(8,128)S(1)} %get-tuple-element.58.refs_0_, s32[2048,128]{1,0:T(8,128)S(1)} %get-tuple-element.59.refs_1_, f32[8,512]{1,0:T(8,128)S(1)} %get-tuple-element.65.refs_2_.refs_4_, ...), custom_call_target="tpu_custom_call" | custom-call | flops 1024 | bytes 1024 | tf_op jit(solution)/shard_map/forward_01_03/pallas_call | solution.py:181
  41.2 0.0 collective-permute-done.refs_3_.refs_7_
  41.2 0.6 collective-permute-start.6
  41.8 0.0 collective-permute-done.3.refs_4_.refs_9_
  41.8 0.0 collective-permute-done.5.refs_6_.refs_13_
  41.8 0.2 collective-permute-done.4.refs_5_.refs_11_
  42.0 1.7 %forward_02_10_11_13.1 = (f32[8,512]{1,0:T(8,128)S(1)}, f32[1024,512]{1,0:T(8,128)S(1)}, f32[1024,512]{1,0:T(8,128)S(1)}) custom-call(s32[8,512]{1,0:T(8,128)S(1)} %get-tuple-element.58.refs_0_, s32[2048,128]{1,0:T(8,128)S(1)} %get-tuple-element.59.refs_1_, f32[8,512]{1,0:T(8,128)S(1)} %get-tuple-element.69.refs_2_.refs_5_.refs_8_, ...), custom_call_target="tpu_custom_call" | custom-call | flops 1024 | bytes 1024 | tf_op jit(solution)/shard_map/forward_02_10_11_13/pallas_call | solution.py:181
  43.7 0.0 collective-permute-done.6.refs_3_.refs_15_
  43.7 0.5 forward_12.1
  44.3 0.5 backward_12.1
  44.8 0.5 collective-permute-start.7
  45.2 0.9 %backward_11_13.1 = (bf16[256,640]{1,0:T(8,128)(2,1)S(1)}, bf16[256,512]{1,0:T(8,128)(2,1)S(1)}, bf16[256,640]{1,0:T(8,128)(2,1)S(1)}, bf16[256,512]{1,0:T(8,128)(2,1)S(1)}) custom-call(f32[8,512]{1,0:T(8,128)S(1)} %get-tuple-element.92.refs_0_.refs_1_, f32[8,512]{1,0:T(8,128)S(1)} %get-tuple-element.71.refs_2_.refs_1_.refs_4_, ...), custom_call_target="tpu_custom_call" | custom-call | flops 1024 | bytes 1024 | tf_op jit(solution)/shard_map/backward_11_13/pallas_call | solution.py:181
  46.1 0.2 collective-permute-start.8
  46.3 0.4 collective-permute-start.9
  46.7 0.0 collective-permute-done.7.refs_4_
  46.7 1.2 %backward_02_01_03.1 = (bf16[256,640]{1,0:T(8,128)(2,1)S(1)}, bf16[256,512]{1,0:T(8,128)(2,1)S(1)}, f32[256,640]{1,0:T(8,128)S(1)}, bf16[256,512]{1,0:T(8,128)(2...) custom-call(f32[8,512]{1,0:T(8,128)S(1)} %get-tuple-element.92.refs_0_.refs_1_, ...), custom_call_target="tpu_custom_call" | custom-call | flops 1024 | bytes 1024 | tf_op jit(solution)/shard_map/backward_02_01_03/pallas_call | solution.py:181
  47.9 0.0 collective-permute-done.8.refs_2_
  48.0 0.3 collective-permute-done.9.refs_3_
  48.3 0.1 add_cores.1
  48.4 0.6 collective-permute-start.10
  49.0 0.9 %collective-permute-start.11 = (bf16[256,640]{1,0:T(8,128)(2,1)S(1)}, bf16[256,640]{1,0:T(8,128)(2,1)S(1)}, u32[]{:S(2)}, u32[]{:S(2)}) collective-permute-start(bf16[256,640]{1,0:T(8,128)(2,1)S(1)} %get-tuple-element.90), channel_id=1, source_target_pairs={{0,3},{1,0},{2,1},{3,2},{4,7},{5,4},{6,5},{7,6},{8,28},{9,29},{10,... | collective-permute-start | bytes 983048 | tf_op jit(solution)/shard_map/ppermute | solution.py:52
  49.9 0.6 collective-permute-start.12
  50.5 0.9 %backward_10_00.1 = (bf16[256,640]{1,0:T(8,128)(2,1)S(1)}, bf16[256,512]{1,0:T(8,128)(2,1)S(1)}, f32[256,640]{1,0:T(8,128)S(1)}, bf16[256,512]{1,0:T(8,128)(2,1)S(1)}) custom-call(f32[8,512]{1,0:T(8,128)S(1)} %get-tuple-element.92.refs_0_.refs_1_, f32[8,512]{1,0:T(8,128)S(1)} %get-tuple-element.71.refs_2_.refs_1_.refs_4_, ...), custom_call_target="tpu_custom_call" | custom-call | flops 1024 | bytes 1024 | tf_op jit(solution)/shard_map/backward_10_00/pallas_call | solution.py:181
  51.3 2.8 %collective-permute-start.13 = (bf16[256,640]{1,0:T(8,128)(2,1)S(1)}, bf16[256,640]{1,0:T(8,128)(2,1)S(1)}, u32[]{:S(2)}, u32[]{:S(2)}) collective-permute-start(bf16[256,640]{1,0:T(8,128)(2,1)S(1)} %get-tuple-element.95), channel_id=1, source_target_pairs={{0,8},{8,0},{1,9},{9,1},{2,10},{10,2},{3,11},{11,3},{4,12},{12,4},... | collective-permute-start | bytes 983048 | tf_op jit(solution)/shard_map/ppermute | solution.py:56
  54.1 2.7 %query_grad.1 = bf16[512,576]{1,0:T(8,128)(2,1)} custom-call(bf16[256,512]{1,0:T(8,128)(2,1)S(1)} %get-tuple-element.96.refs_0_, bf16[256,640]{1,0:T(8,128)(2,1)S(1)} %bitcast.16, bf16[256,512]{1,0:T(8,128)(2,1)S(1)} %get-tuple-element.97.refs_2_, bf16[256,640]{1,0:T(8,128)(2,1)S(1)} %collective-permute-done.2.refs_3_, ...), custom_call_target="tpu_custom_call" | custom-call | flops 1024 | bytes 1024 | tf_op jit(solution)/shard_map/query_grad/pallas_call | solution.py:181
  56.8 0.0 collective-permute-done.10
  56.8 0.9 %collective-permute-done.11 = bf16[256,640]{1,0:T(8,128)(2,1)S(1)} collective-permute-done((bf16[256,640]{1,0:T(8,128)(2,1)S(1)}, bf16[256,640]{1,0:T(8,128)(2,1)S(1)}, u32[]{:S(2)}, u32[]{:S(2)}) %collective-permute-start.11) | collective-permute-done | bytes 327712 | tf_op jit(solution)/shard_map/ppermute | solution.py:52
  57.7 2.0 %collective-permute-done.12 = bf16[256,640]{1,0:T(8,128)(2,1)S(1)} collective-permute-done((bf16[256,640]{1,0:T(8,128)(2,1)S(1)}, bf16[256,640]{1,0:T(8,128)(2,1)S(1)}, u32[]{:S(2)}, u32[]{:S(2)}) %collective-permute-start.12) | collective-permute-done | bytes 327712 | tf_op jit(solution)/shard_map/ppermute | solution.py:52
  59.7 0.2 fusion
  59.9 19.4 %all_to_all.11 = bf16[32,8,640]{2,1,0:T(8,128)(2,1)S(1)} all-to-all(bf16[32,8,640]{2,1,0:T(8,128)(2,1)S(1)} %fusion), channel_id=1, replica_groups={{0,4,16,20,32,36,48,52,64,68,80,84,96,100,112,116,128,132,144,148,160,1..., dimensions={0} | all-to-all | bytes 655360 | tf_op jit(solution)/shard_map/all_to_all | solution.py:295
  79.3 0.7 convert_reduce_fusion
  (7 shorter events, 0.0 us)
Async XLA Ops:
  0.6 0.9 %copy-start = (bf16[64,576]{1,0:T(8,128)(2,1)S(1)}, bf16[64,576]{1,0:T(8,128)(2,1)}, u32[]{:S(2)}) copy-start(bf16[64,576]{1,0:T(8,128)(2,1)} %param.5) | copy-start | bytes 221188
  25.3 13.3 %collective-permute-start.2 = (bf16[256,640]{1,0:T(8,128)(2,1)S(1)}, bf16[256,640]{1,0:T(8,128)(2,1)S(1)}, u32[]{:S(2)}, u32[]{:S(2)}) collective-permute-start(bf16[256,640]{1,0:T(8,128)(2,1)S(1)} %bitcast.11), channel_id=1, source_target_pairs={{0,1},{1,2},{2,3},{3,0},{4,5},{5,6},{6,7},{7,4},{8,24},{9,25},{10,... | collective-permute-start | bytes 983048 | tf_op jit(solution)/shard_map/ppermute | solution.py:52
  26.8 11.7 %collective-permute-start.1 = (bf16[256,640]{1,0:T(8,128)(2,1)S(1)}, bf16[256,640]{1,0:T(8,128)(2,1)S(1)}, u32[]{:S(2)}, u32[]{:S(2)}) collective-permute-start(bf16[256,640]{1,0:T(8,128)(2,1)S(1)} %bitcast.12), channel_id=1, source_target_pairs={{0,3},{1,0},{2,1},{3,2},{4,7},{5,4},{6,5},{7,6},{8,28},{9,29},{10,... | collective-permute-start | bytes 983048 | tf_op jit(solution)/shard_map/ppermute | solution.py:52
  28.6 12.7 %collective-permute-start = (bf16[256,640]{1,0:T(8,128)(2,1)S(1)}, bf16[256,640]{1,0:T(8,128)(2,1)S(1)}, u32[]{:S(2)}, u32[]{:S(2)}) collective-permute-start(bf16[256,640]{1,0:T(8,128)(2,1)S(1)} %bitcast.13), channel_id=1, source_target_pairs={{0,2},{1,3},{2,0},{3,1},{4,6},{5,7},{6,4},{7,5},{8,12},{9,13},{10,... | collective-permute-start | bytes 983048 | tf_op jit(solution)/shard_map/ppermute | solution.py:52
  30.2 11.6 %collective-permute-start.3 = (bf16[256,640]{1,0:T(8,128)(2,1)S(1)}, bf16[256,640]{1,0:T(8,128)(2,1)S(1)}, u32[]{:S(2)}, u32[]{:S(2)}) collective-permute-start(bf16[256,640]{1,0:T(8,128)(2,1)S(1)} %bitcast.14), channel_id=1, source_target_pairs={{0,8},{8,0},{1,9},{9,1},{2,10},{10,2},{3,11},{11,3},{4,12},{12,4},... | collective-permute-start | bytes 983048 | tf_op jit(solution)/shard_map/ppermute | solution.py:56
  33.9 1.1 %copy-start.1 = (bf16[64,8,576]{2,1,0:T(8,128)(2,1)S(1)}, bf16[64,8,576]{2,1,0:T(8,128)(2,1)}, u32[]{:S(2)}) copy-start(bf16[64,8,576]{2,1,0:T(8,128)(2,1)} %param.4) | copy-start | bytes 1769476
  35.0 1.0 %copy-start.2 = (bf16[64,8,512]{2,1,0:T(8,128)(2,1)S(1)}, bf16[64,8,512]{2,1,0:T(8,128)(2,1)}, u32[]{:S(2)}) copy-start(bf16[64,8,512]{2,1,0:T(8,128)(2,1)} %param.6) | copy-start | bytes 1572868
  36.0 0.7 copy-start.3
  38.6 3.3 %collective-permute-start.5 = (bf16[256,640]{1,0:T(8,128)(2,1)S(1)}, bf16[256,640]{1,0:T(8,128)(2,1)S(1)}, u32[]{:S(2)}, u32[]{:S(2)}) collective-permute-start(bf16[256,640]{1,0:T(8,128)(2,1)S(1)} %collective-permute-done.1.refs_4_.refs_5_), channel_id=1, source_target_pairs={{0,8},{8,0},{1,9},{9,1},{2,10},{10,2},{3,11},{11,3},{4,12},{12,4},... | collective-permute-start | bytes 983048 | tf_op jit(solution)/shard_map/ppermute | solution.py:56
  40.3 1.7 %collective-permute-start.4 = (bf16[256,640]{1,0:T(8,128)(2,1)S(1)}, bf16[256,640]{1,0:T(8,128)(2,1)S(1)}, u32[]{:S(2)}, u32[]{:S(2)}) collective-permute-start(bf16[256,640]{1,0:T(8,128)(2,1)S(1)} %collective-permute-done.2.refs_3_), channel_id=1, source_target_pairs={{0,8},{8,0},{1,9},{9,1},{2,10},{10,2},{3,11},{11,3},{4,12},{12,4},... | collective-permute-start | bytes 983048 | tf_op jit(solution)/shard_map/ppermute | solution.py:56
  41.2 2.5 %collective-permute-start.6 = (bf16[256,640]{1,0:T(8,128)(2,1)S(1)}, bf16[256,640]{1,0:T(8,128)(2,1)S(1)}, u32[]{:S(2)}, u32[]{:S(2)}) collective-permute-start(bf16[256,640]{1,0:T(8,128)(2,1)S(1)} %collective-permute-done.refs_3_.refs_7_), channel_id=1, source_target_pairs={{0,8},{8,0},{1,9},{9,1},{2,10},{10,2},{3,11},{11,3},{4,12},{12,4},... | collective-permute-start | bytes 983048 | tf_op jit(solution)/shard_map/ppermute | solution.py:56
  44.8 1.9 %collective-permute-start.7 = (bf16[256,640]{1,0:T(8,128)(2,1)S(1)}, bf16[256,640]{1,0:T(8,128)(2,1)S(1)}, u32[]{:S(2)}, u32[]{:S(2)}) collective-permute-start(bf16[256,640]{1,0:T(8,128)(2,1)S(1)} %get-tuple-element.79), channel_id=1, source_target_pairs={{0,8},{8,0},{1,9},{9,1},{2,10},{10,2},{3,11},{11,3},{4,12},{12,4},... | collective-permute-start | bytes 983048 | tf_op jit(solution)/shard_map/ppermute | solution.py:56
  46.1 1.8 %collective-permute-start.8 = (bf16[256,640]{1,0:T(8,128)(2,1)S(1)}, bf16[256,640]{1,0:T(8,128)(2,1)S(1)}, u32[]{:S(2)}, u32[]{:S(2)}) collective-permute-start(bf16[256,640]{1,0:T(8,128)(2,1)S(1)} %get-tuple-element.85), channel_id=1, source_target_pairs={{0,8},{8,0},{1,9},{9,1},{2,10},{10,2},{3,11},{11,3},{4,12},{12,4},... | collective-permute-start | bytes 983048 | tf_op jit(solution)/shard_map/ppermute | solution.py:56
  46.3 2.0 %collective-permute-start.9 = (bf16[256,640]{1,0:T(8,128)(2,1)S(1)}, bf16[256,640]{1,0:T(8,128)(2,1)S(1)}, u32[]{:S(2)}, u32[]{:S(2)}) collective-permute-start(bf16[256,640]{1,0:T(8,128)(2,1)S(1)} %get-tuple-element.86), channel_id=1, source_target_pairs={{0,8},{8,0},{1,9},{9,1},{2,10},{10,2},{3,11},{11,3},{4,12},{12,4},... | collective-permute-start | bytes 983048 | tf_op jit(solution)/shard_map/ppermute | solution.py:56
  48.4 8.4 %collective-permute-start.10 = (bf16[256,640]{1,0:T(8,128)(2,1)S(1)}, bf16[256,640]{1,0:T(8,128)(2,1)S(1)}, u32[]{:S(2)}, u32[]{:S(2)}) collective-permute-start(bf16[256,640]{1,0:T(8,128)(2,1)S(1)} %get-tuple-element.89), channel_id=1, source_target_pairs={{0,2},{1,3},{2,0},{3,1},{4,6},{5,7},{6,4},{7,5},{8,12},{9,13},{10,... | collective-permute-start | bytes 983048 | tf_op jit(solution)/shard_map/ppermute | solution.py:52
  49.0 8.7 %collective-permute-start.11 = (bf16[256,640]{1,0:T(8,128)(2,1)S(1)}, bf16[256,640]{1,0:T(8,128)(2,1)S(1)}, u32[]{:S(2)}, u32[]{:S(2)}) collective-permute-start(bf16[256,640]{1,0:T(8,128)(2,1)S(1)} %get-tuple-element.90), channel_id=1, source_target_pairs={{0,3},{1,0},{2,1},{3,2},{4,7},{5,4},{6,5},{7,6},{8,28},{9,29},{10,... | collective-permute-start | bytes 983048 | tf_op jit(solution)/shard_map/ppermute | solution.py:52
  49.9 9.9 %collective-permute-start.12 = (bf16[256,640]{1,0:T(8,128)(2,1)S(1)}, bf16[256,640]{1,0:T(8,128)(2,1)S(1)}, u32[]{:S(2)}, u32[]{:S(2)}) collective-permute-start(bf16[256,640]{1,0:T(8,128)(2,1)S(1)} %get-tuple-element.91), channel_id=1, source_target_pairs={{0,1},{1,2},{2,3},{3,0},{4,5},{5,6},{6,7},{7,4},{8,24},{9,25},{10,... | collective-permute-start | bytes 983048 | tf_op jit(solution)/shard_map/ppermute | solution.py:52
  51.3 8.4 %collective-permute-start.13 = (bf16[256,640]{1,0:T(8,128)(2,1)S(1)}, bf16[256,640]{1,0:T(8,128)(2,1)S(1)}, u32[]{:S(2)}, u32[]{:S(2)}) collective-permute-start(bf16[256,640]{1,0:T(8,128)(2,1)S(1)} %get-tuple-element.95), channel_id=1, source_target_pairs={{0,8},{8,0},{1,9},{9,1},{2,10},{10,2},{3,11},{11,3},{4,12},{12,4},... | collective-permute-start | bytes 983048 | tf_op jit(solution)/shard_map/ppermute | solution.py:56

commit v5 on v4

--- a/solution.py
+++ b/solution.py
@@ -19,7 +19,7 @@
 ROWS = 512
 PART = 256
 bf16, f32 = jnp.bfloat16, jnp.float32
-FORWARD = (((0, 0),), ((0, 1), (0, 3)), ((0, 2), (1, 0), (1, 1), (1, 3)), ((1, 2),))
+FORWARD = (((0, 0),), ((0, 1), (0, 3), (1, 0)), ((0, 2), (1, 1), (1, 3)), ((1, 2),))
 BACKWARD = (((1, 2, 0),), ((1, 1, 0), (1, 3, 0)), ((0, 2, 1), (0, 1, 0), (0, 3, 0)), ((1, 0, 0), (0, 0, 0)))
 ORDER = tuple(w for call in FORWARD for w in call)
 
@@ -32,11 +32,19 @@
     return (((z * 2 + yl) * 2 + c) * 2 + yh) * 4 + x
 
 
-def first_groups():
+def groups(key):
     found = {}
     for z, yl, c, yh, x in places():
-        found.setdefault((c, x) if c == 0 else (c, yl, yh), []).append(flat(z, yl, c, yh, x))
+        found.setdefault(key(z, yl, c, yh, x), []).append(flat(z, yl, c, yh, x))
     return list(found.values())
+
+
+def gather_groups():
+    return groups(lambda z, yl, c, yh, x: (c, yh, x) if c == 0 else (c, yl, yh, x // 2))
+
+
+def scatter_groups():
+    return groups(lambda z, yl, c, yh, x: (c, x) if c == 0 else (c, yl, yh))
 
 
 def turn(value, shift):
@@ -80,13 +88,17 @@
     return jnp.concatenate(tiles, axis=0)
 
 
-def prepare_kernel(order_ref, where_ref, q_ref, g_ref, q_out, g_out, qt_out, gt_out, key_out, query_out):
+def prepare_kernel(where_ref, order_hbm, q_hbm, g_hbm, q_out, g_out, qt_out, gt_out, key_out, query_out,
+                   order_ref, sems):
+    copies = [
+        pltpu.make_async_copy(order_hbm, order_ref, sems.at[0]),
+        pltpu.make_async_copy(q_hbm, q_out, sems.at[1]),
+        pltpu.make_async_copy(g_hbm, g_out, sems.at[2]),
+    ]
+    for copy in copies:
+        copy.start()
     ctx, core = where_ref[0], where_ref[1]
-    q, g = q_ref[...], g_ref[...]
-    q_out[...] = q
-    g_out[...] = g
-    qt_out[...] = q.T
-    gt_out[...] = g.T
+    copies[0].wait()
     for i, (half, shift) in enumerate(ORDER):
         key_core = core if half == 0 else 1 - core
         key_out[i * PART:(i + 1) * PART, :] = key_positions(order_ref, where_ref, key_core, shift)
@@ -94,6 +106,10 @@
     query_out[...] = jnp.where(
         tok < 32, order_ref[2 * ctx] * 32 + tok, order_ref[2 * ctx + 1] * 32 + tok - 32
     )
+    copies[1].wait()
+    qt_out[...] = q_out[...].T
+    copies[2].wait()
+    gt_out[...] = g_out[...].T
 
 
 def load_part(refs, width):
@@ -197,7 +213,16 @@
     shapes = [jax.ShapeDtypeStruct(s, bf16) for s in (
         (ROWS, WIDTH), (ROWS, KV_RANK), (WIDTH, ROWS), (KV_RANK, ROWS))]
     shapes += [jax.ShapeDtypeStruct((8 * PART, 128), jnp.int32), jax.ShapeDtypeStruct((8, ROWS), jnp.int32)]
-    return call(prepare_kernel, "prepare", shapes, 2, [order, where, q, g])
+    return pl.pallas_call(
+        prepare_kernel,
+        out_shape=shapes,
+        in_specs=[SMEM] + [pl.BlockSpec(memory_space=pltpu.HBM)] * 3,
+        out_specs=[VMEM] * len(shapes),
+        scratch_shapes=[pltpu.SMEM((64,), jnp.int32), pltpu.SemaphoreType.DMA((3,))],
+        compiler_params=PARAMS,
+        cost_estimate=LIGHT,
+        name="prepare",
+    )(where, order, q, g)
 
 
 def forward_call(parts, query_pos, key_pos, stat, keys, qt, gt):
@@ -253,15 +278,18 @@
         lax.axis_index(CTX), lax.axis_index("c"), lax.axis_index("x"),
         2 * lax.axis_index("yh") + lax.axis_index("yl"),
     ]).astype(jnp.int32)
-    groups = first_groups()
-    piece = lax.dynamic_slice_in_dim(latent, lax.axis_index(HEAD) * 8, 8, 0)
+    core, x, yh = lax.axis_index("c"), lax.axis_index("x"), lax.axis_index("yh")
+    low = jnp.where(core == 0, x, yh * 4 + 2 * (x % 2)) * 8
+    high = jnp.where(core == 0, x + 4, yh * 4 + 2 * (x % 2) + 1) * 8
+    piece = jnp.concatenate([lax.dynamic_slice_in_dim(latent, at, 8, 0) for at in (low, high)])
     piece = jnp.pad(piece, ((0, 0), (0, SENT - WIDTH)))
     first = lax.all_to_all(
-        jnp.broadcast_to(piece[None], (32, 8, SENT)), ALL, 0, 0, axis_index_groups=groups, tiled=True
+        jnp.broadcast_to(piece[None], (16, 16, SENT)), ALL, 0, 0,
+        axis_index_groups=gather_groups(), tiled=True,
     ).reshape(PART, SENT)
     q, g, first = lax.optimization_barrier((q, g, first))
     keys = {(0, 0): [first]}
-    for shift in (1, 3, 2):
+    for shift in (2, 1, 3):
         keys[0, shift] = [turn(first, shift)]
     q, g, qt, gt, key_pos, query_pos = prepare_call(block_order, where, q, g)
     stat = None
@@ -293,7 +321,7 @@
     arrived = [a.astype(f32) for a in arrived] + [done[0, 0][0]]
     part = (arrived[0] + arrived[1] + arrived[2] + arrived[3] + arrived[4]).astype(bf16)
     part = lax.all_to_all(
-        part.reshape(32, 8, SENT), ALL, 0, 0, axis_index_groups=groups, tiled=True
+        part.reshape(32, 8, SENT), ALL, 0, 0, axis_index_groups=scatter_groups(), tiled=True
     )
     grad_latent = jnp.sum(part.astype(f32), axis=0)[:, :WIDTH]
     return dq.reshape(tok_rows, head_count, width), grad_latent

time: 80.2 us -> 76.2 us (0.950); the launches traced: 79.9 us -> 74.9 us
  blocking collectives: 43.1 us -> 40.3 us
  starting transfers between devices: 16.8 us -> 14.7 us
  local copies, waits for them, and re-layouts: 3.7 us -> 2.51 us
    ppermute x8, starting transfers between devices: 9.84 us -> 5.28 us  [swap(): return lax.ppermute(value, 'c', [(0, 1), (1, 0)])]
    all_to_all x2, blocking collectives: 43.1 us -> 40.3 us  [the longest x1 22 us: shards(): lax.all_to_all(jnp.broadcast_to(piece[None], (16, 16, SENT)), ALL, 0, 0,...]
    ppermute x6, starting transfers between devices: 6.92 us -> 9.44 us  [turn(): return lax.ppermute(value, ALL, pairs)]
    pallas_call x0 -> x1, Pallas kernels: none -> 2 us  [prepare_call(): pl.pallas_call(prepare_kernel, out_shape=shapes, in_specs=[SMEM] + [pl.Bl...]
    unnamed x8 -> x6, local copies, waits for them, and re-layouts: 3.66 us -> 1.7 us
    pallas_call x11 -> x10, Pallas kernels: 11.2 us -> 9.93 us  [call(): pl.pallas_call(kernel, out_shape=shapes, in_specs=[SMEM] * smem + [VMEM]...]
  transfers between devices with their start and end apart: 14 -> 14, of which waited for: 4 -> 3; matrix products, arithmetic and copies ran while one was open for 0% -> 0% of each run, Pallas kernels for 13% -> 14%
where the time goes in v5:
time: 76.2 us; the launch traced here: 74.9 us
  blocking collectives  40.3 us (53%)
  starting transfers between devices  14.7 us (19%)
  Pallas kernels  11.9 us (16%)
  waiting for transfers between devices  3.71 us (5%)
  local copies, waits for them, and re-layouts  2.51 us (3%)
  other arithmetic  0.94 us (1%)
  between operations  0.81 us (1%)
    all_to_all x1, blocking collectives, shards(): lax.all_to_all(jnp.broadcast_to(piece[None], (16, 16, SENT)), ALL, 0, 0,...  22 us
    all_to_all x1, blocking collectives, shards(): lax.all_to_all(part.reshape(32, 8, SENT), ALL, 0, 0, axis_index_groups=sc...  18.3 us
    pallas_call x10, Pallas kernels, call(): pl.pallas_call(kernel, out_shape=shapes, in_specs=[SMEM] * smem + [VMEM]...  9.93 us
    ppermute x6, starting transfers between devices, turn(): return lax.ppermute(value, ALL, pairs)  9.44 us
    ppermute x8, starting transfers between devices, swap(): return lax.ppermute(value, 'c', [(0, 1), (1, 0)])  5.28 us
    ppermute x6, waiting for transfers between devices, turn(): return lax.ppermute(value, ALL, pairs)  3.35 us
    pallas_call x1, Pallas kernels, prepare_call(): pl.pallas_call(prepare_kernel, out_shape=shapes, in_specs=[SMEM] + [pl.Bl...  2 us
    unnamed x6, local copies, waits for them, and re-layouts  1.7 us
  transfers between devices with their start and end apart: 14, of which 3 were waited for; matrix products, arithmetic and copies ran while one was open for 0% of the time, Pallas kernels for 14%

profile of v5, /device:TPU:1, one launch (start us, length us, event | category | flops | bytes accessed | tf_op | source)
XLA Modules:
  0.0 74.9 jit_solution(3424047689266327064)
XLA Ops:
  0.6 0.0 copy-start
  0.7 0.8 %constant_dynamic-slice_fusion.1 = (bf16[8,576]{1,0:T(8,128)(2,1)S(1)}, bf16[8,576]{1,0:T(8,128)(2,1)S(1)}) fusion(bf16[64,576]{1,0:T(8,128)(2,1)} %param.5, s32[]{:T(128)S(6)} %select_n.23, s32[]{:T(128)S(6)} %select_n.25), kind=kLoop, calls=%fused_computation.9 | loop fusion | bytes 36872 | tf_op jit(solution)/shard_map/dynamic_slice | solution.py:284
  1.5 22.0 %all_to_all.10 = bf16[16,16,640]{2,1,0:T(8,128)(2,1)S(1)} all-to-all(bf16[16,16,640]{2,1,0:T(8,128)(2,1)S(1)} %broadcast_in_dim.2), channel_id=1, replica_groups={{0,16,32,48,64,80,96,112,128,144,160,176,192,208,224,240},{1,17,33,49,6..., dimensions={0} | all-to-all | bytes 655360 | tf_op jit(solution)/shard_map/all_to_all | solution.py:286
  23.5 1.1 %collective-permute-start.2 = (bf16[256,640]{1,0:T(8,128)(2,1)S(1)}, bf16[256,640]{1,0:T(8,128)(2,1)S(1)}, u32[]{:S(2)}, u32[]{:S(2)}) collective-permute-start(bf16[256,640]{1,0:T(8,128)(2,1)S(1)} %bitcast.11), channel_id=1, source_target_pairs={{0,1},{1,2},{2,3},{3,0},{4,5},{5,6},{6,7},{7,4},{8,24},{9,25},{10,... | collective-permute-start | bytes 983048 | tf_op jit(solution)/shard_map/ppermute | solution.py:60
  24.6 1.6 %collective-permute-start.1 = (bf16[256,640]{1,0:T(8,128)(2,1)S(1)}, bf16[256,640]{1,0:T(8,128)(2,1)S(1)}, u32[]{:S(2)}, u32[]{:S(2)}) collective-permute-start(bf16[256,640]{1,0:T(8,128)(2,1)S(1)} %bitcast.12), channel_id=1, source_target_pairs={{0,3},{1,0},{2,1},{3,2},{4,7},{5,4},{6,5},{7,6},{8,28},{9,29},{10,... | collective-permute-start | bytes 983048 | tf_op jit(solution)/shard_map/ppermute | solution.py:60
  26.2 2.4 %collective-permute-start.3 = (bf16[256,640]{1,0:T(8,128)(2,1)S(1)}, bf16[256,640]{1,0:T(8,128)(2,1)S(1)}, u32[]{:S(2)}, u32[]{:S(2)}) collective-permute-start(bf16[256,640]{1,0:T(8,128)(2,1)S(1)} %bitcast.13), channel_id=1, source_target_pairs={{0,8},{8,0},{1,9},{9,1},{2,10},{10,2},{3,11},{11,3},{4,12},{12,4},... | collective-permute-start | bytes 983048 | tf_op jit(solution)/shard_map/ppermute | solution.py:64
  28.6 2.6 %collective-permute-start = (bf16[256,640]{1,0:T(8,128)(2,1)S(1)}, bf16[256,640]{1,0:T(8,128)(2,1)S(1)}, u32[]{:S(2)}, u32[]{:S(2)}) collective-permute-start(bf16[256,640]{1,0:T(8,128)(2,1)S(1)} %bitcast.14), channel_id=1, source_target_pairs={{0,2},{1,3},{2,0},{3,1},{4,6},{5,7},{6,4},{7,5},{8,12},{9,13},{10,... | collective-permute-start | bytes 983048 | tf_op jit(solution)/shard_map/ppermute | solution.py:60
  31.2 0.1 pad_add_fusion.where_ref
  31.3 1.0 %copy-done.1 = bf16[64,8,512]{2,1,0:T(8,128)(2,1)S(1)} copy-done((bf16[64,8,512]{2,1,0:T(8,128)(2,1)S(1)}, bf16[64,8,512]{2,1,0:T(8,128)(2,1)}, u32[]{:S(2)}) %copy-start.1) | copy-done | bytes 524312
  32.3 0.7 copy-done.2
  33.0 2.0 %prepare.1 = (bf16[512,576]{1,0:T(8,128)(2,1)S(1)}, bf16[512,512]{1,0:T(8,128)(2,1)S(1)}, bf16[576,512]{1,0:T(8,128)(2,1)S(1)}, bf16[512,512]{1,0:T(8,128)(2,1)S...) custom-call(s32[4]{0:T(128)S(1)} %pad_add_fusion.where_ref, s32[64]{0:T(128)S(1)} %copy-done.2, ...), custom_call_target="tpu_custom_call" | custom-call | flops 1024 | bytes 1024 | tf_op jit(solution)/shard_map/prepare/pallas_call | solution.py:216
  35.0 0.5 forward_00.1
  35.5 0.0 collective-permute-done.2.refs_3_
  35.5 0.0 collective-permute-done.1.refs_4_.refs_5_
  35.6 0.1 collective-permute-start.4
  35.7 0.5 collective-permute-start.5
  36.2 0.0 collective-permute-done.3.refs_5_.refs_7_
  36.2 1.3 %forward_01_03_10.1 = (f32[8,512]{1,0:T(8,128)S(1)}, f32[768,512]{1,0:T(8,128)S(1)}, f32[768,512]{1,0:T(8,128)S(1)}) custom-call(s32[8,512]{1,0:T(8,128)S(1)} %get-tuple-element.58.refs_0_, s32[2048,128]{1,0:T(8,128)S(1)} %get-tuple-element.59.refs_1_, f32[8,512]{1,0:T(8,128)S(1)} %get-tuple-element.65.refs_2_.refs_4_, ...), custom_call_target="tpu_custom_call" | custom-call | flops 1024 | bytes 1024 | tf_op jit(solution)/shard_map/forward_01_03_10/pallas_call | solution.py:197
  37.5 0.0 collective-permute-done.refs_3_.refs_9_
  37.5 1.0 %collective-permute-start.6 = (bf16[256,640]{1,0:T(8,128)(2,1)S(1)}, bf16[256,640]{1,0:T(8,128)(2,1)S(1)}, u32[]{:S(2)}, u32[]{:S(2)}) collective-permute-start(bf16[256,640]{1,0:T(8,128)(2,1)S(1)} %collective-permute-done.refs_3_.refs_9_), channel_id=1, source_target_pairs={{0,8},{8,0},{1,9},{9,1},{2,10},{10,2},{3,11},{11,3},{4,12},{12,4},... | collective-permute-start | bytes 983048 | tf_op jit(solution)/shard_map/ppermute | solution.py:64
  38.4 0.0 collective-permute-done.4.refs_4_.refs_11_
  38.4 0.0 collective-permute-done.5.refs_5_.refs_13_
  38.4 1.3 %forward_02_11_13.1 = (f32[8,512]{1,0:T(8,128)S(1)}, f32[768,512]{1,0:T(8,128)S(1)}, f32[768,512]{1,0:T(8,128)S(1)}) custom-call(s32[8,512]{1,0:T(8,128)S(1)} %get-tuple-element.58.refs_0_, s32[2048,128]{1,0:T(8,128)S(1)} %get-tuple-element.59.refs_1_, f32[8,512]{1,0:T(8,128)S(1)} %get-tuple-element.69.refs_2_.refs_5_.refs_8_.refs_1_, ...), custom_call_target="tpu_custom_call" | custom-call | flops 1024 | bytes 1024 | tf_op jit(solution)/shard_map/forward_02_11_13/pallas_call | solution.py:197
  39.7 0.0 collective-permute-done.6.refs_3_.refs_15_
  39.7 0.5 forward_12.1
  40.3 0.5 backward_12.1
  40.8 0.4 collective-permute-start.7
  41.2 0.9 %backward_11_13.1 = (bf16[256,640]{1,0:T(8,128)(2,1)S(1)}, bf16[256,512]{1,0:T(8,128)(2,1)S(1)}, bf16[256,640]{1,0:T(8,128)(2,1)S(1)}, bf16[256,512]{1,0:T(8,128)(2,1)S(1)}) custom-call(f32[8,512]{1,0:T(8,128)S(1)} %get-tuple-element.92.refs_0_.refs_1_, f32[8,512]{1,0:T(8,128)S(1)} %get-tuple-element.71.refs_2_.refs_1_.refs_4_, ...), custom_call_target="tpu_custom_call" | custom-call | flops 1024 | bytes 1024 | tf_op jit(solution)/shard_map/backward_11_13/pallas_call | solution.py:197
  42.1 0.3 collective-permute-start.8
  42.4 0.3 collective-permute-start.9
  42.7 0.0 collective-permute-done.7.refs_4_
  42.7 1.2 %backward_02_01_03.1 = (bf16[256,640]{1,0:T(8,128)(2,1)S(1)}, bf16[256,512]{1,0:T(8,128)(2,1)S(1)}, f32[256,640]{1,0:T(8,128)S(1)}, bf16[256,512]{1,0:T(8,128)(2...) custom-call(f32[8,512]{1,0:T(8,128)S(1)} %get-tuple-element.92.refs_0_.refs_1_, ...), custom_call_target="tpu_custom_call" | custom-call | flops 1024 | bytes 1024 | tf_op jit(solution)/shard_map/backward_02_01_03/pallas_call | solution.py:197
  43.9 0.0 collective-permute-done.8.refs_2_
  43.9 0.3 collective-permute-done.9.refs_3_
  44.3 0.1 add_cores.1
  44.4 2.7 %collective-permute-start.10 = (bf16[256,640]{1,0:T(8,128)(2,1)S(1)}, bf16[256,640]{1,0:T(8,128)(2,1)S(1)}, u32[]{:S(2)}, u32[]{:S(2)}) collective-permute-start(bf16[256,640]{1,0:T(8,128)(2,1)S(1)} %get-tuple-element.89), channel_id=1, source_target_pairs={{0,2},{1,3},{2,0},{3,1},{4,6},{5,7},{6,4},{7,5},{8,12},{9,13},{10,... | collective-permute-start | bytes 983048 | tf_op jit(solution)/shard_map/ppermute | solution.py:60
  47.1 0.2 collective-permute-start.11
  47.2 1.3 %collective-permute-start.12 = (bf16[256,640]{1,0:T(8,128)(2,1)S(1)}, bf16[256,640]{1,0:T(8,128)(2,1)S(1)}, u32[]{:S(2)}, u32[]{:S(2)}) collective-permute-start(bf16[256,640]{1,0:T(8,128)(2,1)S(1)} %get-tuple-element.91), channel_id=1, source_target_pairs={{0,1},{1,2},{2,3},{3,0},{4,5},{5,6},{6,7},{7,4},{8,24},{9,25},{10,... | collective-permute-start | bytes 983048 | tf_op jit(solution)/shard_map/ppermute | solution.py:60
  48.6 0.9 %backward_10_00.1 = (bf16[256,640]{1,0:T(8,128)(2,1)S(1)}, bf16[256,512]{1,0:T(8,128)(2,1)S(1)}, f32[256,640]{1,0:T(8,128)S(1)}, bf16[256,512]{1,0:T(8,128)(2,1)S(1)}) custom-call(f32[8,512]{1,0:T(8,128)S(1)} %get-tuple-element.92.refs_0_.refs_1_, f32[8,512]{1,0:T(8,128)S(1)} %get-tuple-element.69.refs_2_.refs_5_.refs_8_.refs_1_, ...), custom_call_target="tpu_custom_call" | custom-call | flops 1024 | bytes 1024 | tf_op jit(solution)/shard_map/backward_10_00/pallas_call | solution.py:197
  49.4 0.3 collective-permute-start.13
  49.7 2.7 %query_grad.1 = bf16[512,576]{1,0:T(8,128)(2,1)} custom-call(bf16[256,512]{1,0:T(8,128)(2,1)S(1)} %get-tuple-element.96.refs_0_, bf16[256,640]{1,0:T(8,128)(2,1)S(1)} %bitcast.16, bf16[256,512]{1,0:T(8,128)(2,1)S(1)} %get-tuple-element.97.refs_2_, bf16[256,640]{1,0:T(8,128)(2,1)S(1)} %collective-permute-done.2.refs_3_, ...), custom_call_target="tpu_custom_call" | custom-call | flops 1024 | bytes 1024 | tf_op jit(solution)/shard_map/query_grad/pallas_call | solution.py:197
  52.4 0.0 collective-permute-done.10
  52.4 2.9 %collective-permute-done.11 = bf16[256,640]{1,0:T(8,128)(2,1)S(1)} collective-permute-done((bf16[256,640]{1,0:T(8,128)(2,1)S(1)}, bf16[256,640]{1,0:T(8,128)(2,1)S(1)}, u32[]{:S(2)}, u32[]{:S(2)}) %collective-permute-start.11) | collective-permute-done | bytes 327712 | tf_op jit(solution)/shard_map/ppermute | solution.py:60
  55.3 0.4 collective-permute-done.12
  55.7 0.0 collective-permute-done.13
  55.7 0.2 fusion
  55.9 18.3 %all_to_all.11 = bf16[32,8,640]{2,1,0:T(8,128)(2,1)S(1)} all-to-all(bf16[32,8,640]{2,1,0:T(8,128)(2,1)S(1)} %fusion), channel_id=1, replica_groups={{0,4,16,20,32,36,48,52,64,68,80,84,96,100,112,116,128,132,144,148,160,1..., dimensions={0} | all-to-all | bytes 655360 | tf_op jit(solution)/shard_map/all_to_all | solution.py:323
  74.2 0.7 convert_reduce_fusion
  (5 shorter events, 0.0 us)
Async XLA Ops:
  0.6 30.7 %copy-start = (bf16[64,8,576]{2,1,0:T(8,128)(2,1)S(1)}, bf16[64,8,576]{2,1,0:T(8,128)(2,1)}, u32[]{:S(2)}) copy-start(bf16[64,8,576]{2,1,0:T(8,128)(2,1)} %param.4) | copy-start | bytes 1769476
  23.5 12.1 %collective-permute-start.2 = (bf16[256,640]{1,0:T(8,128)(2,1)S(1)}, bf16[256,640]{1,0:T(8,128)(2,1)S(1)}, u32[]{:S(2)}, u32[]{:S(2)}) collective-permute-start(bf16[256,640]{1,0:T(8,128)(2,1)S(1)} %bitcast.11), channel_id=1, source_target_pairs={{0,1},{1,2},{2,3},{3,0},{4,5},{5,6},{6,7},{7,4},{8,24},{9,25},{10,... | collective-permute-start | bytes 983048 | tf_op jit(solution)/shard_map/ppermute | solution.py:60
  24.6 11.0 %collective-permute-start.1 = (bf16[256,640]{1,0:T(8,128)(2,1)S(1)}, bf16[256,640]{1,0:T(8,128)(2,1)S(1)}, u32[]{:S(2)}, u32[]{:S(2)}) collective-permute-start(bf16[256,640]{1,0:T(8,128)(2,1)S(1)} %bitcast.12), channel_id=1, source_target_pairs={{0,3},{1,0},{2,1},{3,2},{4,7},{5,4},{6,5},{7,6},{8,28},{9,29},{10,... | collective-permute-start | bytes 983048 | tf_op jit(solution)/shard_map/ppermute | solution.py:60
  26.2 10.0 %collective-permute-start.3 = (bf16[256,640]{1,0:T(8,128)(2,1)S(1)}, bf16[256,640]{1,0:T(8,128)(2,1)S(1)}, u32[]{:S(2)}, u32[]{:S(2)}) collective-permute-start(bf16[256,640]{1,0:T(8,128)(2,1)S(1)} %bitcast.13), channel_id=1, source_target_pairs={{0,8},{8,0},{1,9},{9,1},{2,10},{10,2},{3,11},{11,3},{4,12},{12,4},... | collective-permute-start | bytes 983048 | tf_op jit(solution)/shard_map/ppermute | solution.py:64
  28.6 8.9 %collective-permute-start = (bf16[256,640]{1,0:T(8,128)(2,1)S(1)}, bf16[256,640]{1,0:T(8,128)(2,1)S(1)}, u32[]{:S(2)}, u32[]{:S(2)}) collective-permute-start(bf16[256,640]{1,0:T(8,128)(2,1)S(1)} %bitcast.14), channel_id=1, source_target_pairs={{0,2},{1,3},{2,0},{3,1},{4,6},{5,7},{6,4},{7,5},{8,12},{9,13},{10,... | collective-permute-start | bytes 983048 | tf_op jit(solution)/shard_map/ppermute | solution.py:60
  31.3 1.0 %copy-start.1 = (bf16[64,8,512]{2,1,0:T(8,128)(2,1)S(1)}, bf16[64,8,512]{2,1,0:T(8,128)(2,1)}, u32[]{:S(2)}) copy-start(bf16[64,8,512]{2,1,0:T(8,128)(2,1)} %param.6) | copy-start | bytes 1572868
  32.3 0.7 copy-start.2
  35.6 2.9 %collective-permute-start.4 = (bf16[256,640]{1,0:T(8,128)(2,1)S(1)}, bf16[256,640]{1,0:T(8,128)(2,1)S(1)}, u32[]{:S(2)}, u32[]{:S(2)}) collective-permute-start(bf16[256,640]{1,0:T(8,128)(2,1)S(1)} %collective-permute-done.2.refs_3_), channel_id=1, source_target_pairs={{0,8},{8,0},{1,9},{9,1},{2,10},{10,2},{3,11},{11,3},{4,12},{12,4},... | collective-permute-start | bytes 983048 | tf_op jit(solution)/shard_map/ppermute | solution.py:64
  35.7 2.8 %collective-permute-start.5 = (bf16[256,640]{1,0:T(8,128)(2,1)S(1)}, bf16[256,640]{1,0:T(8,128)(2,1)S(1)}, u32[]{:S(2)}, u32[]{:S(2)}) collective-permute-start(bf16[256,640]{1,0:T(8,128)(2,1)S(1)} %collective-permute-done.1.refs_4_.refs_5_), channel_id=1, source_target_pairs={{0,8},{8,0},{1,9},{9,1},{2,10},{10,2},{3,11},{11,3},{4,12},{12,4},... | collective-permute-start | bytes 983048 | tf_op jit(solution)/shard_map/ppermute | solution.py:64
  37.5 2.3 %collective-permute-start.6 = (bf16[256,640]{1,0:T(8,128)(2,1)S(1)}, bf16[256,640]{1,0:T(8,128)(2,1)S(1)}, u32[]{:S(2)}, u32[]{:S(2)}) collective-permute-start(bf16[256,640]{1,0:T(8,128)(2,1)S(1)} %collective-permute-done.refs_3_.refs_9_), channel_id=1, source_target_pairs={{0,8},{8,0},{1,9},{9,1},{2,10},{10,2},{3,11},{11,3},{4,12},{12,4},... | collective-permute-start | bytes 983048 | tf_op jit(solution)/shard_map/ppermute | solution.py:64
  40.8 1.9 %collective-permute-start.7 = (bf16[256,640]{1,0:T(8,128)(2,1)S(1)}, bf16[256,640]{1,0:T(8,128)(2,1)S(1)}, u32[]{:S(2)}, u32[]{:S(2)}) collective-permute-start(bf16[256,640]{1,0:T(8,128)(2,1)S(1)} %get-tuple-element.79), channel_id=1, source_target_pairs={{0,8},{8,0},{1,9},{9,1},{2,10},{10,2},{3,11},{11,3},{4,12},{12,4},... | collective-permute-start | bytes 983048 | tf_op jit(solution)/shard_map/ppermute | solution.py:64
  42.1 1.8 %collective-permute-start.8 = (bf16[256,640]{1,0:T(8,128)(2,1)S(1)}, bf16[256,640]{1,0:T(8,128)(2,1)S(1)}, u32[]{:S(2)}, u32[]{:S(2)}) collective-permute-start(bf16[256,640]{1,0:T(8,128)(2,1)S(1)} %get-tuple-element.85), channel_id=1, source_target_pairs={{0,8},{8,0},{1,9},{9,1},{2,10},{10,2},{3,11},{11,3},{4,12},{12,4},... | collective-permute-start | bytes 983048 | tf_op jit(solution)/shard_map/ppermute | solution.py:64
  42.4 1.9 %collective-permute-start.9 = (bf16[256,640]{1,0:T(8,128)(2,1)S(1)}, bf16[256,640]{1,0:T(8,128)(2,1)S(1)}, u32[]{:S(2)}, u32[]{:S(2)}) collective-permute-start(bf16[256,640]{1,0:T(8,128)(2,1)S(1)} %get-tuple-element.86), channel_id=1, source_target_pairs={{0,8},{8,0},{1,9},{9,1},{2,10},{10,2},{3,11},{11,3},{4,12},{12,4},... | collective-permute-start | bytes 983048 | tf_op jit(solution)/shard_map/ppermute | solution.py:64
  44.4 8.0 %collective-permute-start.10 = (bf16[256,640]{1,0:T(8,128)(2,1)S(1)}, bf16[256,640]{1,0:T(8,128)(2,1)S(1)}, u32[]{:S(2)}, u32[]{:S(2)}) collective-permute-start(bf16[256,640]{1,0:T(8,128)(2,1)S(1)} %get-tuple-element.89), channel_id=1, source_target_pairs={{0,2},{1,3},{2,0},{3,1},{4,6},{5,7},{6,4},{7,5},{8,12},{9,13},{10,... | collective-permute-start | bytes 983048 | tf_op jit(solution)/shard_map/ppermute | solution.py:60
  47.1 8.2 %collective-permute-start.11 = (bf16[256,640]{1,0:T(8,128)(2,1)S(1)}, bf16[256,640]{1,0:T(8,128)(2,1)S(1)}, u32[]{:S(2)}, u32[]{:S(2)}) collective-permute-start(bf16[256,640]{1,0:T(8,128)(2,1)S(1)} %get-tuple-element.90), channel_id=1, source_target_pairs={{0,3},{1,0},{2,1},{3,2},{4,7},{5,4},{6,5},{7,6},{8,28},{9,29},{10,... | collective-permute-start | bytes 983048 | tf_op jit(solution)/shard_map/ppermute | solution.py:60
  47.2 8.5 %collective-permute-start.12 = (bf16[256,640]{1,0:T(8,128)(2,1)S(1)}, bf16[256,640]{1,0:T(8,128)(2,1)S(1)}, u32[]{:S(2)}, u32[]{:S(2)}) collective-permute-start(bf16[256,640]{1,0:T(8,128)(2,1)S(1)} %get-tuple-element.91), channel_id=1, source_target_pairs={{0,1},{1,2},{2,3},{3,0},{4,5},{5,6},{6,7},{7,4},{8,24},{9,25},{10,... | collective-permute-start | bytes 983048 | tf_op jit(solution)/shard_map/ppermute | solution.py:60
  49.4 6.3 %collective-permute-start.13 = (bf16[256,640]{1,0:T(8,128)(2,1)S(1)}, bf16[256,640]{1,0:T(8,128)(2,1)S(1)}, u32[]{:S(2)}, u32[]{:S(2)}) collective-permute-start(bf16[256,640]{1,0:T(8,128)(2,1)S(1)} %get-tuple-element.95), channel_id=1, source_target_pairs={{0,8},{8,0},{1,9},{9,1},{2,10},{10,2},{3,11},{11,3},{4,12},{12,4},... | collective-permute-start | bytes 983048 | tf_op jit(solution)/shard_map/ppermute | solution.py:64

commit v6 on v5

--- a/solution.py
+++ b/solution.py
@@ -19,9 +19,10 @@
 ROWS = 512
 PART = 256
 bf16, f32 = jnp.bfloat16, jnp.float32
-FORWARD = (((0, 0),), ((0, 1), (0, 3), (1, 0)), ((0, 2), (1, 1), (1, 3)), ((1, 2),))
-BACKWARD = (((1, 2, 0),), ((1, 1, 0), (1, 3, 0)), ((0, 2, 1), (0, 1, 0), (0, 3, 0)), ((1, 0, 0), (0, 0, 0)))
-ORDER = tuple(w for call in FORWARD for w in call)
+FORWARD = (((0, 0),), ((0, 1), (0, 3), (1, 0)), ((0, 2), (1, 1), (1, 3)))
+LAST = (1, 2)
+BACKWARD = (((1, 1, 0), (1, 3, 0)), ((0, 2, 1), (0, 1, 0), (0, 3, 0)), ((1, 0, 0), (0, 0, 0)))
+ORDER = tuple(w for call in FORWARD for w in call) + (LAST,)
 
 
 def places():
@@ -177,6 +178,41 @@
         at += 4 if added else 3
 
 
+def turning_kernel(part, query_pos_ref, key_pos_ref, stat_ref, key_ref, qt_ref, gt_ref, q_ref, g_ref,
+                   stat_out, out_ref, ds_ref):
+    start = ORDER.index(part) * PART
+    key_pos = key_pos_ref[start:start + PART, :]
+    key_pos = jnp.concatenate([key_pos] * (ROWS // 128), axis=1)
+    visible = key_pos <= query_pos_ref[0:1, :]
+    scores = jnp.where(visible, nn(key_ref[:, :WIDTH], qt_ref[...]) * SCALE, LOW)
+    value_prod = nn(key_ref[:, :KV_RANK], gt_ref[...])
+    final_max = jnp.maximum(stat_ref[0:1, :], jnp.max(scores, axis=0, keepdims=True))
+    carry = jnp.exp(stat_ref[0:1, :] - final_max)
+    p = jnp.where(visible, jnp.exp(scores - final_max), 0.0)
+    total = stat_ref[1:2, :] * carry + jnp.sum(p, axis=0, keepdims=True)
+    weighted = stat_ref[2:3, :] * carry + jnp.sum(p * value_prod, axis=0, keepdims=True)
+    stat_out[0:1, :] = final_max
+    stat_out[1:2, :] = total
+    stat_out[2:3, :] = weighted
+    inv = 1.0 / total
+    attention = p * inv
+    ds = (SCALE * attention * (value_prod - weighted * inv)).astype(bf16)
+    ds_ref[...] = ds
+    q = q_ref[...]
+    out_ref[:, :KV_RANK] = (nn(ds, q[:, :KV_RANK]) + nn(attention.astype(bf16), g_ref[...])).astype(bf16)
+    rope = nn(ds, q[:, KV_RANK:])
+    out_ref[:, KV_RANK:] = jnp.concatenate([rope, jnp.zeros_like(rope)], axis=1).astype(bf16)
+
+
+def turning_call(part, query_pos, key_pos, stat, keys, qt, gt, q, g):
+    shapes = [
+        jax.ShapeDtypeStruct((8, ROWS), f32), jax.ShapeDtypeStruct((PART, SENT), bf16),
+        jax.ShapeDtypeStruct((PART, ROWS), bf16),
+    ]
+    args = [query_pos, key_pos, stat, *keys, qt, gt, q, g]
+    return call(lambda *refs: turning_kernel(part, *refs), "turning_" + label([part]), shapes, 0, args)
+
+
 def query_kernel(counts, *refs):
     out = refs[-1]
     ds, keys, at = [], [], 0
@@ -303,17 +339,17 @@
         stat, p, vp = forward_call(wanted, query_pos, key_pos, stat, [keys[w] for w in wanted], qt, gt)
         for i, w in enumerate(wanted):
             saved[w] = (i, stat, p, vp)
-    last = stat
-    done = {}
-    taken = {}
-    for wanted in BACKWARD[:3]:
+    last, *turned = turning_call(LAST, query_pos, key_pos, stat, keys[LAST], qt, gt, q, g)
+    done = {LAST: tuple(turned)}
+    taken = {LAST[1]: swap(turned[0])}
+    for wanted in BACKWARD[:2]:
         done.update(backward_call(wanted, last, saved, taken, q, g))
         for half, shift, _ in wanted:
             if half:
                 taken[shift] = swap(done[1, shift][0])
     near = add_call([done[0, s][0] for s in (1, 3)], [taken[s] for s in (1, 3)])
     far, near, last = lax.optimization_barrier((done[0, 2][0], near, last))
-    done.update(backward_call(BACKWARD[3], last, saved, taken, q, g))
+    done.update(backward_call(BACKWARD[2], last, saved, taken, q, g))
     taken[0] = swap(done[1, 0][0])
     arrived = [turn(far, 2), turn(near[0], 3), turn(near[1], 1), taken[0]]
     dq = query_call([(done[w][1], keys[w]) for w in ORDER])

time: 76.2 us -> 76.3 us (level)
    pallas_call x10 -> x9, Pallas kernels: 9.93 us -> 9.97 us  [call(): pl.pallas_call(kernel, out_shape=shapes, in_specs=[SMEM] * smem + [VMEM]...]
where the time goes in v6:
time: 76.3 us; the launch traced here: 74.9 us
  blocking collectives  40.2 us (53%)
  starting transfers between devices  14.7 us (19%)
  Pallas kernels  12 us (16%)
  waiting for transfers between devices  3.7 us (5%)
  local copies, waits for them, and re-layouts  2.51 us (3%)
  other arithmetic  0.94 us (1%)
  between operations  0.8 us (1%)
    all_to_all x1, blocking collectives, shards(): lax.all_to_all(jnp.broadcast_to(piece[None], (16, 16, SENT)), ALL, 0, 0,...  22 us
    all_to_all x1, blocking collectives, shards(): lax.all_to_all(part.reshape(32, 8, SENT), ALL, 0, 0, axis_index_groups=sc...  18.3 us
    pallas_call x9, Pallas kernels, call(): pl.pallas_call(kernel, out_shape=shapes, in_specs=[SMEM] * smem + [VMEM]...  9.97 us
    ppermute x6, starting transfers between devices, turn(): return lax.ppermute(value, ALL, pairs)  9.5 us
    ppermute x8, starting transfers between devices, swap(): return lax.ppermute(value, 'c', [(0, 1), (1, 0)])  5.24 us
    ppermute x6, waiting for transfers between devices, turn(): return lax.ppermute(value, ALL, pairs)  3.32 us
    pallas_call x1, Pallas kernels, prepare_call(): pl.pallas_call(prepare_kernel, out_shape=shapes, in_specs=[SMEM] + [pl.Bl...  2 us
    unnamed x6, local copies, waits for them, and re-layouts  1.7 us
  transfers between devices with their start and end apart: 14, of which 3 were waited for; matrix products, arithmetic and copies ran while one was open for 0% of the time, Pallas kernels for 14%

profile of v6, /device:TPU:1, one launch (start us, length us, event | category | flops | bytes accessed | tf_op | source)
XLA Modules:
  0.0 74.9 jit_solution(5021289772411352742)
XLA Ops:
  0.6 0.0 copy-start
  0.7 0.8 %constant_dynamic-slice_fusion.1 = (bf16[8,576]{1,0:T(8,128)(2,1)S(1)}, bf16[8,576]{1,0:T(8,128)(2,1)S(1)}) fusion(bf16[64,576]{1,0:T(8,128)(2,1)} %param.5, s32[]{:T(128)S(6)} %select_n.23, s32[]{:T(128)S(6)} %select_n.25), kind=kLoop, calls=%fused_computation.9 | loop fusion | bytes 36872 | tf_op jit(solution)/shard_map/dynamic_slice | solution.py:320
  1.5 22.0 %all_to_all.10 = bf16[16,16,640]{2,1,0:T(8,128)(2,1)S(1)} all-to-all(bf16[16,16,640]{2,1,0:T(8,128)(2,1)S(1)} %broadcast_in_dim.2), channel_id=1, replica_groups={{0,16,32,48,64,80,96,112,128,144,160,176,192,208,224,240},{1,17,33,49,6..., dimensions={0} | all-to-all | bytes 655360 | tf_op jit(solution)/shard_map/all_to_all | solution.py:322
  23.5 1.1 %collective-permute-start.2 = (bf16[256,640]{1,0:T(8,128)(2,1)S(1)}, bf16[256,640]{1,0:T(8,128)(2,1)S(1)}, u32[]{:S(2)}, u32[]{:S(2)}) collective-permute-start(bf16[256,640]{1,0:T(8,128)(2,1)S(1)} %bitcast.11), channel_id=1, source_target_pairs={{0,1},{1,2},{2,3},{3,0},{4,5},{5,6},{6,7},{7,4},{8,24},{9,25},{10,... | collective-permute-start | bytes 983048 | tf_op jit(solution)/shard_map/ppermute | solution.py:61
  24.6 1.6 %collective-permute-start.1 = (bf16[256,640]{1,0:T(8,128)(2,1)S(1)}, bf16[256,640]{1,0:T(8,128)(2,1)S(1)}, u32[]{:S(2)}, u32[]{:S(2)}) collective-permute-start(bf16[256,640]{1,0:T(8,128)(2,1)S(1)} %bitcast.12), channel_id=1, source_target_pairs={{0,3},{1,0},{2,1},{3,2},{4,7},{5,4},{6,5},{7,6},{8,28},{9,29},{10,... | collective-permute-start | bytes 983048 | tf_op jit(solution)/shard_map/ppermute | solution.py:61
  26.2 2.4 %collective-permute-start.3 = (bf16[256,640]{1,0:T(8,128)(2,1)S(1)}, bf16[256,640]{1,0:T(8,128)(2,1)S(1)}, u32[]{:S(2)}, u32[]{:S(2)}) collective-permute-start(bf16[256,640]{1,0:T(8,128)(2,1)S(1)} %bitcast.13), channel_id=1, source_target_pairs={{0,8},{8,0},{1,9},{9,1},{2,10},{10,2},{3,11},{11,3},{4,12},{12,4},... | collective-permute-start | bytes 983048 | tf_op jit(solution)/shard_map/ppermute | solution.py:65
  28.6 2.6 %collective-permute-start = (bf16[256,640]{1,0:T(8,128)(2,1)S(1)}, bf16[256,640]{1,0:T(8,128)(2,1)S(1)}, u32[]{:S(2)}, u32[]{:S(2)}) collective-permute-start(bf16[256,640]{1,0:T(8,128)(2,1)S(1)} %bitcast.14), channel_id=1, source_target_pairs={{0,2},{1,3},{2,0},{3,1},{4,6},{5,7},{6,4},{7,5},{8,12},{9,13},{10,... | collective-permute-start | bytes 983048 | tf_op jit(solution)/shard_map/ppermute | solution.py:61
  31.2 0.1 pad_add_fusion.where_ref
  31.3 0.0 copy-done
  31.3 1.0 %copy-done.1 = bf16[64,8,512]{2,1,0:T(8,128)(2,1)S(1)} copy-done((bf16[64,8,512]{2,1,0:T(8,128)(2,1)S(1)}, bf16[64,8,512]{2,1,0:T(8,128)(2,1)}, u32[]{:S(2)}) %copy-start.1) | copy-done | bytes 524312
  32.3 0.7 copy-done.2
  33.0 2.0 %prepare.1 = (bf16[512,576]{1,0:T(8,128)(2,1)S(1)}, bf16[512,512]{1,0:T(8,128)(2,1)S(1)}, bf16[576,512]{1,0:T(8,128)(2,1)S(1)}, bf16[512,512]{1,0:T(8,128)(2,1)S...) custom-call(s32[4]{0:T(128)S(1)} %pad_add_fusion.where_ref, s32[64]{0:T(128)S(1)} %copy-done.2, ...), custom_call_target="tpu_custom_call" | custom-call | flops 1024 | bytes 1024 | tf_op jit(solution)/shard_map/prepare/pallas_call | solution.py:252
  35.0 0.5 forward_00.1
  35.5 0.0 collective-permute-done.2.refs_3_
  35.5 0.0 collective-permute-done.1.refs_4_.refs_5_
  35.6 0.1 collective-permute-start.4
  35.7 0.5 collective-permute-start.5
  36.2 0.0 collective-permute-done.3.refs_5_.refs_7_
  36.2 1.3 %forward_01_03_10.1 = (f32[8,512]{1,0:T(8,128)S(1)}, f32[768,512]{1,0:T(8,128)S(1)}, f32[768,512]{1,0:T(8,128)S(1)}) custom-call(s32[8,512]{1,0:T(8,128)S(1)} %get-tuple-element.56.refs_0_, s32[2048,128]{1,0:T(8,128)S(1)} %get-tuple-element.57.refs_1_, f32[8,512]{1,0:T(8,128)S(1)} %get-tuple-element.63.refs_2_.refs_4_, ...), custom_call_target="tpu_custom_call" | custom-call | flops 1024 | bytes 1024 | tf_op jit(solution)/shard_map/forward_01_03_10/pallas_call | solution.py:233
  37.5 0.0 collective-permute-done.refs_3_.refs_9_
  37.5 1.0 %collective-permute-start.6 = (bf16[256,640]{1,0:T(8,128)(2,1)S(1)}, bf16[256,640]{1,0:T(8,128)(2,1)S(1)}, u32[]{:S(2)}, u32[]{:S(2)}) collective-permute-start(bf16[256,640]{1,0:T(8,128)(2,1)S(1)} %collective-permute-done.refs_3_.refs_9_), channel_id=1, source_target_pairs={{0,8},{8,0},{1,9},{9,1},{2,10},{10,2},{3,11},{11,3},{4,12},{12,4},... | collective-permute-start | bytes 983048 | tf_op jit(solution)/shard_map/ppermute | solution.py:65
  38.4 0.0 collective-permute-done.4.refs_4_.refs_11_
  38.4 0.0 collective-permute-done.5.refs_5_.refs_13_
  38.4 1.3 %forward_02_11_13.1 = (f32[8,512]{1,0:T(8,128)S(1)}, f32[768,512]{1,0:T(8,128)S(1)}, f32[768,512]{1,0:T(8,128)S(1)}) custom-call(s32[8,512]{1,0:T(8,128)S(1)} %get-tuple-element.56.refs_0_, s32[2048,128]{1,0:T(8,128)S(1)} %get-tuple-element.57.refs_1_, f32[8,512]{1,0:T(8,128)S(1)} %get-tuple-element.67.refs_2_.refs_5_.refs_8_.refs_1_, ...), custom_call_target="tpu_custom_call" | custom-call | flops 1024 | bytes 1024 | tf_op jit(solution)/shard_map/forward_02_11_13/pallas_call | solution.py:233
  39.7 0.0 collective-permute-done.6.refs_3_.refs_15_
  39.7 1.1 %turning_12.1 = (f32[8,512]{1,0:T(8,128)S(1)}, bf16[256,640]{1,0:T(8,128)(2,1)S(1)}, bf16[256,512]{1,0:T(8,128)(2,1)S(1)}) custom-call(s32[8,512]{1,0:T(8,128)S(1)} %get-tuple-element.56.refs_0_, s32[2048,128]{1,0:T(8,128)S(1)} %get-tuple-element.57.refs_1_, f32[8,512]{1,0:T(8,128)S(1)} %get-tuple-element.69.refs_2_.refs_1_.refs_4_, ...), custom_call_target="tpu_custom_call" | custom-call | flops 1024 | bytes 1024 | tf_op jit(solution)/shard_map/turning_12/pallas_call | solution.py:233
  40.9 0.4 collective-permute-start.7
  41.3 0.9 %backward_11_13.1 = (bf16[256,640]{1,0:T(8,128)(2,1)S(1)}, bf16[256,512]{1,0:T(8,128)(2,1)S(1)}, bf16[256,640]{1,0:T(8,128)(2,1)S(1)}, bf16[256,512]{1,0:T(8,128)(2,1)S(1)}) custom-call(f32[8,512]{1,0:T(8,128)S(1)} %get-tuple-element.88.refs_0_, f32[8,512]{1,0:T(8,128)S(1)} %get-tuple-element.69.refs_2_.refs_1_.refs_4_, ...), custom_call_target="tpu_custom_call" | custom-call | flops 1024 | bytes 1024 | tf_op jit(solution)/shard_map/backward_11_13/pallas_call | solution.py:233
  42.2 0.3 collective-permute-start.8
  42.4 0.3 collective-permute-start.9
  42.8 0.0 collective-permute-done.7.refs_4_
  42.8 1.2 %backward_02_01_03.1 = (bf16[256,640]{1,0:T(8,128)(2,1)S(1)}, bf16[256,512]{1,0:T(8,128)(2,1)S(1)}, f32[256,640]{1,0:T(8,128)S(1)}, bf16[256,512]{1,0:T(8,128)(2...) custom-call(f32[8,512]{1,0:T(8,128)S(1)} %get-tuple-element.88.refs_0_, ...), custom_call_target="tpu_custom_call" | custom-call | flops 1024 | bytes 1024 | tf_op jit(solution)/shard_map/backward_02_01_03/pallas_call | solution.py:233
  44.0 0.0 collective-permute-done.8.refs_2_
  44.0 0.4 collective-permute-done.9.refs_3_
  44.3 0.1 add_cores.1
  44.5 2.7 %collective-permute-start.10 = (bf16[256,640]{1,0:T(8,128)(2,1)S(1)}, bf16[256,640]{1,0:T(8,128)(2,1)S(1)}, u32[]{:S(2)}, u32[]{:S(2)}) collective-permute-start(bf16[256,640]{1,0:T(8,128)(2,1)S(1)} %get-tuple-element.85), channel_id=1, source_target_pairs={{0,2},{1,3},{2,0},{3,1},{4,6},{5,7},{6,4},{7,5},{8,12},{9,13},{10,... | collective-permute-start | bytes 983048 | tf_op jit(solution)/shard_map/ppermute | solution.py:61
  47.2 0.1 collective-permute-start.11
  47.3 1.3 %collective-permute-start.12 = (bf16[256,640]{1,0:T(8,128)(2,1)S(1)}, bf16[256,640]{1,0:T(8,128)(2,1)S(1)}, u32[]{:S(2)}, u32[]{:S(2)}) collective-permute-start(bf16[256,640]{1,0:T(8,128)(2,1)S(1)} %get-tuple-element.87), channel_id=1, source_target_pairs={{0,1},{1,2},{2,3},{3,0},{4,5},{5,6},{6,7},{7,4},{8,24},{9,25},{10,... | collective-permute-start | bytes 983048 | tf_op jit(solution)/shard_map/ppermute | solution.py:61
  48.7 0.9 %backward_10_00.1 = (bf16[256,640]{1,0:T(8,128)(2,1)S(1)}, bf16[256,512]{1,0:T(8,128)(2,1)S(1)}, f32[256,640]{1,0:T(8,128)S(1)}, bf16[256,512]{1,0:T(8,128)(2,1)S(1)}) custom-call(f32[8,512]{1,0:T(8,128)S(1)} %get-tuple-element.88.refs_0_, f32[8,512]{1,0:T(8,128)S(1)} %get-tuple-element.67.refs_2_.refs_5_.refs_8_.refs_1_, ...), custom_call_target="tpu_custom_call" | custom-call | flops 1024 | bytes 1024 | tf_op jit(solution)/shard_map/backward_10_00/pallas_call | solution.py:233
  49.5 0.3 collective-permute-start.13
  49.8 2.7 %query_grad.1 = bf16[512,576]{1,0:T(8,128)(2,1)} custom-call(bf16[256,512]{1,0:T(8,128)(2,1)S(1)} %get-tuple-element.92.refs_0_, bf16[256,640]{1,0:T(8,128)(2,1)S(1)} %bitcast.16, bf16[256,512]{1,0:T(8,128)(2,1)S(1)} %get-tuple-element.93.refs_2_, bf16[256,640]{1,0:T(8,128)(2,1)S(1)} %collective-permute-done.2.refs_3_, ...), custom_call_target="tpu_custom_call" | custom-call | flops 1024 | bytes 1024 | tf_op jit(solution)/shard_map/query_grad/pallas_call | solution.py:233
  52.5 0.0 collective-permute-done.10
  52.5 2.9 %collective-permute-done.11 = bf16[256,640]{1,0:T(8,128)(2,1)S(1)} collective-permute-done((bf16[256,640]{1,0:T(8,128)(2,1)S(1)}, bf16[256,640]{1,0:T(8,128)(2,1)S(1)}, u32[]{:S(2)}, u32[]{:S(2)}) %collective-permute-start.11) | collective-permute-done | bytes 327712 | tf_op jit(solution)/shard_map/ppermute | solution.py:61
  55.4 0.4 collective-permute-done.12
  55.8 0.0 collective-permute-done.13
  55.8 0.2 fusion
  56.0 18.3 %all_to_all.11 = bf16[32,8,640]{2,1,0:T(8,128)(2,1)S(1)} all-to-all(bf16[32,8,640]{2,1,0:T(8,128)(2,1)S(1)} %fusion), channel_id=1, replica_groups={{0,4,16,20,32,36,48,52,64,68,80,84,96,100,112,116,128,132,144,148,160,1..., dimensions={0} | all-to-all | bytes 655360 | tf_op jit(solution)/shard_map/all_to_all | solution.py:359
  74.2 0.7 convert_reduce_fusion
  (4 shorter events, 0.0 us)
Async XLA Ops:
  0.6 30.7 %copy-start = (bf16[64,8,576]{2,1,0:T(8,128)(2,1)S(1)}, bf16[64,8,576]{2,1,0:T(8,128)(2,1)}, u32[]{:S(2)}) copy-start(bf16[64,8,576]{2,1,0:T(8,128)(2,1)} %param.4) | copy-start | bytes 1769476
  23.5 12.1 %collective-permute-start.2 = (bf16[256,640]{1,0:T(8,128)(2,1)S(1)}, bf16[256,640]{1,0:T(8,128)(2,1)S(1)}, u32[]{:S(2)}, u32[]{:S(2)}) collective-permute-start(bf16[256,640]{1,0:T(8,128)(2,1)S(1)} %bitcast.11), channel_id=1, source_target_pairs={{0,1},{1,2},{2,3},{3,0},{4,5},{5,6},{6,7},{7,4},{8,24},{9,25},{10,... | collective-permute-start | bytes 983048 | tf_op jit(solution)/shard_map/ppermute | solution.py:61
  24.6 11.0 %collective-permute-start.1 = (bf16[256,640]{1,0:T(8,128)(2,1)S(1)}, bf16[256,640]{1,0:T(8,128)(2,1)S(1)}, u32[]{:S(2)}, u32[]{:S(2)}) collective-permute-start(bf16[256,640]{1,0:T(8,128)(2,1)S(1)} %bitcast.12), channel_id=1, source_target_pairs={{0,3},{1,0},{2,1},{3,2},{4,7},{5,4},{6,5},{7,6},{8,28},{9,29},{10,... | collective-permute-start | bytes 983048 | tf_op jit(solution)/shard_map/ppermute | solution.py:61
  26.2 10.0 %collective-permute-start.3 = (bf16[256,640]{1,0:T(8,128)(2,1)S(1)}, bf16[256,640]{1,0:T(8,128)(2,1)S(1)}, u32[]{:S(2)}, u32[]{:S(2)}) collective-permute-start(bf16[256,640]{1,0:T(8,128)(2,1)S(1)} %bitcast.13), channel_id=1, source_target_pairs={{0,8},{8,0},{1,9},{9,1},{2,10},{10,2},{3,11},{11,3},{4,12},{12,4},... | collective-permute-start | bytes 983048 | tf_op jit(solution)/shard_map/ppermute | solution.py:65
  28.6 8.9 %collective-permute-start = (bf16[256,640]{1,0:T(8,128)(2,1)S(1)}, bf16[256,640]{1,0:T(8,128)(2,1)S(1)}, u32[]{:S(2)}, u32[]{:S(2)}) collective-permute-start(bf16[256,640]{1,0:T(8,128)(2,1)S(1)} %bitcast.14), channel_id=1, source_target_pairs={{0,2},{1,3},{2,0},{3,1},{4,6},{5,7},{6,4},{7,5},{8,12},{9,13},{10,... | collective-permute-start | bytes 983048 | tf_op jit(solution)/shard_map/ppermute | solution.py:61
  31.3 1.0 %copy-start.1 = (bf16[64,8,512]{2,1,0:T(8,128)(2,1)S(1)}, bf16[64,8,512]{2,1,0:T(8,128)(2,1)}, u32[]{:S(2)}) copy-start(bf16[64,8,512]{2,1,0:T(8,128)(2,1)} %param.6) | copy-start | bytes 1572868
  32.3 0.7 copy-start.2
  35.6 2.9 %collective-permute-start.4 = (bf16[256,640]{1,0:T(8,128)(2,1)S(1)}, bf16[256,640]{1,0:T(8,128)(2,1)S(1)}, u32[]{:S(2)}, u32[]{:S(2)}) collective-permute-start(bf16[256,640]{1,0:T(8,128)(2,1)S(1)} %collective-permute-done.2.refs_3_), channel_id=1, source_target_pairs={{0,8},{8,0},{1,9},{9,1},{2,10},{10,2},{3,11},{11,3},{4,12},{12,4},... | collective-permute-start | bytes 983048 | tf_op jit(solution)/shard_map/ppermute | solution.py:65
  35.7 2.8 %collective-permute-start.5 = (bf16[256,640]{1,0:T(8,128)(2,1)S(1)}, bf16[256,640]{1,0:T(8,128)(2,1)S(1)}, u32[]{:S(2)}, u32[]{:S(2)}) collective-permute-start(bf16[256,640]{1,0:T(8,128)(2,1)S(1)} %collective-permute-done.1.refs_4_.refs_5_), channel_id=1, source_target_pairs={{0,8},{8,0},{1,9},{9,1},{2,10},{10,2},{3,11},{11,3},{4,12},{12,4},... | collective-permute-start | bytes 983048 | tf_op jit(solution)/shard_map/ppermute | solution.py:65
  37.5 2.3 %collective-permute-start.6 = (bf16[256,640]{1,0:T(8,128)(2,1)S(1)}, bf16[256,640]{1,0:T(8,128)(2,1)S(1)}, u32[]{:S(2)}, u32[]{:S(2)}) collective-permute-start(bf16[256,640]{1,0:T(8,128)(2,1)S(1)} %collective-permute-done.refs_3_.refs_9_), channel_id=1, source_target_pairs={{0,8},{8,0},{1,9},{9,1},{2,10},{10,2},{3,11},{11,3},{4,12},{12,4},... | collective-permute-start | bytes 983048 | tf_op jit(solution)/shard_map/ppermute | solution.py:65
  40.9 1.9 %collective-permute-start.7 = (bf16[256,640]{1,0:T(8,128)(2,1)S(1)}, bf16[256,640]{1,0:T(8,128)(2,1)S(1)}, u32[]{:S(2)}, u32[]{:S(2)}) collective-permute-start(bf16[256,640]{1,0:T(8,128)(2,1)S(1)} %get-tuple-element.75), channel_id=1, source_target_pairs={{0,8},{8,0},{1,9},{9,1},{2,10},{10,2},{3,11},{11,3},{4,12},{12,4},... | collective-permute-start | bytes 983048 | tf_op jit(solution)/shard_map/ppermute | solution.py:65
  42.2 1.8 %collective-permute-start.8 = (bf16[256,640]{1,0:T(8,128)(2,1)S(1)}, bf16[256,640]{1,0:T(8,128)(2,1)S(1)}, u32[]{:S(2)}, u32[]{:S(2)}) collective-permute-start(bf16[256,640]{1,0:T(8,128)(2,1)S(1)} %get-tuple-element.81), channel_id=1, source_target_pairs={{0,8},{8,0},{1,9},{9,1},{2,10},{10,2},{3,11},{11,3},{4,12},{12,4},... | collective-permute-start | bytes 983048 | tf_op jit(solution)/shard_map/ppermute | solution.py:65
  42.4 1.9 %collective-permute-start.9 = (bf16[256,640]{1,0:T(8,128)(2,1)S(1)}, bf16[256,640]{1,0:T(8,128)(2,1)S(1)}, u32[]{:S(2)}, u32[]{:S(2)}) collective-permute-start(bf16[256,640]{1,0:T(8,128)(2,1)S(1)} %get-tuple-element.82), channel_id=1, source_target_pairs={{0,8},{8,0},{1,9},{9,1},{2,10},{10,2},{3,11},{11,3},{4,12},{12,4},... | collective-permute-start | bytes 983048 | tf_op jit(solution)/shard_map/ppermute | solution.py:65
  44.5 8.0 %collective-permute-start.10 = (bf16[256,640]{1,0:T(8,128)(2,1)S(1)}, bf16[256,640]{1,0:T(8,128)(2,1)S(1)}, u32[]{:S(2)}, u32[]{:S(2)}) collective-permute-start(bf16[256,640]{1,0:T(8,128)(2,1)S(1)} %get-tuple-element.85), channel_id=1, source_target_pairs={{0,2},{1,3},{2,0},{3,1},{4,6},{5,7},{6,4},{7,5},{8,12},{9,13},{10,... | collective-permute-start | bytes 983048 | tf_op jit(solution)/shard_map/ppermute | solution.py:61
  47.2 8.2 %collective-permute-start.11 = (bf16[256,640]{1,0:T(8,128)(2,1)S(1)}, bf16[256,640]{1,0:T(8,128)(2,1)S(1)}, u32[]{:S(2)}, u32[]{:S(2)}) collective-permute-start(bf16[256,640]{1,0:T(8,128)(2,1)S(1)} %get-tuple-element.86), channel_id=1, source_target_pairs={{0,3},{1,0},{2,1},{3,2},{4,7},{5,4},{6,5},{7,6},{8,28},{9,29},{10,... | collective-permute-start | bytes 983048 | tf_op jit(solution)/shard_map/ppermute | solution.py:61
  47.3 8.5 %collective-permute-start.12 = (bf16[256,640]{1,0:T(8,128)(2,1)S(1)}, bf16[256,640]{1,0:T(8,128)(2,1)S(1)}, u32[]{:S(2)}, u32[]{:S(2)}) collective-permute-start(bf16[256,640]{1,0:T(8,128)(2,1)S(1)} %get-tuple-element.87), channel_id=1, source_target_pairs={{0,1},{1,2},{2,3},{3,0},{4,5},{5,6},{6,7},{7,4},{8,24},{9,25},{10,... | collective-permute-start | bytes 983048 | tf_op jit(solution)/shard_map/ppermute | solution.py:61
  49.5 6.3 %collective-permute-start.13 = (bf16[256,640]{1,0:T(8,128)(2,1)S(1)}, bf16[256,640]{1,0:T(8,128)(2,1)S(1)}, u32[]{:S(2)}, u32[]{:S(2)}) collective-permute-start(bf16[256,640]{1,0:T(8,128)(2,1)S(1)} %get-tuple-element.91), channel_id=1, source_target_pairs={{0,8},{8,0},{1,9},{9,1},{2,10},{10,2},{3,11},{11,3},{4,12},{12,4},... | collective-permute-start | bytes 983048 | tf_op jit(solution)/shard_map/ppermute | solution.py:65
